TPU v7x, 1024 devices: a whole 8x8x8 slice. The times are simulated.
1024 devices in a mesh: gx: 16 (over x, z_hi), gy: 8 (over y), gz: 8 (over z_lo, core).
Axes of the slice: x: 8, y: 8, z: 8 (z_hi: 2, z_lo: 4; z = z_hi * 4 + z_lo), core: 2. Of those that a mesh axis runs over, the one named last changes fastest.
Arguments:
- flow_moments: float32 [10, 64, 64, 1024], P(None, 'gx', 'gy', 'gz'), may hold values from -4 to 4
- species_moments: float32 [4, 64, 64, 1024], P(None, 'gx', 'gy', 'gz'), may hold values from -6 to 6
- fluid_mask: int32 [64, 64, 1024], P('gx', 'gy', 'gz'), may hold values from 0 to 1, as said below
- reactive_mask: int32 [64, 64, 1024], P('gx', 'gy', 'gz'), may hold values 0 or 1
Outputs:
- flow_out: float32 [10, 64, 64, 1024], P(None, 'gx', 'gy', 'gz')
- species_out: float32 [4, 64, 64, 1024], P(None, 'gx', 'gy', 'gz')
- dissolved: float32 [64, 64, 1024], P('gx', 'gy', 'gz')
Inputs may be any that keep to these rules, and one draw needn't show every extreme that they name: `fluid_mask`: the share of fluid voxels differs from one block of 4 x 8 x 128 voxels to another. `reactive_mask`: read only at solid voxels.
All inputs are finite; a program needn't handle non-finite values. No bound on the sum of `reactive_mask` on one device may be relied on, other than what follows from the above.
Results may differ from a plain program's by a relative error of at most 0.0003.
Values sent between devices are 32-bit elements; how exact they have to be, the bound alone decides.
No kernel may reach another device: no remote copies, remote signals or barrier semaphores. Data moves between devices by JAX's collectives and lax.ppermute only.
A program may use at most 32 MiB of HBM per device.

v0:
```python
import jax
import jax.numpy as jnp
from jax import lax
from jax.sharding import PartitionSpec as P

ITERS = 4


KEEP_FLOW = 1.0 - 1.0 / 0.8
KEEP_SPECIES = 1.0 - 1.0 / 0.7
REACT_RATE = 0.5
SATURATION = 1.0
GRAVITY = 0.001
FLOW_DIRECTIONS = [
    (0, 0, 0),
    (1, 0, 0),
    (-1, 0, 0),
    (0, 1, 0),
    (0, -1, 0),
    (0, 0, 1),
    (0, 0, -1),
    (1, 1, 0),
    (-1, -1, 0),
    (1, -1, 0),
    (-1, 1, 0),
    (1, 0, 1),
    (-1, 0, -1),
    (1, 0, -1),
    (-1, 0, 1),
    (0, 1, 1),
    (0, -1, -1),
    (0, 1, -1),
    (0, -1, 1),
]
FLOW_WEIGHTS = [1.0 / 3.0] + [1.0 / 18.0] * 6 + [1.0 / 36.0] * 12
SPECIES_DIRECTIONS = FLOW_DIRECTIONS[:7]
SPECIES_WEIGHTS = [0.25] + [0.125] * 6


def padded_2(x, sides, width, wrap):
    for axis, dim in sides:
        count, length = (lax.axis_size(axis), x.shape[dim])
        up = [(i, (i + 1) % count) for i in range(count if wrap else count - 1)]
        down = [(j, i) for i, j in up]
        last = lax.slice_in_dim(x, length - width, length, axis=dim)
        leading = lax.slice_in_dim(x, 0, width, axis=dim)
        before = lax.ppermute(last, axis, up)
        after = lax.ppermute(leading, axis, down)
        x = jnp.concatenate([before, x, after], axis=dim)
    return x


def window(padded, vel, sign):
    size_a = padded.shape[-3] - 2
    size_b = padded.shape[-2] - 2
    size_c = padded.shape[-1] - 2
    start_a = 1 + sign * vel[0]
    start_b = 1 + sign * vel[1]
    start_c = 1 + sign * vel[2]
    return padded[
        ..., start_a : start_a + size_a, start_b : start_b + size_b, start_c : start_c + size_c
    ]


def rebuild_flow(moments, vel, weight):
    rho = moments[0]
    axx = moments[4] - rho / 3.0
    ayy = moments[5] - rho / 3.0
    azz = moments[6] - rho / 3.0
    quad = vel[0] * vel[0] * axx + vel[1] * vel[1] * ayy + vel[2] * vel[2] * azz
    quad = quad + 2.0 * (
        vel[0] * vel[1] * moments[7] + vel[0] * vel[2] * moments[8] + vel[1] * vel[2] * moments[9]
    )
    quad = quad - (axx + ayy + azz) / 3.0
    lin = vel[0] * moments[1] + vel[1] * moments[2] + vel[2] * moments[3]
    return weight * (rho + 3.0 * lin + 4.5 * quad)


def rebuild_species(moments, vel, weight):
    lin = vel[0] * moments[1] + vel[1] * moments[2] + vel[2] * moments[3]
    return weight * (moments[0] + 4.0 * lin)


def flow_collide(moments, fluid):
    rho = moments[0]
    jx, jy, jz = (moments[1], moments[2], moments[3])
    equil = [
        rho / 3.0 + jx * jx,
        rho / 3.0 + jy * jy,
        rho / 3.0 + jz * jz,
        jx * jy,
        jx * jz,
        jy * jz,
    ]
    stress = [equil[k] + KEEP_FLOW * (moments[4 + k] - equil[k]) for k in range(6)]
    return jnp.stack([rho, jx, jy, jz] + stress) * fluid


def species_collide(species, flow, fluid):
    conc = species[0]
    fluxes = [
        conc * flow[1 + k] + KEEP_SPECIES * (species[1 + k] - conc * flow[1 + k]) for k in range(3)
    ]
    return jnp.stack([conc] + fluxes) * fluid


def advance(flow_pad, species_pad, flag_pad, flow_own, species_own, fluid, react, dissolved):
    totals = [jnp.zeros_like(fluid) for k in range(10)]
    for index, vel in enumerate(FLOW_DIRECTIONS):
        weight = FLOW_WEIGHTS[index]
        back = (-vel[0], -vel[1], -vel[2])
        source_fluid = window(flag_pad[0], vel, -1)
        popul = jnp.where(
            source_fluid > 0.5,
            rebuild_flow(window(flow_pad, vel, -1), vel, weight),
            rebuild_flow(flow_own, back, weight),
        )
        coefs = [
            1,
            vel[0],
            vel[1],
            vel[2],
            vel[0] * vel[0],
            vel[1] * vel[1],
            vel[2] * vel[2],
            vel[0] * vel[1],
            vel[0] * vel[2],
            vel[1] * vel[2],
        ]
        for k in range(10):
            if coefs[k] != 0:
                totals[k] = totals[k] + coefs[k] * popul
    totals[1] = totals[1] + GRAVITY
    new_flow = jnp.stack(totals) * fluid
    sums = [jnp.zeros_like(fluid) for k in range(4)]
    for index, vel in enumerate(SPECIES_DIRECTIONS):
        weight = SPECIES_WEIGHTS[index]
        back = (-vel[0], -vel[1], -vel[2])
        source_fluid = window(flag_pad[0], vel, -1)
        source_react = window(flag_pad[1], vel, -1)
        bounced = rebuild_species(species_own, back, weight)
        reacted = bounced + REACT_RATE * source_react * (weight * SATURATION - bounced)
        popul = jnp.where(
            source_fluid > 0.5, rebuild_species(window(species_pad, vel, -1), vel, weight), reacted
        )
        coefs = [1, vel[0], vel[1], vel[2]]
        for k in range(4):
            if coefs[k] != 0:
                sums[k] = sums[k] + coefs[k] * popul
        if index > 0:
            neighbour_fluid = window(flag_pad[0], vel, 1)
            outgoing = rebuild_species(window(species_pad, vel, 1), back, weight)
            release = REACT_RATE * react * (weight * SATURATION - outgoing)
            dissolved = dissolved + jnp.where(neighbour_fluid > 0.5, release, 0.0) * (1.0 - fluid)
    new_species = jnp.stack(sums) * fluid
    return (new_flow, new_species, dissolved)


def per_device(flow_moments, species_moments, fluid_mask, reactive_mask):
    fluid = fluid_mask.astype(jnp.float32)
    react = reactive_mask.astype(jnp.float32)
    flags = jnp.stack([fluid, react])
    flow, species = (flow_moments, species_moments)
    dissolved = jnp.zeros_like(fluid)

    def extend_flow(values):
        wide = padded_2(values, (("gx", 1),), 1, True)
        return padded_2(wide, (("gy", 2), ("gz", 3)), 1, False)

    flag_pad = extend_flow(flags)
    for step in range(ITERS):
        flow_own = flow_collide(flow, fluid)
        species_own = species_collide(species, flow_own, fluid)
        flow_pad = extend_flow(flow_own)
        extend_wide = padded_2(species_own, (("gx", 1),), 1, True)
        species_pad = padded_2(extend_wide, (("gy", 2), ("gz", 3)), 1, False)
        flow, species, dissolved = advance(
            flow_pad, species_pad, flag_pad, flow_own, species_own, fluid, react, dissolved
        )
    return (flow, species, dissolved)


def solution(mesh):
    return jax.shard_map(
        per_device,
        mesh=mesh,
        in_specs=(
            P(None, "gx", "gy", "gz"),
            P(None, "gx", "gy", "gz"),
            P("gx", "gy", "gz"),
            P("gx", "gy", "gz"),
        ),
        out_specs=(P(None, "gx", "gy", "gz"), P(None, "gx", "gy", "gz"), P("gx", "gy", "gz")),
        check_vma=False,
    )
```

profile of v0, /device:TPU:199, one launch (start us, length us, event | category | flops | bytes accessed | tf_op | source)
XLA Modules:
  0.0 311.6 jit_solution(10903150574984134664)
XLA Ops:
  1.4 13.4 %collective-permute-start = (f32[2,1,8,128]{3,2,1,0:T(8,128)S(1)}, f32[2,1,8,128]{3,2,1,0:T(8,128)S(1)}, u32[]{:S(2)}, u32[]{:S(2)}) collective-permute-start(f32[2,1,8,128]{3,2,1,0:T(8,128)S(1)} %get-tuple-element.273), channel_id=1, source_target_pairs={{0,64},{64,128},{128,192},{192,256},{256,320},{320,384},{384,448},... | collective-permute-start | bytes 24584 | tf_op jit(solution)/shard_map/ppermute | solution.py:47
  18.6 7.3 %collective-permute-start.30 = (f32[4,1,8,128]{3,2,1,0:T(8,128)S(1)}, f32[4,1,8,128]{3,2,1,0:T(8,128)S(1)}, u32[]{:S(2)}, u32[]{:S(2)}) collective-permute-start(f32[4,1,8,128]{3,2,1,0:T(8,128)S(1)} %get-tuple-element.268), channel_id=1, source_target_pairs={{0,64},{64,128},{128,192},{192,256},{256,320},{320,384},{384,448},... | collective-permute-start | bytes 49160 | tf_op jit(solution)/shard_map/ppermute | solution.py:47
  28.7 6.3 %collective-permute-start.7 = (f32[10,1,8,128]{3,2,1,0:T(8,128)S(1)}, f32[10,1,8,128]{3,2,1,0:T(8,128)S(1)}, u32[]{:S(2)}, u32[]{:S(2)}) collective-permute-start(f32[10,1,8,128]{3,2,1,0:T(8,128)S(1)} %get-tuple-element.239), channel_id=1, source_target_pairs={{64,0},{128,64},{192,128},{256,192},{320,256},{384,320},{448,384},... | collective-permute-start | bytes 122888 | tf_op jit(solution)/shard_map/ppermute | solution.py:48
  37.5 4.1 %collective-permute-start.3 = (f32[2,6,1,128]{3,2,1,0:T(1,128)S(1)}, f32[2,6,1,128]{3,2,1,0:T(1,128)S(1)}, u32[]{:S(2)}, u32[]{:S(2)}) collective-permute-start(f32[2,6,1,128]{3,2,1,0:T(1,128)S(1)} %get-tuple-element.272), channel_id=1, source_target_pairs={{8,0},{16,8},{24,16},{32,24},{40,32},{48,40},{56,48},{9,1},{17,9},... | collective-permute-start | bytes 18440 | tf_op jit(solution)/shard_map/ppermute | solution.py:48
  42.5 7.1 %collective-permute-start.4 = (f32[2,6,10,1]{3,2,1,0:T(8,128)S(1)}, f32[2,6,10,1]{3,2,1,0:T(8,128)S(1)}, u32[]{:S(2)}, u32[]{:S(2)}) collective-permute-start(f32[2,6,10,1]{3,2,1,0:T(8,128)S(1)} %get-tuple-element.257), channel_id=1, source_target_pairs={{0,1},{1,2},{2,3},{3,4},{4,5},{5,6},{6,7},{8,9},{9,10},{10,11},{11... | collective-permute-start | bytes 1448 | tf_op jit(solution)/shard_map/ppermute | solution.py:47
  58.0 4.8 %collective-permute-start.33 = (f32[4,6,1,128]{3,2,1,0:T(1,128)S(1)}, f32[4,6,1,128]{3,2,1,0:T(1,128)S(1)}, u32[]{:S(2)}, u32[]{:S(2)}) collective-permute-start(f32[4,6,1,128]{3,2,1,0:T(1,128)S(1)} %get-tuple-element.256), channel_id=1, source_target_pairs={{8,0},{16,8},{24,16},{32,24},{40,32},{48,40},{56,48},{9,1},{17,9},... | collective-permute-start | bytes 36872 | tf_op jit(solution)/shard_map/ppermute | solution.py:48
  70.1 4.4 %collective-permute-done.35 = f32[4,6,10,1]{3,2,1,0:T(8,128)S(1)} collective-permute-done((f32[4,6,10,1]{3,2,1,0:T(8,128)S(1)}, f32[4,6,10,1]{3,2,1,0:T(8,128)S(1)}, u32[]{:S(2)}, u32[]{:S(2)}) %collective-permute-start.35) | collective-permute-done | bytes 992 | tf_op jit(solution)/shard_map/ppermute | solution.py:48
  74.8 5.1 %collective-permute-start.9 = (f32[10,6,1,128]{3,2,1,0:T(1,128)S(1)}, f32[10,6,1,128]{3,2,1,0:T(1,128)S(1)}, u32[]{:S(2)}, u32[]{:S(2)}) collective-permute-start(f32[10,6,1,128]{3,2,1,0:T(1,128)S(1)} %get-tuple-element.189), channel_id=1, source_target_pairs={{8,0},{16,8},{24,16},{32,24},{40,32},{48,40},{56,48},{9,1},{17,9},... | collective-permute-start | bytes 92168 | tf_op jit(solution)/shard_map/ppermute | solution.py:48
  81.9 3.9 %collective-permute-done.8 = f32[10,6,1,128]{3,2,1,0:T(1,128)S(1)} collective-permute-done((f32[10,6,1,128]{3,2,1,0:T(1,128)S(1)}, f32[10,6,1,128]{3,2,1,0:T(1,128)S(1)}, u32[]{:S(2)}, u32[]{:S(2)}) %collective-permute-start.8) | collective-permute-done | bytes 30752 | tf_op jit(solution)/shard_map/ppermute | solution.py:47
  91.8 4.7 %collective-permute-done.11 = f32[10,6,10,1]{3,2,1,0:T(8,128)S(1)} collective-permute-done((f32[10,6,10,1]{3,2,1,0:T(8,128)S(1)}, f32[10,6,10,1]{3,2,1,0:T(8,128)S(1)}, u32[]{:S(2)}, u32[]{:S(2)}) %collective-permute-start.11) | collective-permute-done | bytes 2432 | tf_op jit(solution)/shard_map/ppermute | solution.py:48
  101.1 8.9 %collective-permute-start.36 = (f32[4,1,8,128]{3,2,1,0:T(8,128)S(1)}, f32[4,1,8,128]{3,2,1,0:T(8,128)S(1)}, u32[]{:S(2)}, u32[]{:S(2)}) collective-permute-start(f32[4,1,8,128]{3,2,1,0:T(8,128)S(1)} %get-tuple-element.265), channel_id=1, source_target_pairs={{0,64},{64,128},{128,192},{192,256},{256,320},{320,384},{384,448},... | collective-permute-start | bytes 49160 | tf_op jit(solution)/shard_map/ppermute | solution.py:47
  112.0 6.4 %collective-permute-done.37 = f32[4,1,8,128]{3,2,1,0:T(8,128)S(1)} collective-permute-done((f32[4,1,8,128]{3,2,1,0:T(8,128)S(1)}, f32[4,1,8,128]{3,2,1,0:T(8,128)S(1)}, u32[]{:S(2)}, u32[]{:S(2)}) %collective-permute-start.37) | collective-permute-done | bytes 16416 | tf_op jit(solution)/shard_map/ppermute | solution.py:48
  120.4 4.6 %collective-permute-start.39 = (f32[4,6,1,128]{3,2,1,0:T(1,128)S(1)}, f32[4,6,1,128]{3,2,1,0:T(1,128)S(1)}, u32[]{:S(2)}, u32[]{:S(2)}) collective-permute-start(f32[4,6,1,128]{3,2,1,0:T(1,128)S(1)} %get-tuple-element.246), channel_id=1, source_target_pairs={{8,0},{16,8},{24,16},{32,24},{40,32},{48,40},{56,48},{9,1},{17,9},... | collective-permute-start | bytes 36872 | tf_op jit(solution)/shard_map/ppermute | solution.py:48
  127.8 6.4 %collective-permute-start.12 = (f32[10,1,8,128]{3,2,1,0:T(8,128)S(1)}, f32[10,1,8,128]{3,2,1,0:T(8,128)S(1)}, u32[]{:S(2)}, u32[]{:S(2)}) collective-permute-start(f32[10,1,8,128]{3,2,1,0:T(8,128)S(1)} %get-tuple-element.236), channel_id=1, source_target_pairs={{0,64},{64,128},{128,192},{192,256},{256,320},{320,384},{384,448},... | collective-permute-start | bytes 122888 | tf_op jit(solution)/shard_map/ppermute | solution.py:47
  134.4 6.9 %collective-permute-start.40 = (f32[4,6,10,1]{3,2,1,0:T(8,128)S(1)}, f32[4,6,10,1]{3,2,1,0:T(8,128)S(1)}, u32[]{:S(2)}, u32[]{:S(2)}) collective-permute-start(f32[4,6,10,1]{3,2,1,0:T(8,128)S(1)} %get-tuple-element.219), channel_id=1, source_target_pairs={{0,1},{1,2},{2,3},{3,4},{4,5},{5,6},{6,7},{8,9},{9,10},{10,11},{11... | collective-permute-start | bytes 2888 | tf_op jit(solution)/shard_map/ppermute | solution.py:47
  143.9 4.4 %collective-permute-done.41 = f32[4,6,10,1]{3,2,1,0:T(8,128)S(1)} collective-permute-done((f32[4,6,10,1]{3,2,1,0:T(8,128)S(1)}, f32[4,6,10,1]{3,2,1,0:T(8,128)S(1)}, u32[]{:S(2)}, u32[]{:S(2)}) %collective-permute-start.41) | collective-permute-done | bytes 992 | tf_op jit(solution)/shard_map/ppermute | solution.py:48
  162.4 4.8 %collective-permute-done.17 = f32[10,6,10,1]{3,2,1,0:T(8,128)S(1)} collective-permute-done((f32[10,6,10,1]{3,2,1,0:T(8,128)S(1)}, f32[10,6,10,1]{3,2,1,0:T(8,128)S(1)}, u32[]{:S(2)}, u32[]{:S(2)}) %collective-permute-start.17) | collective-permute-done | bytes 2432 | tf_op jit(solution)/shard_map/ppermute | solution.py:48
  171.7 7.8 %collective-permute-start.42 = (f32[4,1,8,128]{3,2,1,0:T(8,128)S(1)}, f32[4,1,8,128]{3,2,1,0:T(8,128)S(1)}, u32[]{:S(2)}, u32[]{:S(2)}) collective-permute-start(f32[4,1,8,128]{3,2,1,0:T(8,128)S(1)} %get-tuple-element.262), channel_id=1, source_target_pairs={{0,64},{64,128},{128,192},{192,256},{256,320},{320,384},{384,448},... | collective-permute-start | bytes 49160 | tf_op jit(solution)/shard_map/ppermute | solution.py:47
  181.9 6.1 %collective-permute-done.43 = f32[4,1,8,128]{3,2,1,0:T(8,128)S(1)} collective-permute-done((f32[4,1,8,128]{3,2,1,0:T(8,128)S(1)}, f32[4,1,8,128]{3,2,1,0:T(8,128)S(1)}, u32[]{:S(2)}, u32[]{:S(2)}) %collective-permute-start.43) | collective-permute-done | bytes 16416 | tf_op jit(solution)/shard_map/ppermute | solution.py:48
  190.1 4.3 %collective-permute-start.45 = (f32[4,6,1,128]{3,2,1,0:T(1,128)S(1)}, f32[4,6,1,128]{3,2,1,0:T(1,128)S(1)}, u32[]{:S(2)}, u32[]{:S(2)}) collective-permute-start(f32[4,6,1,128]{3,2,1,0:T(1,128)S(1)} %get-tuple-element.244), channel_id=1, source_target_pairs={{8,0},{16,8},{24,16},{32,24},{40,32},{48,40},{56,48},{9,1},{17,9},... | collective-permute-start | bytes 36872 | tf_op jit(solution)/shard_map/ppermute | solution.py:48
  197.7 6.0 %collective-permute-start.18 = (f32[10,1,8,128]{3,2,1,0:T(8,128)S(1)}, f32[10,1,8,128]{3,2,1,0:T(8,128)S(1)}, u32[]{:S(2)}, u32[]{:S(2)}) collective-permute-start(f32[10,1,8,128]{3,2,1,0:T(8,128)S(1)} %get-tuple-element.232), channel_id=1, source_target_pairs={{0,64},{64,128},{128,192},{192,256},{256,320},{320,384},{384,448},... | collective-permute-start | bytes 122888 | tf_op jit(solution)/shard_map/ppermute | solution.py:47
  203.9 6.9 %collective-permute-start.46 = (f32[4,6,10,1]{3,2,1,0:T(8,128)S(1)}, f32[4,6,10,1]{3,2,1,0:T(8,128)S(1)}, u32[]{:S(2)}, u32[]{:S(2)}) collective-permute-start(f32[4,6,10,1]{3,2,1,0:T(8,128)S(1)} %get-tuple-element.217), channel_id=1, source_target_pairs={{0,1},{1,2},{2,3},{3,4},{4,5},{5,6},{6,7},{8,9},{9,10},{10,11},{11... | collective-permute-start | bytes 2888 | tf_op jit(solution)/shard_map/ppermute | solution.py:47
  213.4 4.4 %collective-permute-done.47 = f32[4,6,10,1]{3,2,1,0:T(8,128)S(1)} collective-permute-done((f32[4,6,10,1]{3,2,1,0:T(8,128)S(1)}, f32[4,6,10,1]{3,2,1,0:T(8,128)S(1)}, u32[]{:S(2)}, u32[]{:S(2)}) %collective-permute-start.47) | collective-permute-done | bytes 992 | tf_op jit(solution)/shard_map/ppermute | solution.py:48
  231.9 4.8 %collective-permute-done.23 = f32[10,6,10,1]{3,2,1,0:T(8,128)S(1)} collective-permute-done((f32[10,6,10,1]{3,2,1,0:T(8,128)S(1)}, f32[10,6,10,1]{3,2,1,0:T(8,128)S(1)}, u32[]{:S(2)}, u32[]{:S(2)}) %collective-permute-start.23) | collective-permute-done | bytes 2432 | tf_op jit(solution)/shard_map/ppermute | solution.py:48
  241.2 6.8 %collective-permute-start.48 = (f32[4,1,8,128]{3,2,1,0:T(8,128)S(1)}, f32[4,1,8,128]{3,2,1,0:T(8,128)S(1)}, u32[]{:S(2)}, u32[]{:S(2)}) collective-permute-start(f32[4,1,8,128]{3,2,1,0:T(8,128)S(1)} %get-tuple-element.259), channel_id=1, source_target_pairs={{0,64},{64,128},{128,192},{192,256},{256,320},{320,384},{384,448},... | collective-permute-start | bytes 49160 | tf_op jit(solution)/shard_map/ppermute | solution.py:47
  251.4 5.0 %collective-permute-done.49 = f32[4,1,8,128]{3,2,1,0:T(8,128)S(1)} collective-permute-done((f32[4,1,8,128]{3,2,1,0:T(8,128)S(1)}, f32[4,1,8,128]{3,2,1,0:T(8,128)S(1)}, u32[]{:S(2)}, u32[]{:S(2)}) %collective-permute-start.49) | collective-permute-done | bytes 16416 | tf_op jit(solution)/shard_map/ppermute | solution.py:48
  258.6 4.3 %collective-permute-start.51 = (f32[4,6,1,128]{3,2,1,0:T(1,128)S(1)}, f32[4,6,1,128]{3,2,1,0:T(1,128)S(1)}, u32[]{:S(2)}, u32[]{:S(2)}) collective-permute-start(f32[4,6,1,128]{3,2,1,0:T(1,128)S(1)} %get-tuple-element.242), channel_id=1, source_target_pairs={{8,0},{16,8},{24,16},{32,24},{40,32},{48,40},{56,48},{9,1},{17,9},... | collective-permute-start | bytes 36872 | tf_op jit(solution)/shard_map/ppermute | solution.py:48
  263.0 4.2 %collective-permute-start.25 = (f32[10,1,8,128]{3,2,1,0:T(8,128)S(1)}, f32[10,1,8,128]{3,2,1,0:T(8,128)S(1)}, u32[]{:S(2)}, u32[]{:S(2)}) collective-permute-start(f32[10,1,8,128]{3,2,1,0:T(8,128)S(1)} %get-tuple-element.227), channel_id=1, source_target_pairs={{64,0},{128,64},{192,128},{256,192},{320,256},{384,320},{448,384},... | collective-permute-start | bytes 122888 | tf_op jit(solution)/shard_map/ppermute | solution.py:48
  267.2 5.0 %collective-permute-start.24 = (f32[10,1,8,128]{3,2,1,0:T(8,128)S(1)}, f32[10,1,8,128]{3,2,1,0:T(8,128)S(1)}, u32[]{:S(2)}, u32[]{:S(2)}) collective-permute-start(f32[10,1,8,128]{3,2,1,0:T(8,128)S(1)} %get-tuple-element.228), channel_id=1, source_target_pairs={{0,64},{64,128},{128,192},{192,256},{256,320},{320,384},{384,448},... | collective-permute-start | bytes 122888 | tf_op jit(solution)/shard_map/ppermute | solution.py:47
  272.4 6.9 %collective-permute-start.52 = (f32[4,6,10,1]{3,2,1,0:T(8,128)S(1)}, f32[4,6,10,1]{3,2,1,0:T(8,128)S(1)}, u32[]{:S(2)}, u32[]{:S(2)}) collective-permute-start(f32[4,6,10,1]{3,2,1,0:T(8,128)S(1)} %get-tuple-element.215), channel_id=1, source_target_pairs={{0,1},{1,2},{2,3},{3,4},{4,5},{5,6},{6,7},{8,9},{9,10},{10,11},{11... | collective-permute-start | bytes 2888 | tf_op jit(solution)/shard_map/ppermute | solution.py:47
  282.3 4.0 %collective-permute-done.53 = f32[4,6,10,1]{3,2,1,0:T(8,128)S(1)} collective-permute-done((f32[4,6,10,1]{3,2,1,0:T(8,128)S(1)}, f32[4,6,10,1]{3,2,1,0:T(8,128)S(1)}, u32[]{:S(2)}, u32[]{:S(2)}) %collective-permute-start.53) | collective-permute-done | bytes 992 | tf_op jit(solution)/shard_map/ppermute | solution.py:48
  301.8 4.8 %collective-permute-done.29 = f32[10,6,10,1]{3,2,1,0:T(8,128)S(1)} collective-permute-done((f32[10,6,10,1]{3,2,1,0:T(8,128)S(1)}, f32[10,6,10,1]{3,2,1,0:T(8,128)S(1)}, u32[]{:S(2)}, u32[]{:S(2)}) %collective-permute-start.29) | collective-permute-done | bytes 2432 | tf_op jit(solution)/shard_map/ppermute | solution.py:48
  (241 shorter events, 124.4 us)
Async XLA Ops:
  1.4 33.6 %collective-permute-start = (f32[2,1,8,128]{3,2,1,0:T(8,128)S(1)}, f32[2,1,8,128]{3,2,1,0:T(8,128)S(1)}, u32[]{:S(2)}, u32[]{:S(2)}) collective-permute-start(f32[2,1,8,128]{3,2,1,0:T(8,128)S(1)} %get-tuple-element.273), channel_id=1, source_target_pairs={{0,64},{64,128},{128,192},{192,256},{256,320},{320,384},{384,448},... | collective-permute-start | bytes 24584 | tf_op jit(solution)/shard_map/ppermute | solution.py:47
  14.8 20.3 %collective-permute-start.1 = (f32[2,1,8,128]{3,2,1,0:T(8,128)S(1)}, f32[2,1,8,128]{3,2,1,0:T(8,128)S(1)}, u32[]{:S(2)}, u32[]{:S(2)}) collective-permute-start(f32[2,1,8,128]{3,2,1,0:T(8,128)S(1)} %get-tuple-element.274), channel_id=1, source_target_pairs={{64,0},{128,64},{192,128},{256,192},{320,256},{384,320},{448,384},... | collective-permute-start | bytes 24584 | tf_op jit(solution)/shard_map/ppermute | solution.py:48
  18.6 37.1 %collective-permute-start.30 = (f32[4,1,8,128]{3,2,1,0:T(8,128)S(1)}, f32[4,1,8,128]{3,2,1,0:T(8,128)S(1)}, u32[]{:S(2)}, u32[]{:S(2)}) collective-permute-start(f32[4,1,8,128]{3,2,1,0:T(8,128)S(1)} %get-tuple-element.268), channel_id=1, source_target_pairs={{0,64},{64,128},{128,192},{192,256},{256,320},{320,384},{384,448},... | collective-permute-start | bytes 49160 | tf_op jit(solution)/shard_map/ppermute | solution.py:47
  25.9 29.9 %collective-permute-start.31 = (f32[4,1,8,128]{3,2,1,0:T(8,128)S(1)}, f32[4,1,8,128]{3,2,1,0:T(8,128)S(1)}, u32[]{:S(2)}, u32[]{:S(2)}) collective-permute-start(f32[4,1,8,128]{3,2,1,0:T(8,128)S(1)} %get-tuple-element.269), channel_id=1, source_target_pairs={{64,0},{128,64},{192,128},{256,192},{320,256},{384,320},{448,384},... | collective-permute-start | bytes 49160 | tf_op jit(solution)/shard_map/ppermute | solution.py:48
  28.7 46.1 %collective-permute-start.7 = (f32[10,1,8,128]{3,2,1,0:T(8,128)S(1)}, f32[10,1,8,128]{3,2,1,0:T(8,128)S(1)}, u32[]{:S(2)}, u32[]{:S(2)}) collective-permute-start(f32[10,1,8,128]{3,2,1,0:T(8,128)S(1)} %get-tuple-element.239), channel_id=1, source_target_pairs={{64,0},{128,64},{192,128},{256,192},{320,256},{384,320},{448,384},... | collective-permute-start | bytes 122888 | tf_op jit(solution)/shard_map/ppermute | solution.py:48
  51.6 23.2 %collective-permute-start.6 = (f32[10,1,8,128]{3,2,1,0:T(8,128)S(1)}, f32[10,1,8,128]{3,2,1,0:T(8,128)S(1)}, u32[]{:S(2)}, u32[]{:S(2)}) collective-permute-start(f32[10,1,8,128]{3,2,1,0:T(8,128)S(1)} %get-tuple-element.240), channel_id=1, source_target_pairs={{0,64},{64,128},{128,192},{192,256},{256,320},{320,384},{384,448},... | collective-permute-start | bytes 122888 | tf_op jit(solution)/shard_map/ppermute | solution.py:47
  86.1 10.4 %collective-permute-start.11 = (f32[10,6,10,1]{3,2,1,0:T(8,128)S(1)}, f32[10,6,10,1]{3,2,1,0:T(8,128)S(1)}, u32[]{:S(2)}, u32[]{:S(2)}) collective-permute-start(f32[10,6,10,1]{3,2,1,0:T(8,128)S(1)} %get-tuple-element.173), channel_id=1, source_target_pairs={{1,0},{2,1},{3,2},{4,3},{5,4},{6,5},{7,6},{9,8},{10,9},{11,10},{12... | collective-permute-start | bytes 7208 | tf_op jit(solution)/shard_map/ppermute | solution.py:48
  88.0 9.4 %collective-permute-start.10 = (f32[10,6,10,1]{3,2,1,0:T(8,128)S(1)}, f32[10,6,10,1]{3,2,1,0:T(8,128)S(1)}, u32[]{:S(2)}, u32[]{:S(2)}) collective-permute-start(f32[10,6,10,1]{3,2,1,0:T(8,128)S(1)} %get-tuple-element.174), channel_id=1, source_target_pairs={{0,1},{1,2},{2,3},{3,4},{4,5},{5,6},{6,7},{8,9},{9,10},{10,11},{11... | collective-permute-start | bytes 7208 | tf_op jit(solution)/shard_map/ppermute | solution.py:47
  101.1 10.9 %collective-permute-start.36 = (f32[4,1,8,128]{3,2,1,0:T(8,128)S(1)}, f32[4,1,8,128]{3,2,1,0:T(8,128)S(1)}, u32[]{:S(2)}, u32[]{:S(2)}) collective-permute-start(f32[4,1,8,128]{3,2,1,0:T(8,128)S(1)} %get-tuple-element.265), channel_id=1, source_target_pairs={{0,64},{64,128},{128,192},{192,256},{256,320},{320,384},{384,448},... | collective-permute-start | bytes 49160 | tf_op jit(solution)/shard_map/ppermute | solution.py:47
  118.5 15.7 %collective-permute-start.38 = (f32[4,6,1,128]{3,2,1,0:T(1,128)S(1)}, f32[4,6,1,128]{3,2,1,0:T(1,128)S(1)}, u32[]{:S(2)}, u32[]{:S(2)}) collective-permute-start(f32[4,6,1,128]{3,2,1,0:T(1,128)S(1)} %get-tuple-element.245), channel_id=1, source_target_pairs={{0,8},{8,16},{16,24},{24,32},{32,40},{40,48},{48,56},{1,9},{9,17},... | collective-permute-start | bytes 36872 | tf_op jit(solution)/shard_map/ppermute | solution.py:47
  120.4 13.8 %collective-permute-start.39 = (f32[4,6,1,128]{3,2,1,0:T(1,128)S(1)}, f32[4,6,1,128]{3,2,1,0:T(1,128)S(1)}, u32[]{:S(2)}, u32[]{:S(2)}) collective-permute-start(f32[4,6,1,128]{3,2,1,0:T(1,128)S(1)} %get-tuple-element.246), channel_id=1, source_target_pairs={{8,0},{16,8},{24,16},{32,24},{40,32},{48,40},{56,48},{9,1},{17,9},... | collective-permute-start | bytes 36872 | tf_op jit(solution)/shard_map/ppermute | solution.py:48
  125.0 23.6 %collective-permute-start.13 = (f32[10,1,8,128]{3,2,1,0:T(8,128)S(1)}, f32[10,1,8,128]{3,2,1,0:T(8,128)S(1)}, u32[]{:S(2)}, u32[]{:S(2)}) collective-permute-start(f32[10,1,8,128]{3,2,1,0:T(8,128)S(1)} %get-tuple-element.235), channel_id=1, source_target_pairs={{64,0},{128,64},{192,128},{256,192},{320,256},{384,320},{448,384},... | collective-permute-start | bytes 122888 | tf_op jit(solution)/shard_map/ppermute | solution.py:48
  127.8 20.8 %collective-permute-start.12 = (f32[10,1,8,128]{3,2,1,0:T(8,128)S(1)}, f32[10,1,8,128]{3,2,1,0:T(8,128)S(1)}, u32[]{:S(2)}, u32[]{:S(2)}) collective-permute-start(f32[10,1,8,128]{3,2,1,0:T(8,128)S(1)} %get-tuple-element.236), channel_id=1, source_target_pairs={{0,64},{64,128},{128,192},{192,256},{256,320},{320,384},{384,448},... | collective-permute-start | bytes 122888 | tf_op jit(solution)/shard_map/ppermute | solution.py:47
  134.4 9.5 %collective-permute-start.40 = (f32[4,6,10,1]{3,2,1,0:T(8,128)S(1)}, f32[4,6,10,1]{3,2,1,0:T(8,128)S(1)}, u32[]{:S(2)}, u32[]{:S(2)}) collective-permute-start(f32[4,6,10,1]{3,2,1,0:T(8,128)S(1)} %get-tuple-element.219), channel_id=1, source_target_pairs={{0,1},{1,2},{2,3},{3,4},{4,5},{5,6},{6,7},{8,9},{9,10},{10,11},{11... | collective-permute-start | bytes 2888 | tf_op jit(solution)/shard_map/ppermute | solution.py:47
  156.7 10.4 %collective-permute-start.17 = (f32[10,6,10,1]{3,2,1,0:T(8,128)S(1)}, f32[10,6,10,1]{3,2,1,0:T(8,128)S(1)}, u32[]{:S(2)}, u32[]{:S(2)}) collective-permute-start(f32[10,6,10,1]{3,2,1,0:T(8,128)S(1)} %get-tuple-element.171), channel_id=1, source_target_pairs={{1,0},{2,1},{3,2},{4,3},{5,4},{6,5},{7,6},{9,8},{10,9},{11,10},{12... | collective-permute-start | bytes 7208 | tf_op jit(solution)/shard_map/ppermute | solution.py:48
  158.6 9.4 %collective-permute-start.16 = (f32[10,6,10,1]{3,2,1,0:T(8,128)S(1)}, f32[10,6,10,1]{3,2,1,0:T(8,128)S(1)}, u32[]{:S(2)}, u32[]{:S(2)}) collective-permute-start(f32[10,6,10,1]{3,2,1,0:T(8,128)S(1)} %get-tuple-element.172), channel_id=1, source_target_pairs={{0,1},{1,2},{2,3},{3,4},{4,5},{5,6},{6,7},{8,9},{9,10},{10,11},{11... | collective-permute-start | bytes 7208 | tf_op jit(solution)/shard_map/ppermute | solution.py:47
  171.7 10.1 %collective-permute-start.42 = (f32[4,1,8,128]{3,2,1,0:T(8,128)S(1)}, f32[4,1,8,128]{3,2,1,0:T(8,128)S(1)}, u32[]{:S(2)}, u32[]{:S(2)}) collective-permute-start(f32[4,1,8,128]{3,2,1,0:T(8,128)S(1)} %get-tuple-element.262), channel_id=1, source_target_pairs={{0,64},{64,128},{128,192},{192,256},{256,320},{320,384},{384,448},... | collective-permute-start | bytes 49160 | tf_op jit(solution)/shard_map/ppermute | solution.py:47
  188.0 15.7 %collective-permute-start.44 = (f32[4,6,1,128]{3,2,1,0:T(1,128)S(1)}, f32[4,6,1,128]{3,2,1,0:T(1,128)S(1)}, u32[]{:S(2)}, u32[]{:S(2)}) collective-permute-start(f32[4,6,1,128]{3,2,1,0:T(1,128)S(1)} %get-tuple-element.243), channel_id=1, source_target_pairs={{0,8},{8,16},{16,24},{24,32},{32,40},{40,48},{48,56},{1,9},{9,17},... | collective-permute-start | bytes 36872 | tf_op jit(solution)/shard_map/ppermute | solution.py:47
  190.1 13.6 %collective-permute-start.45 = (f32[4,6,1,128]{3,2,1,0:T(1,128)S(1)}, f32[4,6,1,128]{3,2,1,0:T(1,128)S(1)}, u32[]{:S(2)}, u32[]{:S(2)}) collective-permute-start(f32[4,6,1,128]{3,2,1,0:T(1,128)S(1)} %get-tuple-element.244), channel_id=1, source_target_pairs={{8,0},{16,8},{24,16},{32,24},{40,32},{48,40},{56,48},{9,1},{17,9},... | collective-permute-start | bytes 36872 | tf_op jit(solution)/shard_map/ppermute | solution.py:48
  194.5 23.6 %collective-permute-start.19 = (f32[10,1,8,128]{3,2,1,0:T(8,128)S(1)}, f32[10,1,8,128]{3,2,1,0:T(8,128)S(1)}, u32[]{:S(2)}, u32[]{:S(2)}) collective-permute-start(f32[10,1,8,128]{3,2,1,0:T(8,128)S(1)} %get-tuple-element.231), channel_id=1, source_target_pairs={{64,0},{128,64},{192,128},{256,192},{320,256},{384,320},{448,384},... | collective-permute-start | bytes 122888 | tf_op jit(solution)/shard_map/ppermute | solution.py:48
  197.7 20.4 %collective-permute-start.18 = (f32[10,1,8,128]{3,2,1,0:T(8,128)S(1)}, f32[10,1,8,128]{3,2,1,0:T(8,128)S(1)}, u32[]{:S(2)}, u32[]{:S(2)}) collective-permute-start(f32[10,1,8,128]{3,2,1,0:T(8,128)S(1)} %get-tuple-element.232), channel_id=1, source_target_pairs={{0,64},{64,128},{128,192},{192,256},{256,320},{320,384},{384,448},... | collective-permute-start | bytes 122888 | tf_op jit(solution)/shard_map/ppermute | solution.py:47
  203.9 9.5 %collective-permute-start.46 = (f32[4,6,10,1]{3,2,1,0:T(8,128)S(1)}, f32[4,6,10,1]{3,2,1,0:T(8,128)S(1)}, u32[]{:S(2)}, u32[]{:S(2)}) collective-permute-start(f32[4,6,10,1]{3,2,1,0:T(8,128)S(1)} %get-tuple-element.217), channel_id=1, source_target_pairs={{0,1},{1,2},{2,3},{3,4},{4,5},{5,6},{6,7},{8,9},{9,10},{10,11},{11... | collective-permute-start | bytes 2888 | tf_op jit(solution)/shard_map/ppermute | solution.py:47
  226.2 10.4 %collective-permute-start.23 = (f32[10,6,10,1]{3,2,1,0:T(8,128)S(1)}, f32[10,6,10,1]{3,2,1,0:T(8,128)S(1)}, u32[]{:S(2)}, u32[]{:S(2)}) collective-permute-start(f32[10,6,10,1]{3,2,1,0:T(8,128)S(1)} %get-tuple-element.169), channel_id=1, source_target_pairs={{1,0},{2,1},{3,2},{4,3},{5,4},{6,5},{7,6},{9,8},{10,9},{11,10},{12... | collective-permute-start | bytes 7208 | tf_op jit(solution)/shard_map/ppermute | solution.py:48
  228.1 9.4 %collective-permute-start.22 = (f32[10,6,10,1]{3,2,1,0:T(8,128)S(1)}, f32[10,6,10,1]{3,2,1,0:T(8,128)S(1)}, u32[]{:S(2)}, u32[]{:S(2)}) collective-permute-start(f32[10,6,10,1]{3,2,1,0:T(8,128)S(1)} %get-tuple-element.170), channel_id=1, source_target_pairs={{0,1},{1,2},{2,3},{3,4},{4,5},{5,6},{6,7},{8,9},{9,10},{10,11},{11... | collective-permute-start | bytes 7208 | tf_op jit(solution)/shard_map/ppermute | solution.py:47
  241.2 10.1 %collective-permute-start.48 = (f32[4,1,8,128]{3,2,1,0:T(8,128)S(1)}, f32[4,1,8,128]{3,2,1,0:T(8,128)S(1)}, u32[]{:S(2)}, u32[]{:S(2)}) collective-permute-start(f32[4,1,8,128]{3,2,1,0:T(8,128)S(1)} %get-tuple-element.259), channel_id=1, source_target_pairs={{0,64},{64,128},{128,192},{192,256},{256,320},{320,384},{384,448},... | collective-permute-start | bytes 49160 | tf_op jit(solution)/shard_map/ppermute | solution.py:47
  256.4 15.7 %collective-permute-start.50 = (f32[4,6,1,128]{3,2,1,0:T(1,128)S(1)}, f32[4,6,1,128]{3,2,1,0:T(1,128)S(1)}, u32[]{:S(2)}, u32[]{:S(2)}) collective-permute-start(f32[4,6,1,128]{3,2,1,0:T(1,128)S(1)} %get-tuple-element.241), channel_id=1, source_target_pairs={{0,8},{8,16},{16,24},{24,32},{32,40},{40,48},{48,56},{1,9},{9,17},... | collective-permute-start | bytes 36872 | tf_op jit(solution)/shard_map/ppermute | solution.py:47
  258.6 13.6 %collective-permute-start.51 = (f32[4,6,1,128]{3,2,1,0:T(1,128)S(1)}, f32[4,6,1,128]{3,2,1,0:T(1,128)S(1)}, u32[]{:S(2)}, u32[]{:S(2)}) collective-permute-start(f32[4,6,1,128]{3,2,1,0:T(1,128)S(1)} %get-tuple-element.242), channel_id=1, source_target_pairs={{8,0},{16,8},{24,16},{32,24},{40,32},{48,40},{56,48},{9,1},{17,9},... | collective-permute-start | bytes 36872 | tf_op jit(solution)/shard_map/ppermute | solution.py:48
  263.0 25.0 %collective-permute-start.25 = (f32[10,1,8,128]{3,2,1,0:T(8,128)S(1)}, f32[10,1,8,128]{3,2,1,0:T(8,128)S(1)}, u32[]{:S(2)}, u32[]{:S(2)}) collective-permute-start(f32[10,1,8,128]{3,2,1,0:T(8,128)S(1)} %get-tuple-element.227), channel_id=1, source_target_pairs={{64,0},{128,64},{192,128},{256,192},{320,256},{384,320},{448,384},... | collective-permute-start | bytes 122888 | tf_op jit(solution)/shard_map/ppermute | solution.py:48
  267.2 20.8 %collective-permute-start.24 = (f32[10,1,8,128]{3,2,1,0:T(8,128)S(1)}, f32[10,1,8,128]{3,2,1,0:T(8,128)S(1)}, u32[]{:S(2)}, u32[]{:S(2)}) collective-permute-start(f32[10,1,8,128]{3,2,1,0:T(8,128)S(1)} %get-tuple-element.228), channel_id=1, source_target_pairs={{0,64},{64,128},{128,192},{192,256},{256,320},{320,384},{384,448},... | collective-permute-start | bytes 122888 | tf_op jit(solution)/shard_map/ppermute | solution.py:47
  272.4 10.0 %collective-permute-start.52 = (f32[4,6,10,1]{3,2,1,0:T(8,128)S(1)}, f32[4,6,10,1]{3,2,1,0:T(8,128)S(1)}, u32[]{:S(2)}, u32[]{:S(2)}) collective-permute-start(f32[4,6,10,1]{3,2,1,0:T(8,128)S(1)} %get-tuple-element.215), channel_id=1, source_target_pairs={{0,1},{1,2},{2,3},{3,4},{4,5},{5,6},{6,7},{8,9},{9,10},{10,11},{11... | collective-permute-start | bytes 2888 | tf_op jit(solution)/shard_map/ppermute | solution.py:47
  296.1 10.4 %collective-permute-start.29 = (f32[10,6,10,1]{3,2,1,0:T(8,128)S(1)}, f32[10,6,10,1]{3,2,1,0:T(8,128)S(1)}, u32[]{:S(2)}, u32[]{:S(2)}) collective-permute-start(f32[10,6,10,1]{3,2,1,0:T(8,128)S(1)} %get-tuple-element.167), channel_id=1, source_target_pairs={{1,0},{2,1},{3,2},{4,3},{5,4},{6,5},{7,6},{9,8},{10,9},{11,10},{12... | collective-permute-start | bytes 7208 | tf_op jit(solution)/shard_map/ppermute | solution.py:48
  298.0 9.4 %collective-permute-start.28 = (f32[10,6,10,1]{3,2,1,0:T(8,128)S(1)}, f32[10,6,10,1]{3,2,1,0:T(8,128)S(1)}, u32[]{:S(2)}, u32[]{:S(2)}) collective-permute-start(f32[10,6,10,1]{3,2,1,0:T(8,128)S(1)} %get-tuple-element.168), channel_id=1, source_target_pairs={{0,1},{1,2},{2,3},{3,4},{4,5},{5,6},{6,7},{8,9},{9,10},{10,11},{11... | collective-permute-start | bytes 7208 | tf_op jit(solution)/shard_map/ppermute | solution.py:47
  (26 other events, 164.9 us)
where the time goes:
time: 314 us; the launch traced here: 312 us
  starting transfers between devices  212 us (68%)
  waiting for transfers between devices  73.7 us (23%)
  other arithmetic  19.5 us (6%)
  local copies, waits for them, and re-layouts  3.77 us (1%)
    ppermute x27, starting transfers between devices, padded_2(): before = lax.ppermute(last, axis, up)  133 us
    ppermute x27, starting transfers between devices, padded_2(): after = lax.ppermute(leading, axis, down)  79.1 us
    ppermute x27, waiting for transfers between devices, padded_2(): after = lax.ppermute(leading, axis, down)  56.6 us
    ppermute x27, waiting for transfers between devices, padded_2(): before = lax.ppermute(last, axis, up)  17.1 us
    unnamed x56, other arithmetic  13.8 us
  transfers between devices with their start and end apart: 54, of which 26 were waited for; matrix products, arithmetic and copies ran while one was open for 2% of the time, Pallas kernels for 0%

commit v1 on v0

v1 whole, which is shorter than its diff:
```python
import jax
import jax.numpy as jnp
from jax import lax
from jax.experimental import pallas as pl
from jax.experimental.pallas import tpu as pltpu
from jax.sharding import PartitionSpec as P

STEPS = 4
DEEP = 4
KEEP_FLOW = 1.0 - 1.0 / 0.8
KEEP_SPECIES = 1.0 - 1.0 / 0.7
REACT_RATE = 0.5
GRAVITY = 0.001
MOVING = [
    (1, 0, 0),
    (-1, 0, 0),
    (0, 1, 0),
    (0, -1, 0),
    (0, 0, 1),
    (0, 0, -1),
    (1, 1, 0),
    (-1, -1, 0),
    (1, -1, 0),
    (-1, 1, 0),
    (1, 0, 1),
    (-1, 0, -1),
    (1, 0, -1),
    (-1, 0, 1),
    (0, 1, 1),
    (0, -1, -1),
    (0, 1, -1),
    (0, -1, 1),
]
NFLOW = 18
NSPEC = 6
SPECIES_WEIGHT = 0.125
INPLANE = [(0, 0), (1, 0), (-1, 0), (0, 1), (0, -1), (1, 1), (-1, -1), (1, -1), (-1, 1)]
PLANE_OF = {shift: place for place, shift in enumerate(INPLANE)}
FIELDS = 15
FLUID = 14
ROWS = 8
LANES = 128


def opposite(index):
    return index ^ 1


def flow_populations(m):
    third = m[0] * (1.0 / 3.0)
    axx, ayy, azz = m[4] - third, m[5] - third, m[6] - third
    base = m[0] - 1.5 * (axx + ayy + azz)
    sides = (4.5 * axx, 4.5 * ayy, 4.5 * azz)
    drift = [m[1 + k] * (1.0 / 12.0) for k in range(3)]
    moving = []
    lifted = [base + side for side in sides]
    for k in range(3):
        even, odd = lifted[k] * (1.0 / 18.0), m[1 + k] * (1.0 / 6.0)
        moving += [even + odd, even - odd]
    for a, b, cross in ((0, 1, 7), (0, 2, 8), (1, 2, 9)):
        both = (lifted[a] + sides[b]) * (1.0 / 36.0)
        mixed = m[cross] * 0.25
        same, differ = both + mixed, both - mixed
        plus, minus = drift[a] + drift[b], drift[a] - drift[b]
        moving += [same + plus, same - plus, differ + minus, differ - minus]
    return base * (1.0 / 3.0), moving


def species_populations(s):
    part = s[0] * SPECIES_WEIGHT
    moving = []
    for k in range(3):
        odd = s[1 + k] * 0.5
        moving += [part + odd, part - odd]
    return s[0] * 0.25, moving


def collide(flow, species):
    rho = flow[0]
    j = flow[1:4]
    third = rho * (1.0 / 3.0)
    equil = [third + j[0] * j[0], third + j[1] * j[1], third + j[2] * j[2], j[0] * j[1], j[0] * j[2], j[1] * j[2]]
    stress = [KEEP_FLOW * flow[4 + k] + (1.0 - KEEP_FLOW) * equil[k] for k in range(6)]
    conc = species[0]
    flux = [KEEP_SPECIES * species[1 + k] + (1.0 - KEEP_SPECIES) * (conc * j[k]) for k in range(3)]
    return [rho] + list(j) + stress + [conc] + flux


def pass_on(post, arriving, flags, arriving_species, slow, fluid):
    rest, own = flow_populations(post[:10])
    f = [jnp.where(flags(c) > 0.5, arriving(c), own[opposite(c)]) for c in range(NFLOW)]
    total = [f[2 * k] + f[2 * k + 1] for k in range(9)]
    diff = [f[2 * k] - f[2 * k + 1] for k in range(9)]
    xy, xz, yz = total[3] + total[4], total[5] + total[6], total[7] + total[8]
    rho = rest + (total[0] + total[1] + total[2]) + (xy + xz + yz)
    jx = diff[0] + (diff[3] + diff[4]) + (diff[5] + diff[6]) + GRAVITY
    jy = diff[1] + (diff[3] - diff[4]) + (diff[7] + diff[8])
    jz = diff[2] + (diff[5] - diff[6]) + (diff[7] - diff[8])
    flow = [
        rho,
        jx,
        jy,
        jz,
        total[0] + xy + xz,
        total[1] + xy + yz,
        total[2] + xz + yz,
        total[3] - total[4],
        total[5] - total[6],
        total[7] - total[8],
    ]
    flow = [value * fluid for value in flow]
    rest, own = species_populations(post[10:14])
    g = []
    for c in range(NSPEC):
        back = own[opposite(c)]
        g.append(jnp.where(flags(c) > 0.5, arriving_species(c), back + slow(c) * (SPECIES_WEIGHT - back)))
    conc = rest + (g[0] + g[1]) + (g[2] + g[3]) + (g[4] + g[5])
    species = [conc, g[0] - g[1], g[2] - g[3], g[4] - g[5]]
    return flow, [value * fluid for value in species]


def lanes_of(shape):
    return lax.broadcasted_iota(jnp.int32, shape, len(shape) - 1)


def rows_of(shape):
    return lax.broadcasted_iota(jnp.int32, shape, len(shape) - 2)


def roll(value, shift, axis):
    size = value.shape[axis]
    if isinstance(shift, int):
        shift = shift % size
        if shift == 0:
            return value
    return pltpu.roll(value, shift, axis)


def edge_lanes(layers, field):
    shape = layers[0].shape
    slot = lanes_of(shape) // 8
    first = 4 * (field % 4)
    out = jnp.zeros(shape, jnp.float32)
    for x, layer in enumerate(layers):
        out = jnp.where(slot == first + x, roll(layer, 8 * (first + x) + 4, len(shape) - 1), out)
    return out


def start_kernel(flow_ref, species_ref, fluid_ref, react_ref, block_ref, edge_ref):
    for x in range(DEEP):
        fluid = fluid_ref[x].astype(jnp.float32)
        react = react_ref[x].astype(jnp.float32)
        flow = [flow_ref[k, x] * fluid for k in range(10)]
        species = [species_ref[k, x] * fluid for k in range(4)]
        post = collide(flow, species)
        block_ref[0, x] = jnp.where(fluid > 0.5, post[0], react)
        for k in range(1, 14):
            block_ref[k, x] = post[k]
        block_ref[FLUID, x] = fluid
    for tile in range(4):
        packed = jnp.zeros((ROWS, LANES), jnp.float32)
        for field in range(4 * tile, min(4 * tile + 4, FIELDS)):
            packed = packed + edge_lanes([block_ref[field, x] for x in range(DEEP)], field)
        edge_ref[tile] = packed


def rows_kernel(own_ref, left_ref, right_ref, strip_ref, strip_left_ref, strip_right_ref, up_ref, down_ref):
    high = rows_of((ROWS, LANES)) >= 4

    def put(place, one, two):
        two = roll(two, 4, 0)
        up_ref[place] = jnp.where(high, one, two)
        down_ref[place] = jnp.where(high, two, one)

    layers = [(ref, x) for ref in (left_ref, own_ref, right_ref) for x in range(DEEP)]
    for field in range(FIELDS):
        for k in range(6):
            (one, a), (two, b) = layers[k], layers[k + 6]
            put(field * 6 + k, one[field, a], two[field, b])
    tiles = [(ref, t) for ref in (strip_left_ref, strip_ref, strip_right_ref) for t in range(4)]
    for k in range(6):
        (one, a), (two, b) = tiles[k], tiles[k + 6]
        put(FIELDS * 6 + k, one[a], two[b])


def steps_kernel(
    own_ref,
    left_ref,
    right_ref,
    strip_ref,
    strip_left_ref,
    strip_right_ref,
    up_ref,
    down_ref,
    flow_out,
    species_out,
    dissolved_out,
    state,
    fluid_at,
    slow_at,
    sent,
    halo,
    strips,
    strip_fluid,
    strip_slow,
    strip_sent,
    released,
):
    tall = (2 * ROWS, LANES)
    low_rows = rows_of((ROWS, LANES)) < 4
    lane = lanes_of(tall)
    slot_lane = lanes_of((ROWS, LANES)) % 8
    blocks = (left_ref, own_ref, right_ref)

    def halves(place):
        up, down = up_ref[place], down_ref[place]
        return jnp.where(low_rows, down, up), roll(jnp.where(low_rows, up, down), 4, 0)

    for field in range(FIELDS):
        for x in range(12):
            state[field, x, 0:ROWS] = blocks[x // 4][field, x % 4]
        for k in range(6):
            one, two = halves(field * 6 + k)
            state[field, k, ROWS : 2 * ROWS] = one
            state[field, k + 6, ROWS : 2 * ROWS] = two
    strip_blocks = (strip_left_ref, strip_ref, strip_right_ref)
    for place in range(12):
        halo[place, 0:ROWS] = strip_blocks[place // 4][place % 4]
    for k in range(6):
        one, two = halves(FIELDS * 6 + k)
        halo[k, ROWS : 2 * ROWS] = one
        halo[k + 6, ROWS : 2 * ROWS] = two

    inner = lanes_of(tall) % 8 < 4
    group = lanes_of(tall) // 32
    for field in range(FIELDS):
        low = jnp.zeros(tall, jnp.float32)
        far = jnp.zeros(tall, jnp.float32)
        for b, target in ((0, 3), (1, 0), (2, 1)):
            edge = edge_lanes([state[field, 4 * b + x] for x in range(DEEP)], 0)
            edge = roll(edge, 32 * target, 1)
            beyond = roll(halo[4 * b + field // 4], 32 * ((target - field % 4) % 4), 1)
            here = group == target
            low = jnp.where(here, jnp.where(inner, beyond, edge), low)
            far = jnp.where(here, jnp.where(inner, edge, beyond), far)
        strips[0, field] = low
        strips[1, field] = far

    def split_first(value, fluid):
        return value * fluid, REACT_RATE * value * (1.0 - fluid)

    def strip_moved(value, c):
        cx, cy, cz = MOVING[c]
        return roll(roll(value, 8 * cx + cz, 1), cy, 0)

    strip_slow_here = []
    for side in range(2):
        fluid = strips[side, FLUID]
        rho, slow = split_first(strips[side, 0], fluid)
        strips[side, 0] = rho
        strip_slow_here.append(slow)
        for c in range(NFLOW):
            strip_fluid[side, c] = strip_moved(fluid, c)
        for c in range(NSPEC):
            strip_slow[side, c] = strip_moved(slow, c)

    def from_strip(value, x, cz):
        slot = lax.rem(x + 12, 16)
        if cz > 0:
            return pltpu.roll(value, lax.rem(125 + 128 - 8 * slot, 128), 1)
        return pltpu.roll(value, lax.rem(123 + 128 - 8 * slot, 128), 1)

    def moved(value, x, cy, cz, strip_value):
        if cz > 0:
            value = jnp.where(lane == 0, from_strip(strip_value, x, 1), roll(value, 1, 1))
        elif cz < 0:
            value = jnp.where(lane == LANES - 1, from_strip(strip_value, x, -1), roll(value, -1, 1))
        return roll(value, cy, 0)

    def side_of(cz):
        return 0 if cz > 0 else 1

    def flags_at(x, carry):
        fluid = state[FLUID, x]
        rho, slow = split_first(state[0, x], fluid)
        state[0, x] = rho
        for place, (cy, cz) in enumerate(INPLANE):
            fluid_at[place, x] = moved(fluid, x, cy, cz, strips[side_of(cz), FLUID])
            if place < 5:
                slow_at[place, x] = moved(slow, x, cy, cz, strip_slow_here[side_of(cz)])
        return carry

    lax.fori_loop(0, 12, flags_at, 0)
    for x in range(DEEP, 2 * DEEP):
        released[x] = jnp.zeros((ROWS, LANES), jnp.float32)

    for step in range(STEPS):
        last = step == STEPS - 1
        for side in range(2):
            post = [strips[side, k] for k in range(14)]
            _, flow_pops = flow_populations(post[:10])
            _, species_pops = species_populations(post[10:])
            for c in range(NFLOW):
                if MOVING[c][2] == (1, -1)[side]:
                    strip_sent[c] = flow_pops[c]
                    if c < NSPEC:
                        strip_sent[NFLOW + c] = species_pops[c]
            if not last:
                new_flow, new_species = pass_on(
                    post,
                    lambda c: strip_moved(flow_pops[c], c),
                    lambda c: strip_fluid[side, c],
                    lambda c: strip_moved(species_pops[c], c),
                    lambda c: strip_slow[side, c],
                    strips[side, FLUID],
                )
                for k, value in enumerate(collide(new_flow, new_species)):
                    strips[side, k] = value

        def send(x, carry):
            _, flow_pops = flow_populations([state[k, x] for k in range(10)])
            _, species_pops = species_populations([state[k, x] for k in range(10, 14)])
            for c in range(NFLOW):
                _, cy, cz = MOVING[c]
                sent[c, x] = moved(flow_pops[c], x, cy, cz, strip_sent[c] if cz else None)
            for c in range(NSPEC):
                _, cy, cz = MOVING[c]
                sent[NFLOW + c, x] = moved(species_pops[c], x, cy, cz, strip_sent[NFLOW + c] if cz else None)
            return carry

        lax.fori_loop(step, 12 - step, send, 0)
        height = ROWS if last else 2 * ROWS

        def receive(x, carry):
            def at(ref, place, c):
                return ref[place, x - MOVING[c][0], 0:height]

            post = [state[k, x, 0:height] for k in range(14)]
            new_flow, new_species = pass_on(
                post,
                lambda c: at(sent, c, c),
                lambda c: at(fluid_at, PLANE_OF[MOVING[c][1:]], c),
                lambda c: at(sent, NFLOW + c, c),
                lambda c: at(slow_at, PLANE_OF[MOVING[c][1:]], c),
                state[FLUID, x, 0:height],
            )
            if last:
                for k in range(10):
                    flow_out[k, x - DEEP] = new_flow[k]
                for k in range(4):
                    species_out[k, x - DEEP] = new_species[k]
            else:
                for k, value in enumerate(collide(new_flow, new_species)):
                    state[k, x] = value
            return carry

        lax.fori_loop(step + 1, 11 - step, receive, 0)

        def release(x, carry):
            parts = [sent[NFLOW + c, x - MOVING[c][0], 0:ROWS] for c in range(NSPEC)]
            released[x] = released[x] + ((parts[0] + parts[1]) + (parts[2] + parts[3]) + (parts[4] + parts[5]))
            return carry

        lax.fori_loop(DEEP, 2 * DEEP, release, 0)

    for x in range(DEEP, 2 * DEEP):
        near = [fluid_at[PLANE_OF[MOVING[c][1:]], x - MOVING[c][0], 0:ROWS] for c in range(NSPEC)]
        count = (near[0] + near[1]) + (near[2] + near[3]) + (near[4] + near[5])
        slow = slow_at[PLANE_OF[(0, 0)], x, 0:ROWS]
        dissolved_out[x - DEEP] = slow * (STEPS * SPECIES_WEIGHT * count - released[x])


def shifted(value, axis, wrap):
    count = lax.axis_size(axis)
    up = [(i, (i + 1) % count) for i in range(count if wrap else count - 1)]
    down = [(j, i) for i, j in up]
    return lax.ppermute(value, axis, up), lax.ppermute(value, axis, down)


def vmem(count):
    return [pl.BlockSpec(memory_space=pltpu.VMEM)] * count


def per_device(flow_moments, species_moments, fluid_mask, reactive_mask):
    f32 = jnp.float32
    params = pltpu.CompilerParams(vmem_limit_bytes=24 * 1024 * 1024)
    block, edge = pl.pallas_call(
        start_kernel,
        out_shape=(
            jax.ShapeDtypeStruct((FIELDS, DEEP, ROWS, LANES), f32),
            jax.ShapeDtypeStruct((4, ROWS, LANES), f32),
        ),
        in_specs=vmem(4),
        out_specs=tuple(vmem(2)),
        compiler_params=params,
    )(flow_moments, species_moments, fluid_mask, reactive_mask)
    left, right = shifted(block, "gx", True)
    below, above = shifted(edge, "gz", False)
    strip = jnp.where(lanes_of(edge.shape) % 8 < 4, below, above)
    strip_left, strip_right = shifted(strip, "gx", True)
    tiles = jax.ShapeDtypeStruct((FIELDS * 6 + 6, ROWS, LANES), f32)
    to_up, to_down = pl.pallas_call(
        rows_kernel,
        out_shape=(tiles, tiles),
        in_specs=vmem(6),
        out_specs=tuple(vmem(2)),
        compiler_params=params,
    )(block, left, right, strip, strip_left, strip_right)
    count = lax.axis_size("gy")
    from_low = lax.ppermute(to_up, "gy", [(i, i + 1) for i in range(count - 1)])
    from_high = lax.ppermute(to_down, "gy", [(i + 1, i) for i in range(count - 1)])
    tall = (2 * ROWS, LANES)
    return pl.pallas_call(
        steps_kernel,
        out_shape=(
            jax.ShapeDtypeStruct(flow_moments.shape, f32),
            jax.ShapeDtypeStruct(species_moments.shape, f32),
            jax.ShapeDtypeStruct(fluid_mask.shape, f32),
        ),
        in_specs=vmem(8),
        out_specs=tuple(vmem(3)),
        scratch_shapes=[
            pltpu.VMEM((FIELDS, 12) + tall, f32),
            pltpu.VMEM((9, 12) + tall, f32),
            pltpu.VMEM((5, 12) + tall, f32),
            pltpu.VMEM((NFLOW + NSPEC, 12) + tall, f32),
            pltpu.VMEM((12,) + tall, f32),
            pltpu.VMEM((2, FIELDS) + tall, f32),
            pltpu.VMEM((2, NFLOW) + tall, f32),
            pltpu.VMEM((2, NSPEC) + tall, f32),
            pltpu.VMEM((NFLOW + NSPEC,) + tall, f32),
            pltpu.VMEM((12, ROWS, LANES), f32),
        ],
        compiler_params=params,
    )(block, left, right, strip, strip_left, strip_right, from_low, from_high)


def solution(mesh):
    return jax.shard_map(
        per_device,
        mesh=mesh,
        in_specs=(
            P(None, "gx", "gy", "gz"),
            P(None, "gx", "gy", "gz"),
            P("gx", "gy", "gz"),
            P("gx", "gy", "gz"),
        ),
        out_specs=(P(None, "gx", "gy", "gz"), P(None, "gx", "gy", "gz"), P("gx", "gy", "gz")),
        check_vma=False,
    )
```

time: 314 us -> 79.7 us (0.25)
  the two profiles are of different devices: /device:TPU:199 before, /device:TPU:62 now
where the time goes in v1:
time: 79.7 us; the launch traced here: 79.2 us
  starting transfers between devices  39.4 us (49%)
  waiting for transfers between devices  24.4 us (31%)
  Pallas kernels  11.5 us (14%)
  local copies, waits for them, and re-layouts  3.18 us (4%)
    ppermute x6, starting transfers between devices, shifted(): return (lax.ppermute(value, axis, up), lax.ppermute(value, axis, down))  32.7 us
    ppermute x6, waiting for transfers between devices, shifted(): return (lax.ppermute(value, axis, up), lax.ppermute(value, axis, down))  12.2 us
    pallas_call x1, Pallas kernels, per_device(): pl.pallas_call(steps_kernel, out_shape=(jax.ShapeDtypeStruct(flow_moments...  11.3 us
    ppermute x1, waiting for transfers between devices, per_device(): from_low = lax.ppermute(to_up, 'gy', [(i, i + 1) for i in range(count - 1)])  6.9 us
    ppermute x1, waiting for transfers between devices, per_device(): lax.ppermute(to_down, 'gy', [(i + 1, i) for i in range(count - 1)])  5.33 us
    ppermute x1, starting transfers between devices, per_device(): from_low = lax.ppermute(to_up, 'gy', [(i, i + 1) for i in range(count - 1)])  4.81 us
    unnamed x8, local copies, waits for them, and re-layouts  3.18 us
    ppermute x1, starting transfers between devices, per_device(): lax.ppermute(to_down, 'gy', [(i + 1, i) for i in range(count - 1)])  1.92 us
  transfers between devices with their start and end apart: 8, of which 4 were waited for; matrix products, arithmetic and copies ran while one was open for 0% of the time, Pallas kernels for 0%

profile of v1, /device:TPU:62, one launch (start us, length us, event | category | flops | bytes accessed | tf_op | source)
XLA Modules:
  0.0 79.2 jit_solution(3829147078048037843)
XLA Ops:
  0.6 0.0 copy-start
  0.6 0.9 %copy-done = f32[10,4,8,128]{3,2,1,0:T(8,128)S(1)} copy-done((f32[10,4,8,128]{3,2,1,0:T(8,128)S(1)}, f32[10,4,8,128]{3,2,1,0:T(8,128)}, u32[]{:S(2)}) %copy-start) | copy-done | bytes 163864
  1.5 0.0 copy-start.1
  1.6 0.8 %copy-done.1 = f32[4,4,8,128]{3,2,1,0:T(8,128)S(1)} copy-done((f32[4,4,8,128]{3,2,1,0:T(8,128)S(1)}, f32[4,4,8,128]{3,2,1,0:T(8,128)}, u32[]{:S(2)}) %copy-start.1) | copy-done | bytes 65560
  2.4 0.0 copy-start.2
  2.4 0.7 copy-done.2
  3.1 0.0 copy-start.3
  3.1 0.7 copy-done.3
  3.8 0.1 shard_map.67
  4.0 1.3 %collective-permute-start.3 = (f32[4,8,128]{2,1,0:T(8,128)S(1)}, f32[4,8,128]{2,1,0:T(8,128)S(1)}, u32[]{:S(2)}, u32[]{:S(2)}) collective-permute-start(f32[4,8,128]{2,1,0:T(8,128)S(1)} %get-tuple-element.8), channel_id=1, source_target_pairs={{1,0},{2,1},{3,2},{4,3},{5,4},{6,5},{7,6},{9,8},{10,9},{11,10},{12... | collective-permute-start | bytes 49160 | tf_op jit(solution)/shard_map/ppermute | solution.py:377
  5.3 3.0 %collective-permute-start.2 = (f32[4,8,128]{2,1,0:T(8,128)S(1)}, f32[4,8,128]{2,1,0:T(8,128)S(1)}, u32[]{:S(2)}, u32[]{:S(2)}) collective-permute-start(f32[4,8,128]{2,1,0:T(8,128)S(1)} %get-tuple-element.8), channel_id=1, source_target_pairs={{0,1},{1,2},{2,3},{3,4},{4,5},{5,6},{6,7},{8,9},{9,10},{10,11},{11... | collective-permute-start | bytes 49160 | tf_op jit(solution)/shard_map/ppermute | solution.py:377
  8.3 15.4 %collective-permute-start.1 = (f32[15,4,8,128]{3,2,1,0:T(8,128)S(1)}, f32[15,4,8,128]{3,2,1,0:T(8,128)S(1)}, u32[]{:S(2)}, u32[]{:S(2)}) collective-permute-start(f32[15,4,8,128]{3,2,1,0:T(8,128)S(1)} %get-tuple-element.7.own_ref), channel_id=1, source_target_pairs={{64,0},{128,64},{192,128},{256,192},{320,256},{384,320},{448,384},... | collective-permute-start | bytes 737288 | tf_op jit(solution)/shard_map/ppermute | solution.py:377
  23.7 1.9 %collective-permute-start = (f32[15,4,8,128]{3,2,1,0:T(8,128)S(1)}, f32[15,4,8,128]{3,2,1,0:T(8,128)S(1)}, u32[]{:S(2)}, u32[]{:S(2)}) collective-permute-start(f32[15,4,8,128]{3,2,1,0:T(8,128)S(1)} %get-tuple-element.7.own_ref), channel_id=1, source_target_pairs={{0,64},{64,128},{128,192},{192,256},{256,320},{320,384},{384,448},... | collective-permute-start | bytes 737288 | tf_op jit(solution)/shard_map/ppermute | solution.py:377
  25.7 0.0 collective-permute-done.3
  25.7 0.0 collective-permute-done.2
  25.7 8.7 %collective-permute-start.5 = (f32[4,8,128]{2,1,0:T(8,128)S(1)}, f32[4,8,128]{2,1,0:T(8,128)S(1)}, u32[]{:S(2)}, u32[]{:S(2)}) collective-permute-start(f32[4,8,128]{2,1,0:T(8,128)S(1)} %fusion.strip_ref), channel_id=1, source_target_pairs={{64,0},{128,64},{192,128},{256,192},{320,256},{384,320},{448,384},... | collective-permute-start | bytes 49160 | tf_op jit(solution)/shard_map/ppermute | solution.py:377
  34.5 2.3 %collective-permute-start.4 = (f32[4,8,128]{2,1,0:T(8,128)S(1)}, f32[4,8,128]{2,1,0:T(8,128)S(1)}, u32[]{:S(2)}, u32[]{:S(2)}) collective-permute-start(f32[4,8,128]{2,1,0:T(8,128)S(1)} %fusion.strip_ref), channel_id=1, source_target_pairs={{0,64},{64,128},{128,192},{192,256},{256,320},{320,384},{384,448},... | collective-permute-start | bytes 49160 | tf_op jit(solution)/shard_map/ppermute | solution.py:377
  36.7 10.5 %collective-permute-done.5.strip_right_ref = f32[4,8,128]{2,1,0:T(8,128)S(1)} collective-permute-done((f32[4,8,128]{2,1,0:T(8,128)S(1)}, f32[4,8,128]{2,1,0:T(8,128)S(1)}, u32[]{:S(2)}, u32[]{:S(2)}) %collective-permute-start.5) | collective-permute-done | bytes 16416 | tf_op jit(solution)/shard_map/ppermute | solution.py:377
  47.3 1.6 %collective-permute-done.4.strip_left_ref = f32[4,8,128]{2,1,0:T(8,128)S(1)} collective-permute-done((f32[4,8,128]{2,1,0:T(8,128)S(1)}, f32[4,8,128]{2,1,0:T(8,128)S(1)}, u32[]{:S(2)}, u32[]{:S(2)}) %collective-permute-start.4) | collective-permute-done | bytes 16416 | tf_op jit(solution)/shard_map/ppermute | solution.py:377
  48.9 0.0 collective-permute-done.1.right_ref
  48.9 0.0 collective-permute-done.left_ref
  48.9 0.1 shard_map.68
  49.0 4.8 %collective-permute-start.6 = (f32[96,8,128]{2,1,0:T(8,128)S(1)}, f32[96,8,128]{2,1,0:T(8,128)S(1)}, u32[]{:S(2)}, u32[]{:S(2)}) collective-permute-start(f32[96,8,128]{2,1,0:T(8,128)S(1)} %get-tuple-element.9), channel_id=1, source_target_pairs={{0,8},{8,16},{16,24},{24,32},{32,40},{40,48},{48,56},{1,9},{9,17},... | collective-permute-start | bytes 1179656 | tf_op jit(solution)/shard_map/ppermute | solution.py:410
  53.8 1.9 %collective-permute-start.7 = (f32[96,8,128]{2,1,0:T(8,128)S(1)}, f32[96,8,128]{2,1,0:T(8,128)S(1)}, u32[]{:S(2)}, u32[]{:S(2)}) collective-permute-start(f32[96,8,128]{2,1,0:T(8,128)S(1)} %get-tuple-element.10), channel_id=1, source_target_pairs={{8,0},{16,8},{24,16},{32,24},{40,32},{48,40},{56,48},{9,1},{17,9},... | collective-permute-start | bytes 1179656 | tf_op jit(solution)/shard_map/ppermute | solution.py:411
  55.7 6.9 %collective-permute-done.6.up_ref = f32[96,8,128]{2,1,0:T(8,128)S(1)} collective-permute-done((f32[96,8,128]{2,1,0:T(8,128)S(1)}, f32[96,8,128]{2,1,0:T(8,128)S(1)}, u32[]{:S(2)}, u32[]{:S(2)}) %collective-permute-start.6) | collective-permute-done | bytes 393248 | tf_op jit(solution)/shard_map/ppermute | solution.py:410
  62.6 5.3 %collective-permute-done.7.down_ref = f32[96,8,128]{2,1,0:T(8,128)S(1)} collective-permute-done((f32[96,8,128]{2,1,0:T(8,128)S(1)}, f32[96,8,128]{2,1,0:T(8,128)S(1)}, u32[]{:S(2)}, u32[]{:S(2)}) %collective-permute-start.7) | collective-permute-done | bytes 393248 | tf_op jit(solution)/shard_map/ppermute | solution.py:411
  67.9 11.3 %shard_map.69 = (f32[10,4,8,128]{3,2,1,0:T(8,128)}, f32[4,4,8,128]{3,2,1,0:T(8,128)}, f32[4,8,128]{2,1,0:T(8,128)}) custom-call(f32[15,4,8,128]{3,2,1,0:T(8,128)S(1)} %get-tuple-element.7.own_ref, f32[15,4,8,128]{3,2,1,0:T(8,128)S(1)} %collective-permute-done.left_ref, f32[15,4,8,128]{3,2,1,0:T(8,128)S(1)} %collective-permute-done.1.right_ref, ...), custom_call_target="tpu_custom_call" | custom-call | tf_op jit(solution)/shard_map/pallas_call | solution.py:413
  (3 shorter events, 0.0 us)
Async XLA Ops:
  0.6 0.9 %copy-start = (f32[10,4,8,128]{3,2,1,0:T(8,128)S(1)}, f32[10,4,8,128]{3,2,1,0:T(8,128)}, u32[]{:S(2)}) copy-start(f32[10,4,8,128]{3,2,1,0:T(8,128)} %flow_ref.1) | copy-start | bytes 491524
  1.5 0.8 %copy-start.1 = (f32[4,4,8,128]{3,2,1,0:T(8,128)S(1)}, f32[4,4,8,128]{3,2,1,0:T(8,128)}, u32[]{:S(2)}) copy-start(f32[4,4,8,128]{3,2,1,0:T(8,128)} %species_ref.1) | copy-start | bytes 196612
  2.4 0.7 copy-start.2
  3.1 0.7 copy-start.3
  4.0 21.7 %collective-permute-start.3 = (f32[4,8,128]{2,1,0:T(8,128)S(1)}, f32[4,8,128]{2,1,0:T(8,128)S(1)}, u32[]{:S(2)}, u32[]{:S(2)}) collective-permute-start(f32[4,8,128]{2,1,0:T(8,128)S(1)} %get-tuple-element.8), channel_id=1, source_target_pairs={{1,0},{2,1},{3,2},{4,3},{5,4},{6,5},{7,6},{9,8},{10,9},{11,10},{12... | collective-permute-start | bytes 49160 | tf_op jit(solution)/shard_map/ppermute | solution.py:377
  5.3 20.4 %collective-permute-start.2 = (f32[4,8,128]{2,1,0:T(8,128)S(1)}, f32[4,8,128]{2,1,0:T(8,128)S(1)}, u32[]{:S(2)}, u32[]{:S(2)}) collective-permute-start(f32[4,8,128]{2,1,0:T(8,128)S(1)} %get-tuple-element.8), channel_id=1, source_target_pairs={{0,1},{1,2},{2,3},{3,4},{4,5},{5,6},{6,7},{8,9},{9,10},{10,11},{11... | collective-permute-start | bytes 49160 | tf_op jit(solution)/shard_map/ppermute | solution.py:377
  8.3 40.6 %collective-permute-start.1 = (f32[15,4,8,128]{3,2,1,0:T(8,128)S(1)}, f32[15,4,8,128]{3,2,1,0:T(8,128)S(1)}, u32[]{:S(2)}, u32[]{:S(2)}) collective-permute-start(f32[15,4,8,128]{3,2,1,0:T(8,128)S(1)} %get-tuple-element.7.own_ref), channel_id=1, source_target_pairs={{64,0},{128,64},{192,128},{256,192},{320,256},{384,320},{448,384},... | collective-permute-start | bytes 737288 | tf_op jit(solution)/shard_map/ppermute | solution.py:377
  23.7 25.2 %collective-permute-start = (f32[15,4,8,128]{3,2,1,0:T(8,128)S(1)}, f32[15,4,8,128]{3,2,1,0:T(8,128)S(1)}, u32[]{:S(2)}, u32[]{:S(2)}) collective-permute-start(f32[15,4,8,128]{3,2,1,0:T(8,128)S(1)} %get-tuple-element.7.own_ref), channel_id=1, source_target_pairs={{0,64},{64,128},{128,192},{192,256},{256,320},{320,384},{384,448},... | collective-permute-start | bytes 737288 | tf_op jit(solution)/shard_map/ppermute | solution.py:377
  25.7 21.5 %collective-permute-start.5 = (f32[4,8,128]{2,1,0:T(8,128)S(1)}, f32[4,8,128]{2,1,0:T(8,128)S(1)}, u32[]{:S(2)}, u32[]{:S(2)}) collective-permute-start(f32[4,8,128]{2,1,0:T(8,128)S(1)} %fusion.strip_ref), channel_id=1, source_target_pairs={{64,0},{128,64},{192,128},{256,192},{320,256},{384,320},{448,384},... | collective-permute-start | bytes 49160 | tf_op jit(solution)/shard_map/ppermute | solution.py:377
  34.5 14.4 %collective-permute-start.4 = (f32[4,8,128]{2,1,0:T(8,128)S(1)}, f32[4,8,128]{2,1,0:T(8,128)S(1)}, u32[]{:S(2)}, u32[]{:S(2)}) collective-permute-start(f32[4,8,128]{2,1,0:T(8,128)S(1)} %fusion.strip_ref), channel_id=1, source_target_pairs={{0,64},{64,128},{128,192},{192,256},{256,320},{320,384},{384,448},... | collective-permute-start | bytes 49160 | tf_op jit(solution)/shard_map/ppermute | solution.py:377
  49.0 13.6 %collective-permute-start.6 = (f32[96,8,128]{2,1,0:T(8,128)S(1)}, f32[96,8,128]{2,1,0:T(8,128)S(1)}, u32[]{:S(2)}, u32[]{:S(2)}) collective-permute-start(f32[96,8,128]{2,1,0:T(8,128)S(1)} %get-tuple-element.9), channel_id=1, source_target_pairs={{0,8},{8,16},{16,24},{24,32},{32,40},{40,48},{48,56},{1,9},{9,17},... | collective-permute-start | bytes 1179656 | tf_op jit(solution)/shard_map/ppermute | solution.py:410
  53.8 14.2 %collective-permute-start.7 = (f32[96,8,128]{2,1,0:T(8,128)S(1)}, f32[96,8,128]{2,1,0:T(8,128)S(1)}, u32[]{:S(2)}, u32[]{:S(2)}) collective-permute-start(f32[96,8,128]{2,1,0:T(8,128)S(1)} %get-tuple-element.10), channel_id=1, source_target_pairs={{8,0},{16,8},{24,16},{32,24},{40,32},{48,40},{56,48},{9,1},{17,9},... | collective-permute-start | bytes 1179656 | tf_op jit(solution)/shard_map/ppermute | solution.py:411

commit v2 on v1

v2 whole, which is shorter than its diff:
```python
import jax
import jax.numpy as jnp
from jax import lax
from jax.experimental import pallas as pl
from jax.experimental.pallas import tpu as pltpu
from jax.sharding import PartitionSpec as P

STEPS = 4
DEEP = 4
KEEP_FLOW = 1.0 - 1.0 / 0.8
KEEP_SPECIES = 1.0 - 1.0 / 0.7
REACT_RATE = 0.5
GRAVITY = 0.001
MOVING = [
    (1, 0, 0),
    (-1, 0, 0),
    (0, 1, 0),
    (0, -1, 0),
    (0, 0, 1),
    (0, 0, -1),
    (1, 1, 0),
    (-1, -1, 0),
    (1, -1, 0),
    (-1, 1, 0),
    (1, 0, 1),
    (-1, 0, -1),
    (1, 0, -1),
    (-1, 0, 1),
    (0, 1, 1),
    (0, -1, -1),
    (0, 1, -1),
    (0, -1, 1),
]
NFLOW = 18
NSPEC = 6
SPECIES_WEIGHT = 0.125
FIELDS = 15
FLUID = 14
ROWS = 8
LANES = 128
SOLID = float("nan")
REACTIVE = float("inf")
LARGEST = 3.0e38


def opposite(index):
    return index ^ 1


def flow_populations(m):
    third = m[0] * (1.0 / 3.0)
    axx, ayy, azz = m[4] - third, m[5] - third, m[6] - third
    base = m[0] - 1.5 * (axx + ayy + azz)
    sides = (4.5 * axx, 4.5 * ayy, 4.5 * azz)
    drift = [m[1 + k] * (1.0 / 12.0) for k in range(3)]
    moving = []
    lifted = [base + side for side in sides]
    for k in range(3):
        even, odd = lifted[k] * (1.0 / 18.0), m[1 + k] * (1.0 / 6.0)
        moving += [even + odd, even - odd]
    for a, b, cross in ((0, 1, 7), (0, 2, 8), (1, 2, 9)):
        both = (lifted[a] + sides[b]) * (1.0 / 36.0)
        mixed = m[cross] * 0.25
        same, differ = both + mixed, both - mixed
        plus, minus = drift[a] + drift[b], drift[a] - drift[b]
        moving += [same + plus, same - plus, differ + minus, differ - minus]
    return base * (1.0 / 3.0), moving


def species_populations(s):
    part = s[0] * SPECIES_WEIGHT
    moving = []
    for k in range(3):
        odd = s[1 + k] * 0.5
        moving += [part + odd, part - odd]
    return s[0] * 0.25, moving


def collide(flow, species):
    rho = flow[0]
    j = flow[1:4]
    third = rho * (1.0 / 3.0)
    equil = [third + j[0] * j[0], third + j[1] * j[1], third + j[2] * j[2], j[0] * j[1], j[0] * j[2], j[1] * j[2]]
    stress = [KEEP_FLOW * flow[4 + k] + (1.0 - KEEP_FLOW) * equil[k] for k in range(6)]
    conc = species[0]
    flux = [KEEP_SPECIES * species[1 + k] + (1.0 - KEEP_SPECIES) * (conc * j[k]) for k in range(3)]
    return [rho] + list(j) + stress + [conc] + flux


def is_number(value):
    return value < LARGEST


def pass_on(post, arriving, arriving_species):
    rest, own = flow_populations(post[:10])
    f = []
    for c in range(NFLOW):
        value = arriving(c)
        f.append(jnp.where(is_number(value), value, own[opposite(c)]))
    total = [f[2 * k] + f[2 * k + 1] for k in range(9)]
    diff = [f[2 * k] - f[2 * k + 1] for k in range(9)]
    xy, xz, yz = total[3] + total[4], total[5] + total[6], total[7] + total[8]
    rho = rest + (total[0] + total[1] + total[2]) + (xy + xz + yz)
    jx = diff[0] + (diff[3] + diff[4]) + (diff[5] + diff[6]) + GRAVITY
    jy = diff[1] + (diff[3] - diff[4]) + (diff[7] + diff[8])
    jz = diff[2] + (diff[5] - diff[6]) + (diff[7] - diff[8])
    flow = [
        rho,
        jx,
        jy,
        jz,
        total[0] + xy + xz,
        total[1] + xy + yz,
        total[2] + xz + yz,
        total[3] - total[4],
        total[5] - total[6],
        total[7] - total[8],
    ]
    rest, own = species_populations(post[10:14])
    g = []
    for c in range(NSPEC):
        value = arriving_species(c)
        back = own[opposite(c)]
        slow = jnp.where(value > LARGEST, REACT_RATE, 0.0)
        g.append(jnp.where(is_number(value), value, back + slow * (SPECIES_WEIGHT - back)))
    conc = rest + (g[0] + g[1]) + (g[2] + g[3]) + (g[4] + g[5])
    return flow, [conc, g[0] - g[1], g[2] - g[3], g[4] - g[5]]


def next_post(post, flow, species):
    fluid = is_number(post[0])
    new = collide(flow, species)
    new[0] = jnp.where(fluid, new[0], post[0])
    new[10] = jnp.where(fluid, new[10], post[10])
    for k in range(11, 14):
        new[k] = jnp.where(fluid, new[k], 0.0)
    return new


def lanes_of(shape):
    return lax.broadcasted_iota(jnp.int32, shape, len(shape) - 1)


def rows_of(shape):
    return lax.broadcasted_iota(jnp.int32, shape, len(shape) - 2)


def roll(value, shift, axis):
    size = value.shape[axis]
    if isinstance(shift, int):
        shift = shift % size
        if shift == 0:
            return value
    return pltpu.roll(value, shift, axis)


def first_slot():
    return 4 * lax.rem(lax.axis_index("gx"), 4)


def start_kernel(flow_in, species_in, fluid_in, react_in, block_ref, edge_ref, flow_ref, species_ref, fluid_ref, react_ref, done):
    pairs = ((flow_in, flow_ref), (species_in, species_ref), (fluid_in, fluid_ref), (react_in, react_ref))
    copies = [pltpu.make_async_copy(one, two, done.at[k]) for k, (one, two) in enumerate(pairs)]
    for copy in copies:
        copy.start()
    for copy in copies:
        copy.wait()
    slot_of = lanes_of((ROWS, LANES)) // 8
    edges = [jnp.zeros((ROWS, LANES), jnp.float32)] * FIELDS
    for x in range(DEEP):
        slot = first_slot() + x
        fluid = fluid_ref[x].astype(jnp.float32)
        react = react_ref[x].astype(jnp.float32)
        flow = [flow_ref[k, x] * fluid for k in range(10)]
        species = [species_ref[k, x] * fluid for k in range(4)]
        post = collide(flow, species)
        post[0] = jnp.where(fluid > 0.5, post[0], react)
        for k, value in enumerate(post + [fluid]):
            value = roll(value, 8 * slot + 4, 1)
            block_ref[k, x] = value
            edges[k] = jnp.where(slot_of == slot, value, edges[k])
    for tile in range(4):
        packed = jnp.zeros((ROWS, LANES), jnp.float32)
        for field in range(4 * tile, min(4 * tile + 4, FIELDS)):
            packed = packed + roll(edges[field], 32 * (field % 4), 1)
        edge_ref[tile] = packed


def join_kernel(below_ref, above_ref, block_in, strip_ref, block_ref, done):
    copy = pltpu.make_async_copy(block_in, block_ref, done)
    copy.start()
    for tile in range(4):
        strip_ref[tile] = jnp.where(lanes_of((ROWS, LANES)) % 8 < 4, below_ref[tile], above_ref[tile])
    copy.wait()


def put_rows(up_ref, down_ref, place, one, two):
    high = rows_of((ROWS, LANES)) >= 4
    two = roll(two, 4, 0)
    up_ref[place] = jnp.where(high, one, two)
    down_ref[place] = jnp.where(high, two, one)


def rows_kernel(own_ref, left_ref, right_ref, up_ref, down_ref):
    layers = [(ref, x) for ref in (left_ref, own_ref, right_ref) for x in range(DEEP)]
    for field in range(FIELDS):
        for k in range(6):
            (one, a), (two, b) = layers[k], layers[k + 6]
            put_rows(up_ref, down_ref, field * 6 + k, one[field, a], two[field, b])


def strip_rows_kernel(up_in, down_in, strip_ref, strip_left_ref, strip_right_ref, up_ref, down_ref):
    tiles = [(ref, t) for ref in (strip_left_ref, strip_ref, strip_right_ref) for t in range(4)]
    for k in range(6):
        (one, a), (two, b) = tiles[k], tiles[k + 6]
        put_rows(up_ref, down_ref, FIELDS * 6 + k, one[a], two[b])


def steps_kernel(
    own_ref,
    left_ref,
    right_ref,
    strip_ref,
    strip_left_ref,
    strip_right_ref,
    up_ref,
    down_ref,
    flow_out,
    species_out,
    dissolved_out,
    state,
    sent,
    halo,
    strips,
    strip_sent,
    released,
):
    tall = (2 * ROWS, LANES)
    low_rows = rows_of((ROWS, LANES)) < 4
    lane = lanes_of(tall)
    blocks = (left_ref, own_ref, right_ref)

    def halves(place):
        up, down = up_ref[place], down_ref[place]
        return jnp.where(low_rows, down, up), roll(jnp.where(low_rows, up, down), 4, 0)

    for field in range(FIELDS):
        for x in range(12):
            state[field, x, 0:ROWS] = blocks[x // 4][field, x % 4]
        for k in range(6):
            one, two = halves(field * 6 + k)
            state[field, k, ROWS : 2 * ROWS] = one
            state[field, k + 6, ROWS : 2 * ROWS] = two
    strip_blocks = (strip_left_ref, strip_ref, strip_right_ref)
    for place in range(12):
        halo[place, 0:ROWS] = strip_blocks[place // 4][place % 4]
    for k in range(6):
        one, two = halves(FIELDS * 6 + k)
        halo[k, ROWS : 2 * ROWS] = one
        halo[k + 6, ROWS : 2 * ROWS] = two

    inner = lane % 8 < 4

    def slot_at(x):
        return lax.rem(first_slot() + x + 12, 16)

    for field in range(FIELDS):
        edge = jnp.zeros(tall, jnp.float32)
        beyond = jnp.zeros(tall, jnp.float32)
        for x in range(12):
            edge = jnp.where(lane // 8 == slot_at(x), state[field, x], edge)
        for b in range(3):
            turned = roll(halo[4 * b + field // 4], -32 * (field % 4), 1)
            beyond = jnp.where(lane // 32 == slot_at(4 * b) // 4, turned, beyond)
        strips[0, field] = jnp.where(inner, beyond, edge)
        strips[1, field] = jnp.where(inner, edge, beyond)

    def marked(first, conc, fluid):
        solid = fluid < 0.5
        mark = jnp.where(first > 0.5, REACTIVE, SOLID)
        return jnp.where(solid, SOLID, first), jnp.where(solid, mark, conc)

    for side in range(2):
        rho, conc = marked(strips[side, 0], strips[side, 10], strips[side, FLUID])
        strips[side, 0] = rho
        strips[side, 10] = conc
    for x in range(12):
        rho, conc = marked(state[0, x], state[10, x], state[FLUID, x])
        state[0, x] = rho
        state[10, x] = conc

    def strip_moved(value, c):
        cx, cy, cz = MOVING[c]
        return roll(roll(value, 8 * cx + cz, 1), cy, 0)

    def moved(value, x, c, strip_value):
        cz = MOVING[c][2]
        if cz:
            end = 8 * slot_at(x) + (3 if cz > 0 else 4)
            value = jnp.where(lane == end, strip_value, value)
        return strip_moved(value, c)

    def turned_back(value, x):
        return roll(value, 124 - 8 * slot_at(x), 1)

    for x in range(DEEP, 2 * DEEP):
        released[x] = jnp.zeros((ROWS, LANES), jnp.float32)

    for step in range(STEPS):
        last = step == STEPS - 1
        for side in range(2):
            post = [strips[side, k] for k in range(14)]
            _, flow_pops = flow_populations(post[:10])
            _, species_pops = species_populations(post[10:])
            for c in range(NFLOW):
                if MOVING[c][2] == (1, -1)[side]:
                    strip_sent[c] = flow_pops[c]
                    if c < NSPEC:
                        strip_sent[NFLOW + c] = species_pops[c]
            if not last:
                new_flow, new_species = pass_on(
                    post,
                    lambda c: strip_moved(flow_pops[c], c),
                    lambda c: strip_moved(species_pops[c], c),
                )
                for k, value in enumerate(next_post(post, new_flow, new_species)):
                    strips[side, k] = value

        def send(x):
            _, flow_pops = flow_populations([state[k, x] for k in range(10)])
            _, species_pops = species_populations([state[k, x] for k in range(10, 14)])
            for c in range(NFLOW):
                sent[c, x] = moved(flow_pops[c], x, c, strip_sent[c] if MOVING[c][2] else None)
            for c in range(NSPEC):
                sent[NFLOW + c, x] = moved(species_pops[c], x, c, strip_sent[NFLOW + c] if MOVING[c][2] else None)

        for x in range(step, 12 - step):
            send(x)
        height = ROWS if last else 2 * ROWS

        def receive(x):
            post = [state[k, x, 0:height] for k in range(14)]
            new_flow, new_species = pass_on(
                post,
                lambda c: sent[c, x - MOVING[c][0], 0:height],
                lambda c: sent[NFLOW + c, x - MOVING[c][0], 0:height],
            )
            if last:
                fluid = is_number(post[0])
                for k in range(10):
                    flow_out[k, x - DEEP] = turned_back(jnp.where(fluid, new_flow[k], 0.0), x)
                for k in range(4):
                    species_out[k, x - DEEP] = turned_back(jnp.where(fluid, new_species[k], 0.0), x)
            else:
                for k, value in enumerate(next_post(post, new_flow, new_species)):
                    state[k, x] = value

        for x in range(step + 1, 11 - step):
            receive(x)

        for x in range(DEEP, 2 * DEEP):
            parts = [sent[NFLOW + c, x - MOVING[c][0], 0:ROWS] for c in range(NSPEC)]
            parts = [jnp.where(is_number(part), SPECIES_WEIGHT - part, 0.0) for part in parts]
            released[x] = released[x] + ((parts[0] + parts[1]) + (parts[2] + parts[3]) + (parts[4] + parts[5]))

    for x in range(DEEP, 2 * DEEP):
        reactive = state[10, x, 0:ROWS] > LARGEST
        dissolved_out[x - DEEP] = turned_back(jnp.where(reactive, REACT_RATE * released[x], 0.0), x)


def shifted(value, axis, wrap):
    count = lax.axis_size(axis)
    up = [(i, (i + 1) % count) for i in range(count if wrap else count - 1)]
    down = [(j, i) for i, j in up]
    return lax.ppermute(value, axis, up), lax.ppermute(value, axis, down)


def vmem(count):
    return [pl.BlockSpec(memory_space=pltpu.VMEM)] * count


def per_device(flow_moments, species_moments, fluid_mask, reactive_mask):
    f32 = jnp.float32
    params = pltpu.CompilerParams(vmem_limit_bytes=24 * 1024 * 1024)
    block, edge = pl.pallas_call(
        start_kernel,
        out_shape=(
            jax.ShapeDtypeStruct((FIELDS, DEEP, ROWS, LANES), f32),
            jax.ShapeDtypeStruct((4, ROWS, LANES), f32),
        ),
        in_specs=[pl.BlockSpec(memory_space=pltpu.HBM)] * 4,
        out_specs=tuple(vmem(2)),
        scratch_shapes=[
            pltpu.VMEM(flow_moments.shape, f32),
            pltpu.VMEM(species_moments.shape, f32),
            pltpu.VMEM(fluid_mask.shape, fluid_mask.dtype),
            pltpu.VMEM(reactive_mask.shape, reactive_mask.dtype),
            pltpu.SemaphoreType.DMA((4,)),
        ],
        compiler_params=pltpu.CompilerParams(vmem_limit_bytes=56 * 1024 * 1024),
    )(flow_moments, species_moments, fluid_mask, reactive_mask)
    left, right = shifted(block, "gx", True)
    below, above = shifted(edge, "gz", False)
    strip, block = pl.pallas_call(
        join_kernel,
        out_shape=(jax.ShapeDtypeStruct(edge.shape, f32), jax.ShapeDtypeStruct(block.shape, f32)),
        in_specs=vmem(2) + [pl.BlockSpec(memory_space=pltpu.HBM)],
        out_specs=tuple(vmem(2)),
        scratch_shapes=[pltpu.SemaphoreType.DMA],
        compiler_params=params,
        cost_estimate=pl.CostEstimate(flops=1, bytes_accessed=1, transcendentals=0),
    )(below, above, block)
    strip_left, strip_right = shifted(strip, "gx", True)
    tiles = jax.ShapeDtypeStruct((FIELDS * 6 + 6, ROWS, LANES), f32)
    to_up, to_down = pl.pallas_call(
        rows_kernel,
        out_shape=(tiles, tiles),
        in_specs=vmem(3),
        out_specs=tuple(vmem(2)),
        compiler_params=params,
        cost_estimate=pl.CostEstimate(flops=10**11, bytes_accessed=10**8, transcendentals=0),
    )(block, left, right)
    to_up, to_down = pl.pallas_call(
        strip_rows_kernel,
        out_shape=(tiles, tiles),
        in_specs=vmem(5),
        out_specs=tuple(vmem(2)),
        input_output_aliases={0: 0, 1: 1},
        compiler_params=params,
    )(to_up, to_down, strip, strip_left, strip_right)
    count = lax.axis_size("gy")
    from_low = lax.ppermute(to_up, "gy", [(i, i + 1) for i in range(count - 1)])
    from_high = lax.ppermute(to_down, "gy", [(i + 1, i) for i in range(count - 1)])
    tall = (2 * ROWS, LANES)
    return pl.pallas_call(
        steps_kernel,
        out_shape=(
            jax.ShapeDtypeStruct(flow_moments.shape, f32),
            jax.ShapeDtypeStruct(species_moments.shape, f32),
            jax.ShapeDtypeStruct(fluid_mask.shape, f32),
        ),
        in_specs=vmem(8),
        out_specs=tuple(vmem(3)),
        scratch_shapes=[
            pltpu.VMEM((FIELDS, 12) + tall, f32),
            pltpu.VMEM((NFLOW + NSPEC, 12) + tall, f32),
            pltpu.VMEM((12,) + tall, f32),
            pltpu.VMEM((2, FIELDS) + tall, f32),
            pltpu.VMEM((NFLOW + NSPEC,) + tall, f32),
            pltpu.VMEM((12, ROWS, LANES), f32),
        ],
        compiler_params=params,
    )(block, left, right, strip, strip_left, strip_right, from_low, from_high)


def solution(mesh):
    return jax.shard_map(
        per_device,
        mesh=mesh,
        in_specs=(
            P(None, "gx", "gy", "gz"),
            P(None, "gx", "gy", "gz"),
            P("gx", "gy", "gz"),
            P("gx", "gy", "gz"),
        ),
        out_specs=(P(None, "gx", "gy", "gz"), P(None, "gx", "gy", "gz"), P("gx", "gy", "gz")),
        check_vma=False,
    )
```

time: 79.7 us -> 77.9 us (0.977)
  the two profiles are of different devices: /device:TPU:62 before, /device:TPU:305 now
where the time goes in v2:
time: 77.9 us; the launch traced here: 77.5 us
  starting transfers between devices  39.2 us (50%)
  waiting for transfers between devices  30.8 us (40%)
  Pallas kernels  5.92 us (8%)
  local copies, waits for them, and re-layouts  0.95 us (1%)
    ppermute x6, starting transfers between devices, shifted(): return (lax.ppermute(value, axis, up), lax.ppermute(value, axis, down))  32.7 us
    ppermute x6, waiting for transfers between devices, shifted(): return (lax.ppermute(value, axis, up), lax.ppermute(value, axis, down))  19.9 us
    ppermute x1, waiting for transfers between devices, per_device(): from_low = lax.ppermute(to_up, 'gy', [(i, i + 1) for i in range(count - 1)])  5.6 us
    ppermute x1, waiting for transfers between devices, per_device(): lax.ppermute(to_down, 'gy', [(i + 1, i) for i in range(count - 1)])  5.31 us
    ppermute x1, starting transfers between devices, per_device(): from_low = lax.ppermute(to_up, 'gy', [(i, i + 1) for i in range(count - 1)])  4.52 us
    pallas_call x1, Pallas kernels, per_device(): pl.pallas_call(steps_kernel, out_shape=(jax.ShapeDtypeStruct(flow_moments...  3.76 us
    ppermute x1, starting transfers between devices, per_device(): lax.ppermute(to_down, 'gy', [(i + 1, i) for i in range(count - 1)])  1.92 us
    pallas_call x1, Pallas kernels, per_device(): pl.pallas_call(start_kernel, out_shape=(jax.ShapeDtypeStruct((FIELDS, DEE...  1.81 us
  transfers between devices with their start and end apart: 8, of which 4 were waited for; matrix products, arithmetic and copies ran while one was open for 0% of the time, Pallas kernels for 0%

profile of v2, /device:TPU:305, one launch (start us, length us, event | category | flops | bytes accessed | tf_op | source)
XLA Modules:
  0.0 77.5 jit_solution(14080277567965509944)
XLA Ops:
  0.6 1.8 %shard_map.67 = (f32[15,4,8,128]{3,2,1,0:T(8,128)}, f32[4,8,128]{2,1,0:T(8,128)}) custom-call(f32[10,4,8,128]{3,2,1,0:T(8,128)} %flow_in.1, f32[4,4,8,128]{3,2,1,0:T(8,128)} %species_in.1, s32[4,8,128]{2,1,0:T(8,128)} %fluid_in.1, s32[4,8,128]{2,1,0:T(8,128)} %react_in.1), custom_call_target="tpu_custom_call" | custom-call | tf_op jit(solution)/shard_map/pallas_call | solution.py:385
  2.4 14.8 %collective-permute-start.3 = (f32[15,4,8,128]{3,2,1,0:T(8,128)}, f32[15,4,8,128]{3,2,1,0:T(8,128)S(1)}, u32[]{:S(2)}, u32[]{:S(2)}) collective-permute-start(f32[15,4,8,128]{3,2,1,0:T(8,128)} %get-tuple-element.12.block_in), channel_id=1, source_target_pairs={{64,0},{128,64},{192,128},{256,192},{320,256},{384,320},{448,384},... | collective-permute-start | bytes 737288 | tf_op jit(solution)/shard_map/ppermute | solution.py:375
  17.2 1.9 %collective-permute-start.2 = (f32[15,4,8,128]{3,2,1,0:T(8,128)}, f32[15,4,8,128]{3,2,1,0:T(8,128)S(1)}, u32[]{:S(2)}, u32[]{:S(2)}) collective-permute-start(f32[15,4,8,128]{3,2,1,0:T(8,128)} %get-tuple-element.12.block_in), channel_id=1, source_target_pairs={{0,64},{64,128},{128,192},{192,256},{256,320},{320,384},{384,448},... | collective-permute-start | bytes 737288 | tf_op jit(solution)/shard_map/ppermute | solution.py:375
  19.2 2.9 %collective-permute-start.1 = (f32[4,8,128]{2,1,0:T(8,128)}, f32[4,8,128]{2,1,0:T(8,128)S(1)}, u32[]{:S(2)}, u32[]{:S(2)}) collective-permute-start(f32[4,8,128]{2,1,0:T(8,128)} %get-tuple-element.11), channel_id=1, source_target_pairs={{1,0},{2,1},{3,2},{4,3},{5,4},{6,5},{7,6},{9,8},{10,9},{11,10},{12... | collective-permute-start | bytes 49160 | tf_op jit(solution)/shard_map/ppermute | solution.py:375
  22.0 3.9 %collective-permute-start = (f32[4,8,128]{2,1,0:T(8,128)}, f32[4,8,128]{2,1,0:T(8,128)S(1)}, u32[]{:S(2)}, u32[]{:S(2)}) collective-permute-start(f32[4,8,128]{2,1,0:T(8,128)} %get-tuple-element.11), channel_id=1, source_target_pairs={{0,1},{1,2},{2,3},{3,4},{4,5},{5,6},{6,7},{8,9},{9,10},{10,11},{11... | collective-permute-start | bytes 49160 | tf_op jit(solution)/shard_map/ppermute | solution.py:375
  26.0 11.4 %collective-permute-done.1.above_ref = f32[4,8,128]{2,1,0:T(8,128)S(1)} collective-permute-done((f32[4,8,128]{2,1,0:T(8,128)}, f32[4,8,128]{2,1,0:T(8,128)S(1)}, u32[]{:S(2)}, u32[]{:S(2)}) %collective-permute-start.1) | collective-permute-done | bytes 16416 | tf_op jit(solution)/shard_map/ppermute | solution.py:375
  37.3 0.0 collective-permute-done.below_ref
  37.3 0.0 copy-start
  37.3 0.9 %copy-done = f32[15,4,8,128]{3,2,1,0:T(8,128)S(1)} copy-done((f32[15,4,8,128]{3,2,1,0:T(8,128)S(1)}, f32[15,4,8,128]{3,2,1,0:T(8,128)}, u32[]{:S(2)}) %copy-start) | copy-done | bytes 245784
  38.3 0.3 shard_map.68
  38.6 7.3 %collective-permute-start.5 = (f32[4,8,128]{2,1,0:T(8,128)S(1)}, f32[4,8,128]{2,1,0:T(8,128)S(1)}, u32[]{:S(2)}, u32[]{:S(2)}) collective-permute-start(f32[4,8,128]{2,1,0:T(8,128)S(1)} %get-tuple-element.14.strip_ref), channel_id=1, source_target_pairs={{64,0},{128,64},{192,128},{256,192},{320,256},{384,320},{448,384},... | collective-permute-start | bytes 49160 | tf_op jit(solution)/shard_map/ppermute | solution.py:375
  45.9 1.9 %collective-permute-start.4 = (f32[4,8,128]{2,1,0:T(8,128)S(1)}, f32[4,8,128]{2,1,0:T(8,128)S(1)}, u32[]{:S(2)}, u32[]{:S(2)}) collective-permute-start(f32[4,8,128]{2,1,0:T(8,128)S(1)} %get-tuple-element.14.strip_ref), channel_id=1, source_target_pairs={{0,64},{64,128},{128,192},{192,256},{256,320},{320,384},{384,448},... | collective-permute-start | bytes 49160 | tf_op jit(solution)/shard_map/ppermute | solution.py:375
  47.8 0.0 collective-permute-done.3.right_ref
  47.8 0.0 collective-permute-done.2.left_ref
  47.8 0.1 shard_map.69
  47.9 0.0 collective-permute-done.5.strip_right_ref
  47.9 8.5 %collective-permute-done.4.strip_left_ref = f32[4,8,128]{2,1,0:T(8,128)S(1)} collective-permute-done((f32[4,8,128]{2,1,0:T(8,128)S(1)}, f32[4,8,128]{2,1,0:T(8,128)S(1)}, u32[]{:S(2)}, u32[]{:S(2)}) %collective-permute-start.4) | collective-permute-done | bytes 16416 | tf_op jit(solution)/shard_map/ppermute | solution.py:375
  56.4 4.5 %collective-permute-start.6 = (f32[96,8,128]{2,1,0:T(8,128)S(1)}, f32[96,8,128]{2,1,0:T(8,128)S(1)}, u32[]{:S(2)}, u32[]{:S(2)}) collective-permute-start(f32[96,8,128]{2,1,0:T(8,128)S(1)} %get-tuple-element.17), channel_id=1, source_target_pairs={{0,8},{8,16},{16,24},{24,32},{32,40},{40,48},{48,56},{1,9},{9,17},... | collective-permute-start | bytes 1179656 | tf_op jit(solution)/shard_map/ppermute | solution.py:432
  60.9 1.9 %collective-permute-start.7 = (f32[96,8,128]{2,1,0:T(8,128)S(1)}, f32[96,8,128]{2,1,0:T(8,128)S(1)}, u32[]{:S(2)}, u32[]{:S(2)}) collective-permute-start(f32[96,8,128]{2,1,0:T(8,128)S(1)} %get-tuple-element.18), channel_id=1, source_target_pairs={{8,0},{16,8},{24,16},{32,24},{40,32},{48,40},{56,48},{9,1},{17,9},... | collective-permute-start | bytes 1179656 | tf_op jit(solution)/shard_map/ppermute | solution.py:433
  62.9 5.6 %collective-permute-done.6.up_ref = f32[96,8,128]{2,1,0:T(8,128)S(1)} collective-permute-done((f32[96,8,128]{2,1,0:T(8,128)S(1)}, f32[96,8,128]{2,1,0:T(8,128)S(1)}, u32[]{:S(2)}, u32[]{:S(2)}) %collective-permute-start.6) | collective-permute-done | bytes 393248 | tf_op jit(solution)/shard_map/ppermute | solution.py:432
  68.5 5.3 %collective-permute-done.7.down_ref = f32[96,8,128]{2,1,0:T(8,128)S(1)} collective-permute-done((f32[96,8,128]{2,1,0:T(8,128)S(1)}, f32[96,8,128]{2,1,0:T(8,128)S(1)}, u32[]{:S(2)}, u32[]{:S(2)}) %collective-permute-start.7) | collective-permute-done | bytes 393248 | tf_op jit(solution)/shard_map/ppermute | solution.py:433
  73.8 3.8 %shard_map.71 = (f32[10,4,8,128]{3,2,1,0:T(8,128)}, f32[4,4,8,128]{3,2,1,0:T(8,128)}, f32[4,8,128]{2,1,0:T(8,128)}) custom-call(f32[15,4,8,128]{3,2,1,0:T(8,128)S(1)} %get-tuple-element.13.own_ref, f32[15,4,8,128]{3,2,1,0:T(8,128)S(1)} %collective-permute-done.2.left_ref, f32[15,4,8,128]{3,2,1,0:T(8,128)S(1)} %collective-permute-done.3.right_ref, ...), custom_call_target="tpu_custom_call" | custom-call | tf_op jit(solution)/shard_map/pallas_call | solution.py:435
  (1 shorter events, 0.0 us)
Async XLA Ops:
  2.4 45.4 %collective-permute-start.3 = (f32[15,4,8,128]{3,2,1,0:T(8,128)}, f32[15,4,8,128]{3,2,1,0:T(8,128)S(1)}, u32[]{:S(2)}, u32[]{:S(2)}) collective-permute-start(f32[15,4,8,128]{3,2,1,0:T(8,128)} %get-tuple-element.12.block_in), channel_id=1, source_target_pairs={{64,0},{128,64},{192,128},{256,192},{320,256},{384,320},{448,384},... | collective-permute-start | bytes 737288 | tf_op jit(solution)/shard_map/ppermute | solution.py:375
  17.2 30.6 %collective-permute-start.2 = (f32[15,4,8,128]{3,2,1,0:T(8,128)}, f32[15,4,8,128]{3,2,1,0:T(8,128)S(1)}, u32[]{:S(2)}, u32[]{:S(2)}) collective-permute-start(f32[15,4,8,128]{3,2,1,0:T(8,128)} %get-tuple-element.12.block_in), channel_id=1, source_target_pairs={{0,64},{64,128},{128,192},{192,256},{256,320},{320,384},{384,448},... | collective-permute-start | bytes 737288 | tf_op jit(solution)/shard_map/ppermute | solution.py:375
  19.2 18.1 %collective-permute-start.1 = (f32[4,8,128]{2,1,0:T(8,128)}, f32[4,8,128]{2,1,0:T(8,128)S(1)}, u32[]{:S(2)}, u32[]{:S(2)}) collective-permute-start(f32[4,8,128]{2,1,0:T(8,128)} %get-tuple-element.11), channel_id=1, source_target_pairs={{1,0},{2,1},{3,2},{4,3},{5,4},{6,5},{7,6},{9,8},{10,9},{11,10},{12... | collective-permute-start | bytes 49160 | tf_op jit(solution)/shard_map/ppermute | solution.py:375
  22.0 15.3 %collective-permute-start = (f32[4,8,128]{2,1,0:T(8,128)}, f32[4,8,128]{2,1,0:T(8,128)S(1)}, u32[]{:S(2)}, u32[]{:S(2)}) collective-permute-start(f32[4,8,128]{2,1,0:T(8,128)} %get-tuple-element.11), channel_id=1, source_target_pairs={{0,1},{1,2},{2,3},{3,4},{4,5},{5,6},{6,7},{8,9},{9,10},{10,11},{11... | collective-permute-start | bytes 49160 | tf_op jit(solution)/shard_map/ppermute | solution.py:375
  37.3 0.9 %copy-start = (f32[15,4,8,128]{3,2,1,0:T(8,128)S(1)}, f32[15,4,8,128]{3,2,1,0:T(8,128)}, u32[]{:S(2)}) copy-start(f32[15,4,8,128]{3,2,1,0:T(8,128)} %get-tuple-element.12.block_in) | copy-start | bytes 737284
  38.6 9.3 %collective-permute-start.5 = (f32[4,8,128]{2,1,0:T(8,128)S(1)}, f32[4,8,128]{2,1,0:T(8,128)S(1)}, u32[]{:S(2)}, u32[]{:S(2)}) collective-permute-start(f32[4,8,128]{2,1,0:T(8,128)S(1)} %get-tuple-element.14.strip_ref), channel_id=1, source_target_pairs={{64,0},{128,64},{192,128},{256,192},{320,256},{384,320},{448,384},... | collective-permute-start | bytes 49160 | tf_op jit(solution)/shard_map/ppermute | solution.py:375
  45.9 10.5 %collective-permute-start.4 = (f32[4,8,128]{2,1,0:T(8,128)S(1)}, f32[4,8,128]{2,1,0:T(8,128)S(1)}, u32[]{:S(2)}, u32[]{:S(2)}) collective-permute-start(f32[4,8,128]{2,1,0:T(8,128)S(1)} %get-tuple-element.14.strip_ref), channel_id=1, source_target_pairs={{0,64},{64,128},{128,192},{192,256},{256,320},{320,384},{384,448},... | collective-permute-start | bytes 49160 | tf_op jit(solution)/shard_map/ppermute | solution.py:375
  56.4 12.1 %collective-permute-start.6 = (f32[96,8,128]{2,1,0:T(8,128)S(1)}, f32[96,8,128]{2,1,0:T(8,128)S(1)}, u32[]{:S(2)}, u32[]{:S(2)}) collective-permute-start(f32[96,8,128]{2,1,0:T(8,128)S(1)} %get-tuple-element.17), channel_id=1, source_target_pairs={{0,8},{8,16},{16,24},{24,32},{32,40},{40,48},{48,56},{1,9},{9,17},... | collective-permute-start | bytes 1179656 | tf_op jit(solution)/shard_map/ppermute | solution.py:432
  60.9 12.8 %collective-permute-start.7 = (f32[96,8,128]{2,1,0:T(8,128)S(1)}, f32[96,8,128]{2,1,0:T(8,128)S(1)}, u32[]{:S(2)}, u32[]{:S(2)}) collective-permute-start(f32[96,8,128]{2,1,0:T(8,128)S(1)} %get-tuple-element.18), channel_id=1, source_target_pairs={{8,0},{16,8},{24,16},{32,24},{40,32},{48,40},{56,48},{9,1},{17,9},... | collective-permute-start | bytes 1179656 | tf_op jit(solution)/shard_map/ppermute | solution.py:433

commit v3 on v2

v3 whole, which is shorter than its diff:
```python
import jax
import jax.numpy as jnp
from jax import lax
from jax.experimental import pallas as pl
from jax.experimental.pallas import tpu as pltpu
from jax.sharding import PartitionSpec as P

STEPS = 4
DEEP = 4
KEEP_FLOW = 1.0 - 1.0 / 0.8
KEEP_SPECIES = 1.0 - 1.0 / 0.7
REACT_RATE = 0.5
GRAVITY = 0.001
MOVING = [
    (1, 0, 0),
    (-1, 0, 0),
    (0, 1, 0),
    (0, -1, 0),
    (0, 0, 1),
    (0, 0, -1),
    (1, 1, 0),
    (-1, -1, 0),
    (1, -1, 0),
    (-1, 1, 0),
    (1, 0, 1),
    (-1, 0, -1),
    (1, 0, -1),
    (-1, 0, 1),
    (0, 1, 1),
    (0, -1, -1),
    (0, 1, -1),
    (0, -1, 1),
]
NFLOW = 18
NSPEC = 6
SPECIES_WEIGHT = 0.125
FIELDS = 15
FLUID = 14
NEAR = 3 * FIELDS
HALF = 45 + 7
FAR_ROWS = 5 * FIELDS
ROW_TILES = FAR_ROWS + 7
ROWS = 8
LANES = 128
SOLID = float("nan")
REACTIVE = float("inf")
LARGEST = 3.0e38


def opposite(index):
    return index ^ 1


def flow_populations(m):
    third = m[0] * (1.0 / 3.0)
    axx, ayy, azz = m[4] - third, m[5] - third, m[6] - third
    base = m[0] - 1.5 * (axx + ayy + azz)
    sides = (4.5 * axx, 4.5 * ayy, 4.5 * azz)
    drift = [m[1 + k] * (1.0 / 12.0) for k in range(3)]
    moving = []
    lifted = [base + side for side in sides]
    for k in range(3):
        even, odd = lifted[k] * (1.0 / 18.0), m[1 + k] * (1.0 / 6.0)
        moving += [even + odd, even - odd]
    for a, b, cross in ((0, 1, 7), (0, 2, 8), (1, 2, 9)):
        both = (lifted[a] + sides[b]) * (1.0 / 36.0)
        mixed = m[cross] * 0.25
        same, differ = both + mixed, both - mixed
        plus, minus = drift[a] + drift[b], drift[a] - drift[b]
        moving += [same + plus, same - plus, differ + minus, differ - minus]
    return base * (1.0 / 3.0), moving


def species_populations(s):
    part = s[0] * SPECIES_WEIGHT
    moving = []
    for k in range(3):
        odd = s[1 + k] * 0.5
        moving += [part + odd, part - odd]
    return s[0] * 0.25, moving


def collide(flow, species):
    rho = flow[0]
    j = flow[1:4]
    third = rho * (1.0 / 3.0)
    equil = [third + j[0] * j[0], third + j[1] * j[1], third + j[2] * j[2], j[0] * j[1], j[0] * j[2], j[1] * j[2]]
    stress = [KEEP_FLOW * flow[4 + k] + (1.0 - KEEP_FLOW) * equil[k] for k in range(6)]
    conc = species[0]
    flux = [KEEP_SPECIES * species[1 + k] + (1.0 - KEEP_SPECIES) * (conc * j[k]) for k in range(3)]
    return [rho] + list(j) + stress + [conc] + flux


def is_number(value):
    return value < LARGEST


def pass_on(post, arriving, arriving_species):
    rest, own = flow_populations(post[:10])
    f = []
    for c in range(NFLOW):
        value = arriving[c]
        f.append(jnp.where(is_number(value), value, own[opposite(c)]))
    total = [f[2 * k] + f[2 * k + 1] for k in range(9)]
    diff = [f[2 * k] - f[2 * k + 1] for k in range(9)]
    xy, xz, yz = total[3] + total[4], total[5] + total[6], total[7] + total[8]
    rho = rest + (total[0] + total[1] + total[2]) + (xy + xz + yz)
    jx = diff[0] + (diff[3] + diff[4]) + (diff[5] + diff[6]) + GRAVITY
    jy = diff[1] + (diff[3] - diff[4]) + (diff[7] + diff[8])
    jz = diff[2] + (diff[5] - diff[6]) + (diff[7] - diff[8])
    flow = [
        rho,
        jx,
        jy,
        jz,
        total[0] + xy + xz,
        total[1] + xy + yz,
        total[2] + xz + yz,
        total[3] - total[4],
        total[5] - total[6],
        total[7] - total[8],
    ]
    rest, own = species_populations(post[10:14])
    g = []
    for c in range(NSPEC):
        value = arriving_species[c]
        back = own[opposite(c)]
        slow = jnp.where(value > LARGEST, REACT_RATE, 0.0)
        g.append(jnp.where(is_number(value), value, back + slow * (SPECIES_WEIGHT - back)))
    conc = rest + (g[0] + g[1]) + (g[2] + g[3]) + (g[4] + g[5])
    return flow, [conc, g[0] - g[1], g[2] - g[3], g[4] - g[5]]


def next_post(post, flow, species):
    fluid = is_number(post[0])
    new = collide(flow, species)
    new[0] = jnp.where(fluid, new[0], post[0])
    new[10] = jnp.where(fluid, new[10], post[10])
    for k in range(11, 14):
        new[k] = jnp.where(fluid, new[k], 0.0)
    return new


def lanes_of(shape):
    return lax.broadcasted_iota(jnp.int32, shape, len(shape) - 1)


def rows_of(shape):
    return lax.broadcasted_iota(jnp.int32, shape, len(shape) - 2)


def roll(value, shift, axis):
    size = value.shape[axis]
    if isinstance(shift, int):
        shift = shift % size
        if shift == 0:
            return value
    return pltpu.roll(value, shift, axis)


def first_slot():
    return 4 * lax.rem(lax.axis_index("gx"), 4)


def towards(sign):
    return [c for c in range(NFLOW) if MOVING[c][0] == sign]


def start_kernel(flow_in, species_in, fluid_in, react_in, block_ref, right_ref, left_ref, flow_ref, species_ref, fluid_ref, react_ref, done):
    pairs = ((flow_in, flow_ref), (species_in, species_ref), (fluid_in, fluid_ref), (react_in, react_ref))
    copies = [pltpu.make_async_copy(one, two, done.at[k]) for k, (one, two) in enumerate(pairs)]
    for copy in copies:
        copy.start()
    for copy in copies:
        copy.wait()
    for x in range(DEEP):
        slot = first_slot() + x
        fluid = fluid_ref[x].astype(jnp.float32)
        react = react_ref[x].astype(jnp.float32)
        flow = [flow_ref[k, x] * fluid for k in range(10)]
        species = [species_ref[k, x] * fluid for k in range(4)]
        post = collide(flow, species)
        for far, sign, ref in ((0, 1, right_ref), (3, -1, left_ref)):
            if x == far:
                _, flow_pops = flow_populations(post[:10])
                _, species_pops = species_populations(post[10:])
                parts = [flow_pops[c] for c in towards(sign)] + [species_pops[towards(sign)[0]], fluid]
                parts[0] = jnp.where(fluid > 0.5, parts[0], react)
                for k, value in enumerate(parts):
                    ref[NEAR + k] = roll(value, 8 * slot + 4, 1)
        post[0] = jnp.where(fluid > 0.5, post[0], react)
        for k, value in enumerate(post + [fluid]):
            value = roll(value, 8 * slot + 4, 1)
            block_ref[k, x] = value
            if x > 0:
                right_ref[3 * k + x - 1] = value
            if x < 3:
                left_ref[3 * k + x] = value


def bring_kernel(block_in, block_ref, done):
    copy = pltpu.make_async_copy(block_in, block_ref, done)
    copy.start()
    copy.wait()


def put_rows(up_ref, down_ref, place, one, two):
    high = rows_of((ROWS, LANES)) >= 4
    two = roll(two, 4, 0)
    up_ref[place] = jnp.where(high, one, two)
    down_ref[place] = jnp.where(high, two, one)


def layer_of(field, x, own_ref, left_ref, right_ref):
    if x < 4:
        return left_ref[3 * field + x - 1]
    if x < 8:
        return own_ref[field, x - 4]
    return right_ref[3 * field + x - 8]


def rows_kernel(own_ref, left_ref, right_ref, up_ref, down_ref):
    refs = (own_ref, left_ref, right_ref)
    for field in range(FIELDS):
        for k in range(5):
            put_rows(up_ref, down_ref, 5 * field + k, layer_of(field, k + 1, *refs), layer_of(field, k + 6, *refs))
    for k in range(7):
        put_rows(up_ref, down_ref, FAR_ROWS + k, left_ref[NEAR + k], right_ref[NEAR + k])


def slot_at(x):
    return lax.rem(first_slot() + x + 12, 16)


TALL = (2 * ROWS, LANES)


def halves(up_ref, down_ref, place):
    low = rows_of((ROWS, LANES)) < 4
    up, down = up_ref[place], down_ref[place]
    return jnp.where(low, down, up), roll(jnp.where(low, up, down), 4, 0)


def edges_kernel(own_ref, left_ref, right_ref, up_ref, down_ref, edge_ref):
    refs = (own_ref, left_ref, right_ref)
    slot_of = lanes_of((ROWS, LANES)) // 8
    here = [slot_of == slot_at(x) for x in range(12)]
    for field in range(FIELDS):
        near = jnp.zeros((ROWS, LANES), jnp.float32)
        beyond = near
        for k in range(5):
            one, two = halves(up_ref, down_ref, 5 * field + k)
            for x, value in ((k + 1, one), (k + 6, two)):
                near = jnp.where(here[x], layer_of(field, x, *refs), near)
                beyond = jnp.where(here[x], value, beyond)
        if field < 7:
            one, two = halves(up_ref, down_ref, FAR_ROWS + field)
            for x, value, ref in ((0, one, left_ref), (11, two, right_ref)):
                near = jnp.where(here[x], ref[NEAR + field], near)
                beyond = jnp.where(here[x], value, beyond)
        edge_ref[field, 0:ROWS] = near
        edge_ref[field, ROWS : 2 * ROWS] = beyond


def marked(first, conc, fluid):
    solid = fluid < 0.5
    mark = jnp.where(first > 0.5, REACTIVE, SOLID)
    return jnp.where(solid, SOLID, first), jnp.where(solid, mark, conc)


def marked_far(parts):
    solid = parts[6] < 0.5
    mark = jnp.where(parts[0] > 0.5, REACTIVE, SOLID)
    return [jnp.where(solid, SOLID, part) for part in parts[:5]] + [jnp.where(solid, mark, parts[5])]


def moved(value, c):
    cx, cy, cz = MOVING[c]
    return roll(roll(value, 8 * cx + cz, 1), cy, 0)


def send(state_ref, sent_ref, x):
    _, flow_pops = flow_populations([state_ref[k, x] for k in range(10)])
    _, species_pops = species_populations([state_ref[k, x] for k in range(10, 14)])
    for c in range(NFLOW):
        sent_ref[c, x] = moved(flow_pops[c], c)
    for c in range(NSPEC):
        sent_ref[NFLOW + c, x] = moved(species_pops[c], c)


def first_sends_kernel(own_ref, left_ref, right_ref, up_ref, down_ref, state_ref, sent_ref):
    refs = (own_ref, left_ref, right_ref)
    for field in (FLUID,) + tuple(range(FLUID)):
        for k in range(5):
            one, two = halves(up_ref, down_ref, 5 * field + k)
            for x, value in ((k + 1, one), (k + 6, two)):
                state_ref[field, x, 0:ROWS] = layer_of(field, x, *refs)
                state_ref[field, x, ROWS : 2 * ROWS] = value
    for x in range(1, 11):
        rho, conc = marked(state_ref[0, x], state_ref[10, x], state_ref[FLUID, x])
        state_ref[0, x] = rho
        state_ref[10, x] = conc
        send(state_ref, sent_ref, x)
    beyond = [halves(up_ref, down_ref, FAR_ROWS + k) for k in range(7)]
    for end, (x, sign, ref) in enumerate(((0, 1, left_ref), (11, -1, right_ref))):
        parts = [jnp.concatenate([ref[NEAR + k], beyond[k][end]]) for k in range(7)]
        parts = marked_far(parts)
        along = towards(sign)
        for k, c in enumerate(along):
            sent_ref[c, x] = moved(parts[k], c)
        sent_ref[NFLOW + along[0], x] = moved(parts[5], along[0])


def steps_kernel(
    first_state,
    first_sent,
    edge_ref,
    below_ref,
    above_ref,
    flow_out,
    species_out,
    dissolved_out,
    state,
    sent,
    strips,
    strip_sent,
):
    lane = lanes_of(TALL)
    inner = lane % 8 < 4

    far_strips = []
    for side in range(2):
        for field in range(FIELDS):
            near, beyond = edge_ref[field], (below_ref, above_ref)[side][field]
            strips[side, field] = jnp.where(inner, near, beyond) if side else jnp.where(inner, beyond, near)
        far_strips.append(marked_far([strips[side, k] for k in range(7)]))
        rho, conc = marked(strips[side, 0], strips[side, 10], strips[side, FLUID])
        strips[side, 0] = rho
        strips[side, 10] = conc

    def turned_back(value, x):
        return roll(value, 124 - 8 * slot_at(x), 1)

    released = [jnp.zeros((ROWS, LANES), jnp.float32)] * DEEP
    for step in range(STEPS):
        last = step == STEPS - 1
        state_now, sent_now = (first_state, first_sent) if step == 0 else (state, sent)
        for side in range(2):
            post = [strips[side, k] for k in range(14)]
            _, flow_pops = flow_populations(post[:10])
            _, species_pops = species_populations(post[10:])
            if step == 0:
                for x, sign in ((0, 1), (11, -1)):
                    here = lane // 8 == slot_at(x)
                    for k, c in enumerate(towards(sign)):
                        flow_pops[c] = jnp.where(here, far_strips[side][k], flow_pops[c])
                    c = towards(sign)[0]
                    species_pops[c] = jnp.where(here, far_strips[side][5], species_pops[c])
            wanted = [c for c in range(NFLOW) if not last or MOVING[c][2] == (1, -1)[side]]
            arriving = {c: moved(flow_pops[c], c) for c in wanted}
            arriving_species = {c: moved(species_pops[c], c) for c in wanted if c < NSPEC}
            for c in wanted:
                if MOVING[c][2] == (1, -1)[side]:
                    strip_sent[c] = arriving[c]
                    if c < NSPEC:
                        strip_sent[NFLOW + c] = arriving_species[c]
            if not last:
                new_flow, new_species = pass_on(post, arriving, arriving_species)
                for k, value in enumerate(next_post(post, new_flow, new_species)):
                    strips[side, k] = value
        if step > 0:
            for x in range(step, 12 - step):
                send(state, sent, x)
        height = ROWS if last else 2 * ROWS
        for x in range(step + 1, 11 - step):
            first = lane[0:height] == 8 * slot_at(x) + 4
            end = lane[0:height] == 8 * slot_at(x) + 3

            def arrives(place, c):
                cx, _, cz = MOVING[c]
                value = sent_now[place, x - cx, 0:height]
                if cz:
                    value = jnp.where(first if cz > 0 else end, strip_sent[place, 0:height], value)
                return value

            post = [state_now[k, x, 0:height] for k in range(14)]
            arriving = [arrives(c, c) for c in range(NFLOW)]
            arriving_species = [arrives(NFLOW + c, c) for c in range(NSPEC)]
            new_flow, new_species = pass_on(post, arriving, arriving_species)
            if 0 <= x - DEEP < DEEP:
                parts = [value[0:ROWS] for value in arriving_species]
                parts = [jnp.where(is_number(part), SPECIES_WEIGHT - part, 0.0) for part in parts]
                parts = (parts[0] + parts[1]) + (parts[2] + parts[3]) + (parts[4] + parts[5])
                released[x - DEEP] = released[x - DEEP] + parts
            if last:
                fluid = is_number(post[0])
                for k in range(10):
                    flow_out[k, x - DEEP] = turned_back(jnp.where(fluid, new_flow[k], 0.0), x)
                for k in range(4):
                    species_out[k, x - DEEP] = turned_back(jnp.where(fluid, new_species[k], 0.0), x)
                gone = jnp.where(post[10] > LARGEST, REACT_RATE * released[x - DEEP], 0.0)
                dissolved_out[x - DEEP] = turned_back(gone, x)
            else:
                for k, value in enumerate(next_post(post, new_flow, new_species)):
                    state[k, x] = value


def shifted(upward, downward, axis, wrap):
    count = lax.axis_size(axis)
    up = [(i, (i + 1) % count) for i in range(count if wrap else count - 1)]
    down = [(j, i) for i, j in up]
    return lax.ppermute(upward, axis, up), lax.ppermute(downward, axis, down)


def vmem(count):
    return [pl.BlockSpec(memory_space=pltpu.VMEM)] * count


def per_device(flow_moments, species_moments, fluid_mask, reactive_mask):
    f32 = jnp.float32
    small = pltpu.CompilerParams(vmem_limit_bytes=16 * 1024 * 1024)
    half = jax.ShapeDtypeStruct((HALF, ROWS, LANES), f32)
    block, to_right, to_left = pl.pallas_call(
        start_kernel,
        out_shape=(jax.ShapeDtypeStruct((FIELDS, DEEP, ROWS, LANES), f32), half, half),
        in_specs=[pl.BlockSpec(memory_space=pltpu.HBM)] * 4,
        out_specs=tuple(vmem(3)),
        scratch_shapes=[
            pltpu.VMEM(flow_moments.shape, f32),
            pltpu.VMEM(species_moments.shape, f32),
            pltpu.VMEM(fluid_mask.shape, fluid_mask.dtype),
            pltpu.VMEM(reactive_mask.shape, reactive_mask.dtype),
            pltpu.SemaphoreType.DMA((4,)),
        ],
        compiler_params=pltpu.CompilerParams(vmem_limit_bytes=56 * 1024 * 1024),
    )(flow_moments, species_moments, fluid_mask, reactive_mask)
    left, right = shifted(to_right, to_left, "gx", True)
    block = pl.pallas_call(
        bring_kernel,
        out_shape=jax.ShapeDtypeStruct(block.shape, f32),
        in_specs=[pl.BlockSpec(memory_space=pltpu.HBM)],
        out_specs=vmem(1)[0],
        scratch_shapes=[pltpu.SemaphoreType.DMA],
        compiler_params=small,
        cost_estimate=pl.CostEstimate(flops=10**7, bytes_accessed=10**7, transcendentals=0),
    )(block)
    tiles = jax.ShapeDtypeStruct((ROW_TILES, ROWS, LANES), f32)
    to_up, to_down = pl.pallas_call(
        rows_kernel,
        out_shape=(tiles, tiles),
        in_specs=vmem(3),
        out_specs=tuple(vmem(2)),
        compiler_params=small,
    )(block, left, right)
    from_low, from_high = shifted(to_up, to_down, "gy", False)
    strips = jax.ShapeDtypeStruct((FIELDS,) + TALL, f32)
    edge = pl.pallas_call(
        edges_kernel,
        out_shape=strips,
        in_specs=vmem(5),
        out_specs=vmem(1)[0],
        compiler_params=small,
    )(block, left, right, from_low, from_high)
    below, above = shifted(edge, edge, "gz", False)
    state, sent = pl.pallas_call(
        first_sends_kernel,
        out_shape=(
            jax.ShapeDtypeStruct((FIELDS, 12) + TALL, f32),
            jax.ShapeDtypeStruct((NFLOW + NSPEC, 12) + TALL, f32),
        ),
        in_specs=vmem(5),
        out_specs=tuple(vmem(2)),
        compiler_params=small,
        cost_estimate=pl.CostEstimate(flops=10**7, bytes_accessed=10**7, transcendentals=0),
    )(block, left, right, from_low, from_high)
    return pl.pallas_call(
        steps_kernel,
        out_shape=(
            jax.ShapeDtypeStruct(flow_moments.shape, f32),
            jax.ShapeDtypeStruct(species_moments.shape, f32),
            jax.ShapeDtypeStruct(fluid_mask.shape, f32),
        ),
        in_specs=vmem(5),
        out_specs=tuple(vmem(3)),
        scratch_shapes=[
            pltpu.VMEM((FIELDS, 12) + TALL, f32),
            pltpu.VMEM((NFLOW + NSPEC, 12) + TALL, f32),
            pltpu.VMEM((2, FIELDS) + TALL, f32),
            pltpu.VMEM((NFLOW + NSPEC,) + TALL, f32),
        ],
        compiler_params=small,
    )(state, sent, edge, below, above)


def solution(mesh):
    return jax.shard_map(
        per_device,
        mesh=mesh,
        in_specs=(
            P(None, "gx", "gy", "gz"),
            P(None, "gx", "gy", "gz"),
            P("gx", "gy", "gz"),
            P("gx", "gy", "gz"),
        ),
        out_specs=(P(None, "gx", "gy", "gz"), P(None, "gx", "gy", "gz"), P("gx", "gy", "gz")),
        check_vma=False,
    )
```

time: 77.9 us -> 68.1 us (0.87)
  starting transfers between devices: 39.2 us -> 31.6 us
  waiting for transfers between devices: 30.8 us -> 28.1 us
    ppermute x8 -> x6, starting transfers between devices: 39.2 us -> 31.6 us  [shifted(): return (lax.ppermute(upward, axis, up), lax.ppermute(downward, axis, down))]
    ppermute x8 -> x6, waiting for transfers between devices: 30.8 us -> 28.1 us  [shifted(): return (lax.ppermute(upward, axis, up), lax.ppermute(downward, axis, down))]
  transfers between devices with their start and end apart: 8 -> 6, of which waited for: 4 -> 5; matrix products, arithmetic and copies ran while one was open for 0% -> 0% of each run, Pallas kernels for 0% -> 1%
where the time goes in v3:
time: 68.1 us; the launch traced here: 67.8 us
  starting transfers between devices  31.6 us (46%)
  waiting for transfers between devices  28.1 us (41%)
  Pallas kernels  6.39 us (9%)
  local copies, waits for them, and re-layouts  0.94 us (1%)
  between operations  0.72 us (1%)
    ppermute x6, starting transfers between devices, shifted(): return (lax.ppermute(upward, axis, up), lax.ppermute(downward, axis, down))  31.6 us
    ppermute x6, waiting for transfers between devices, shifted(): return (lax.ppermute(upward, axis, up), lax.ppermute(downward, axis, down))  28.1 us
    pallas_call x1, Pallas kernels, per_device(): pl.pallas_call(steps_kernel, out_shape=(jax.ShapeDtypeStruct(flow_moments...  3.45 us
    pallas_call x1, Pallas kernels, per_device(): pl.pallas_call(start_kernel, out_shape=(jax.ShapeDtypeStruct((FIELDS, DEE...  1.95 us
  transfers between devices with their start and end apart: 6, of which 5 were waited for; matrix products, arithmetic and copies ran while one was open for 0% of the time, Pallas kernels for 1%

profile of v3, /device:TPU:305, one launch (start us, length us, event | category | flops | bytes accessed | tf_op | source)
XLA Modules:
  0.0 67.8 jit_solution(7716530138077505380)
XLA Ops:
  0.6 1.9 %shard_map.67 = (f32[15,4,8,128]{3,2,1,0:T(8,128)}, f32[52,8,128]{2,1,0:T(8,128)}, f32[52,8,128]{2,1,0:T(8,128)}) custom-call(f32[10,4,8,128]{3,2,1,0:T(8,128)} %flow_in.1, f32[4,4,8,128]{3,2,1,0:T(8,128)} %species_in.1, s32[4,8,128]{2,1,0:T(8,128)} %fluid_in.1, s32[4,8,128]{2,1,0:T(8,128)} %react_in.1), custom_call_target="tpu_custom_call" | custom-call | tf_op jit(solution)/shard_map/pallas_call | solution.py:423
  2.6 12.5 %collective-permute-start = (f32[52,8,128]{2,1,0:T(8,128)}, f32[52,8,128]{2,1,0:T(8,128)S(1)}, u32[]{:S(2)}, u32[]{:S(2)}) collective-permute-start(f32[52,8,128]{2,1,0:T(8,128)} %get-tuple-element.11), channel_id=1, source_target_pairs={{0,64},{64,128},{128,192},{192,256},{256,320},{320,384},{384,448},... | collective-permute-start | bytes 638984 | tf_op jit(solution)/shard_map/ppermute | solution.py:412
  15.1 4.2 %collective-permute-start.1 = (f32[52,8,128]{2,1,0:T(8,128)}, f32[52,8,128]{2,1,0:T(8,128)S(1)}, u32[]{:S(2)}, u32[]{:S(2)}) collective-permute-start(f32[52,8,128]{2,1,0:T(8,128)} %get-tuple-element.12), channel_id=1, source_target_pairs={{64,0},{128,64},{192,128},{256,192},{320,256},{384,320},{448,384},... | collective-permute-start | bytes 638984 | tf_op jit(solution)/shard_map/ppermute | solution.py:412
  19.3 0.0 copy-start
  19.3 0.9 %copy-done = f32[15,4,8,128]{3,2,1,0:T(8,128)S(1)} copy-done((f32[15,4,8,128]{3,2,1,0:T(8,128)S(1)}, f32[15,4,8,128]{3,2,1,0:T(8,128)}, u32[]{:S(2)}) %copy-start) | copy-done | bytes 245784
  20.3 0.3 shard_map.68.own_ref
  20.6 11.6 %collective-permute-done.left_ref = f32[52,8,128]{2,1,0:T(8,128)S(1)} collective-permute-done((f32[52,8,128]{2,1,0:T(8,128)}, f32[52,8,128]{2,1,0:T(8,128)S(1)}, u32[]{:S(2)}, u32[]{:S(2)}) %collective-permute-start) | collective-permute-done | bytes 213024 | tf_op jit(solution)/shard_map/ppermute | solution.py:412
  32.2 2.9 %collective-permute-done.1.right_ref = f32[52,8,128]{2,1,0:T(8,128)S(1)} collective-permute-done((f32[52,8,128]{2,1,0:T(8,128)}, f32[52,8,128]{2,1,0:T(8,128)S(1)}, u32[]{:S(2)}, u32[]{:S(2)}) %collective-permute-start.1) | collective-permute-done | bytes 213024 | tf_op jit(solution)/shard_map/ppermute | solution.py:412
  35.2 4.5 %collective-permute-start.2 = (f32[82,8,128]{2,1,0:T(8,128)S(1)}, f32[82,8,128]{2,1,0:T(8,128)S(1)}, u32[]{:S(2)}, u32[]{:S(2)}) collective-permute-start(f32[82,8,128]{2,1,0:T(8,128)S(1)} %get-tuple-element.13), channel_id=1, source_target_pairs={{0,8},{8,16},{16,24},{24,32},{32,40},{40,48},{48,56},{1,9},{9,17},... | collective-permute-start | bytes 1007624 | tf_op jit(solution)/shard_map/ppermute | solution.py:412
  39.7 1.9 %collective-permute-start.3 = (f32[82,8,128]{2,1,0:T(8,128)S(1)}, f32[82,8,128]{2,1,0:T(8,128)S(1)}, u32[]{:S(2)}, u32[]{:S(2)}) collective-permute-start(f32[82,8,128]{2,1,0:T(8,128)S(1)} %get-tuple-element.14), channel_id=1, source_target_pairs={{8,0},{16,8},{24,16},{32,24},{40,32},{48,40},{56,48},{9,1},{17,9},... | collective-permute-start | bytes 1007624 | tf_op jit(solution)/shard_map/ppermute | solution.py:412
  41.7 4.8 %collective-permute-done.2.up_ref = f32[82,8,128]{2,1,0:T(8,128)S(1)} collective-permute-done((f32[82,8,128]{2,1,0:T(8,128)S(1)}, f32[82,8,128]{2,1,0:T(8,128)S(1)}, u32[]{:S(2)}, u32[]{:S(2)}) %collective-permute-start.2) | collective-permute-done | bytes 335904 | tf_op jit(solution)/shard_map/ppermute | solution.py:412
  46.5 5.0 %collective-permute-done.3.down_ref = f32[82,8,128]{2,1,0:T(8,128)S(1)} collective-permute-done((f32[82,8,128]{2,1,0:T(8,128)S(1)}, f32[82,8,128]{2,1,0:T(8,128)S(1)}, u32[]{:S(2)}, u32[]{:S(2)}) %collective-permute-start.3) | collective-permute-done | bytes 335904 | tf_op jit(solution)/shard_map/ppermute | solution.py:412
  51.5 0.1 shard_map.71.edge_ref
  51.6 6.5 %collective-permute-start.4 = (f32[15,16,128]{2,1,0:T(8,128)S(1)}, f32[15,16,128]{2,1,0:T(8,128)S(1)}, u32[]{:S(2)}, u32[]{:S(2)}) collective-permute-start(f32[15,16,128]{2,1,0:T(8,128)S(1)} %shard_map.71.edge_ref), channel_id=1, source_target_pairs={{0,1},{1,2},{2,3},{3,4},{4,5},{5,6},{6,7},{8,9},{9,10},{10,11},{11... | collective-permute-start | bytes 368648 | tf_op jit(solution)/shard_map/ppermute | solution.py:412
  58.1 1.9 %collective-permute-start.5 = (f32[15,16,128]{2,1,0:T(8,128)S(1)}, f32[15,16,128]{2,1,0:T(8,128)S(1)}, u32[]{:S(2)}, u32[]{:S(2)}) collective-permute-start(f32[15,16,128]{2,1,0:T(8,128)S(1)} %shard_map.71.edge_ref), channel_id=1, source_target_pairs={{1,0},{2,1},{3,2},{4,3},{5,4},{6,5},{7,6},{9,8},{10,9},{11,10},{12... | collective-permute-start | bytes 368648 | tf_op jit(solution)/shard_map/ppermute | solution.py:412
  60.0 0.6 shard_map.70
  60.6 0.0 collective-permute-done.4.below_ref
  60.6 3.7 %collective-permute-done.5.above_ref = f32[15,16,128]{2,1,0:T(8,128)S(1)} collective-permute-done((f32[15,16,128]{2,1,0:T(8,128)S(1)}, f32[15,16,128]{2,1,0:T(8,128)S(1)}, u32[]{:S(2)}, u32[]{:S(2)}) %collective-permute-start.5) | collective-permute-done | bytes 122912 | tf_op jit(solution)/shard_map/ppermute | solution.py:412
  64.3 3.4 %shard_map.72 = (f32[10,4,8,128]{3,2,1,0:T(8,128)}, f32[4,4,8,128]{3,2,1,0:T(8,128)}, f32[4,8,128]{2,1,0:T(8,128)}) custom-call(f32[15,12,16,128]{3,2,1,0:T(8,128)S(1)} %get-tuple-element.15.first_state, f32[24,12,16,128]{3,2,1,0:T(8,128)S(1)} %get-tuple-element.16.first_sent, f32[15,16,128]{2,1,0:T(8,128)S(1)} %shard_map.71.edge_ref, ...), custom_call_target="tpu_custom_call" | custom-call | tf_op jit(solution)/shard_map/pallas_call | solution.py:476
  (1 shorter events, 0.0 us)
Async XLA Ops:
  2.6 29.6 %collective-permute-start = (f32[52,8,128]{2,1,0:T(8,128)}, f32[52,8,128]{2,1,0:T(8,128)S(1)}, u32[]{:S(2)}, u32[]{:S(2)}) collective-permute-start(f32[52,8,128]{2,1,0:T(8,128)} %get-tuple-element.11), channel_id=1, source_target_pairs={{0,64},{64,128},{128,192},{192,256},{256,320},{320,384},{384,448},... | collective-permute-start | bytes 638984 | tf_op jit(solution)/shard_map/ppermute | solution.py:412
  15.1 20.1 %collective-permute-start.1 = (f32[52,8,128]{2,1,0:T(8,128)}, f32[52,8,128]{2,1,0:T(8,128)S(1)}, u32[]{:S(2)}, u32[]{:S(2)}) collective-permute-start(f32[52,8,128]{2,1,0:T(8,128)} %get-tuple-element.12), channel_id=1, source_target_pairs={{64,0},{128,64},{192,128},{256,192},{320,256},{384,320},{448,384},... | collective-permute-start | bytes 638984 | tf_op jit(solution)/shard_map/ppermute | solution.py:412
  19.3 0.9 %copy-start = (f32[15,4,8,128]{3,2,1,0:T(8,128)S(1)}, f32[15,4,8,128]{3,2,1,0:T(8,128)}, u32[]{:S(2)}) copy-start(f32[15,4,8,128]{3,2,1,0:T(8,128)} %get-tuple-element.10.block_in) | copy-start | bytes 737284
  35.2 11.3 %collective-permute-start.2 = (f32[82,8,128]{2,1,0:T(8,128)S(1)}, f32[82,8,128]{2,1,0:T(8,128)S(1)}, u32[]{:S(2)}, u32[]{:S(2)}) collective-permute-start(f32[82,8,128]{2,1,0:T(8,128)S(1)} %get-tuple-element.13), channel_id=1, source_target_pairs={{0,8},{8,16},{16,24},{24,32},{32,40},{40,48},{48,56},{1,9},{9,17},... | collective-permute-start | bytes 1007624 | tf_op jit(solution)/shard_map/ppermute | solution.py:412
  39.7 11.7 %collective-permute-start.3 = (f32[82,8,128]{2,1,0:T(8,128)S(1)}, f32[82,8,128]{2,1,0:T(8,128)S(1)}, u32[]{:S(2)}, u32[]{:S(2)}) collective-permute-start(f32[82,8,128]{2,1,0:T(8,128)S(1)} %get-tuple-element.14), channel_id=1, source_target_pairs={{8,0},{16,8},{24,16},{32,24},{40,32},{48,40},{56,48},{9,1},{17,9},... | collective-permute-start | bytes 1007624 | tf_op jit(solution)/shard_map/ppermute | solution.py:412
  51.6 9.0 %collective-permute-start.4 = (f32[15,16,128]{2,1,0:T(8,128)S(1)}, f32[15,16,128]{2,1,0:T(8,128)S(1)}, u32[]{:S(2)}, u32[]{:S(2)}) collective-permute-start(f32[15,16,128]{2,1,0:T(8,128)S(1)} %shard_map.71.edge_ref), channel_id=1, source_target_pairs={{0,1},{1,2},{2,3},{3,4},{4,5},{5,6},{6,7},{8,9},{9,10},{10,11},{11... | collective-permute-start | bytes 368648 | tf_op jit(solution)/shard_map/ppermute | solution.py:412
  58.1 6.2 %collective-permute-start.5 = (f32[15,16,128]{2,1,0:T(8,128)S(1)}, f32[15,16,128]{2,1,0:T(8,128)S(1)}, u32[]{:S(2)}, u32[]{:S(2)}) collective-permute-start(f32[15,16,128]{2,1,0:T(8,128)S(1)} %shard_map.71.edge_ref), channel_id=1, source_target_pairs={{1,0},{2,1},{3,2},{4,3},{5,4},{6,5},{7,6},{9,8},{10,9},{11,10},{12... | collective-permute-start | bytes 368648 | tf_op jit(solution)/shard_map/ppermute | solution.py:412

commit v4 on v3

--- a/solution.py
+++ b/solution.py
@@ -38,8 +38,8 @@
 FLUID = 14
 NEAR = 3 * FIELDS
 HALF = 45 + 7
-FAR_ROWS = 5 * FIELDS
-ROW_TILES = FAR_ROWS + 7
+OWN_TILES = 2 * FIELDS
+FAR_ROWS = 3 * FIELDS
 ROWS = 8
 LANES = 128
 SOLID = float("nan")
@@ -198,12 +198,6 @@
                 left_ref[3 * k + x] = value
 
 
-def bring_kernel(block_in, block_ref, done):
-    copy = pltpu.make_async_copy(block_in, block_ref, done)
-    copy.start()
-    copy.wait()
-
-
 def put_rows(up_ref, down_ref, place, one, two):
     high = rows_of((ROWS, LANES)) >= 4
     two = roll(two, 4, 0)
@@ -219,13 +213,18 @@
     return right_ref[3 * field + x - 8]
 
 
-def rows_kernel(own_ref, left_ref, right_ref, up_ref, down_ref):
-    refs = (own_ref, left_ref, right_ref)
+def own_rows_kernel(block_in, block_ref, up_ref, down_ref, done):
+    copy = pltpu.make_async_copy(block_in, block_ref, done)
+    copy.start()
+    copy.wait()
     for field in range(FIELDS):
-        for k in range(5):
-            put_rows(up_ref, down_ref, 5 * field + k, layer_of(field, k + 1, *refs), layer_of(field, k + 6, *refs))
-    for k in range(7):
-        put_rows(up_ref, down_ref, FAR_ROWS + k, left_ref[NEAR + k], right_ref[NEAR + k])
+        for k in range(2):
+            put_rows(up_ref, down_ref, 2 * field + k, block_ref[field, k], block_ref[field, k + 2])
+
+
+def rows_kernel(left_ref, right_ref, own_up, own_down, up_ref, down_ref):
+    for k in range(HALF):
+        put_rows(up_ref, down_ref, k, left_ref[k], right_ref[k])
 
 
 def slot_at(x):
@@ -241,18 +240,33 @@
     return jnp.where(low, down, up), roll(jnp.where(low, up, down), 4, 0)
 
 
-def edges_kernel(own_ref, left_ref, right_ref, up_ref, down_ref, edge_ref):
+def layer_of(field, x, own_ref, left_ref, right_ref):
+    if x < 4:
+        return left_ref[3 * field + x - 1]
+    if x < 8:
+        return own_ref[field, x - 4]
+    return right_ref[3 * field + x - 8]
+
+
+def rows_beyond(field, own_up, own_down, up_ref, down_ref):
+    found = {}
+    for k in range(2):
+        found[4 + k], found[6 + k] = halves(own_up, own_down, 2 * field + k)
+    for k in range(3):
+        found[1 + k], found[8 + k] = halves(up_ref, down_ref, 3 * field + k)
+    return found
+
+
+def edges_kernel(own_ref, left_ref, right_ref, own_up, own_down, up_ref, down_ref, edge_ref):
     refs = (own_ref, left_ref, right_ref)
     slot_of = lanes_of((ROWS, LANES)) // 8
     here = [slot_of == slot_at(x) for x in range(12)]
     for field in range(FIELDS):
         near = jnp.zeros((ROWS, LANES), jnp.float32)
         beyond = near
-        for k in range(5):
-            one, two = halves(up_ref, down_ref, 5 * field + k)
-            for x, value in ((k + 1, one), (k + 6, two)):
-                near = jnp.where(here[x], layer_of(field, x, *refs), near)
-                beyond = jnp.where(here[x], value, beyond)
+        for x, value in rows_beyond(field, own_up, own_down, up_ref, down_ref).items():
+            near = jnp.where(here[x], layer_of(field, x, *refs), near)
+            beyond = jnp.where(here[x], value, beyond)
         if field < 7:
             one, two = halves(up_ref, down_ref, FAR_ROWS + field)
             for x, value, ref in ((0, one, left_ref), (11, two, right_ref)):
@@ -288,14 +302,12 @@
         sent_ref[NFLOW + c, x] = moved(species_pops[c], c)
 
 
-def first_sends_kernel(own_ref, left_ref, right_ref, up_ref, down_ref, state_ref, sent_ref):
+def first_sends_kernel(own_ref, left_ref, right_ref, own_up, own_down, up_ref, down_ref, state_ref, sent_ref):
     refs = (own_ref, left_ref, right_ref)
-    for field in (FLUID,) + tuple(range(FLUID)):
-        for k in range(5):
-            one, two = halves(up_ref, down_ref, 5 * field + k)
-            for x, value in ((k + 1, one), (k + 6, two)):
-                state_ref[field, x, 0:ROWS] = layer_of(field, x, *refs)
-                state_ref[field, x, ROWS : 2 * ROWS] = value
+    for field in range(FIELDS):
+        for x, value in rows_beyond(field, own_up, own_down, up_ref, down_ref).items():
+            state_ref[field, x, 0:ROWS] = layer_of(field, x, *refs)
+            state_ref[field, x, ROWS : 2 * ROWS] = value
     for x in range(1, 11):
         rho, conc = marked(state_ref[0, x], state_ref[10, x], state_ref[FLUID, x])
         state_ref[0, x] = rho
@@ -435,32 +447,34 @@
         compiler_params=pltpu.CompilerParams(vmem_limit_bytes=56 * 1024 * 1024),
     )(flow_moments, species_moments, fluid_mask, reactive_mask)
     left, right = shifted(to_right, to_left, "gx", True)
-    block = pl.pallas_call(
-        bring_kernel,
-        out_shape=jax.ShapeDtypeStruct(block.shape, f32),
+    own_tiles = jax.ShapeDtypeStruct((OWN_TILES, ROWS, LANES), f32)
+    block, own_to_up, own_to_down = pl.pallas_call(
+        own_rows_kernel,
+        out_shape=(jax.ShapeDtypeStruct(block.shape, f32), own_tiles, own_tiles),
         in_specs=[pl.BlockSpec(memory_space=pltpu.HBM)],
-        out_specs=vmem(1)[0],
+        out_specs=tuple(vmem(3)),
         scratch_shapes=[pltpu.SemaphoreType.DMA],
         compiler_params=small,
         cost_estimate=pl.CostEstimate(flops=10**7, bytes_accessed=10**7, transcendentals=0),
     )(block)
-    tiles = jax.ShapeDtypeStruct((ROW_TILES, ROWS, LANES), f32)
+    own_rows = shifted(own_to_up, own_to_down, "gy", False)
+    tiles = jax.ShapeDtypeStruct((HALF, ROWS, LANES), f32)
     to_up, to_down = pl.pallas_call(
         rows_kernel,
         out_shape=(tiles, tiles),
-        in_specs=vmem(3),
+        in_specs=vmem(2) + [pl.BlockSpec(memory_space=pl.ANY)] * 2,
         out_specs=tuple(vmem(2)),
         compiler_params=small,
-    )(block, left, right)
-    from_low, from_high = shifted(to_up, to_down, "gy", False)
+    )(left, right, *own_rows)
+    rows = own_rows + shifted(to_up, to_down, "gy", False)
     strips = jax.ShapeDtypeStruct((FIELDS,) + TALL, f32)
     edge = pl.pallas_call(
         edges_kernel,
         out_shape=strips,
-        in_specs=vmem(5),
+        in_specs=vmem(7),
         out_specs=vmem(1)[0],
         compiler_params=small,
-    )(block, left, right, from_low, from_high)
+    )(block, left, right, *rows)
     below, above = shifted(edge, edge, "gz", False)
     state, sent = pl.pallas_call(
         first_sends_kernel,
@@ -468,11 +482,11 @@
             jax.ShapeDtypeStruct((FIELDS, 12) + TALL, f32),
             jax.ShapeDtypeStruct((NFLOW + NSPEC, 12) + TALL, f32),
         ),
-        in_specs=vmem(5),
+        in_specs=vmem(7),
         out_specs=tuple(vmem(2)),
         compiler_params=small,
         cost_estimate=pl.CostEstimate(flops=10**7, bytes_accessed=10**7, transcendentals=0),
-    )(block, left, right, from_low, from_high)
+    )(block, left, right, *rows)
     return pl.pallas_call(
         steps_kernel,
         out_shape=(

time: 68.1 us -> 66.3 us (0.974)
  the two profiles are of different devices: /device:TPU:305 before, /device:TPU:57 now
where the time goes in v4:
time: 66.3 us; the launch traced here: 65.9 us
  starting transfers between devices  40.7 us (61%)
  waiting for transfers between devices  17 us (26%)
  Pallas kernels  6.48 us (10%)
  local copies, waits for them, and re-layouts  0.94 us (1%)
  between operations  0.75 us (1%)
    ppermute x8, starting transfers between devices, shifted(): return (lax.ppermute(upward, axis, up), lax.ppermute(downward, axis, down))  40.7 us
    ppermute x8, waiting for transfers between devices, shifted(): return (lax.ppermute(upward, axis, up), lax.ppermute(downward, axis, down))  17 us
    pallas_call x1, Pallas kernels, per_device(): pl.pallas_call(steps_kernel, out_shape=(jax.ShapeDtypeStruct(flow_moments...  3.51 us
    pallas_call x1, Pallas kernels, per_device(): pl.pallas_call(start_kernel, out_shape=(jax.ShapeDtypeStruct((FIELDS, DEE...  1.95 us
  transfers between devices with their start and end apart: 8, of which 6 were waited for; matrix products, arithmetic and copies ran while one was open for 0% of the time, Pallas kernels for 1%

profile of v4, /device:TPU:57, one launch (start us, length us, event | category | flops | bytes accessed | tf_op | source)
XLA Modules:
  0.0 65.9 jit_solution(8835689437176658334)
XLA Ops:
  0.6 1.9 %shard_map.67 = (f32[15,4,8,128]{3,2,1,0:T(8,128)}, f32[52,8,128]{2,1,0:T(8,128)}, f32[52,8,128]{2,1,0:T(8,128)}) custom-call(f32[10,4,8,128]{3,2,1,0:T(8,128)} %flow_in.1, f32[4,4,8,128]{3,2,1,0:T(8,128)} %species_in.1, s32[4,8,128]{2,1,0:T(8,128)} %fluid_in.1, s32[4,8,128]{2,1,0:T(8,128)} %react_in.1), custom_call_target="tpu_custom_call" | custom-call | tf_op jit(solution)/shard_map/pallas_call | solution.py:435
  2.6 14.3 %collective-permute-start = (f32[52,8,128]{2,1,0:T(8,128)}, f32[52,8,128]{2,1,0:T(8,128)S(1)}, u32[]{:S(2)}, u32[]{:S(2)}) collective-permute-start(f32[52,8,128]{2,1,0:T(8,128)} %get-tuple-element.15), channel_id=1, source_target_pairs={{0,64},{64,128},{128,192},{192,256},{256,320},{320,384},{384,448},... | collective-permute-start | bytes 638984 | tf_op jit(solution)/shard_map/ppermute | solution.py:424
  16.9 1.9 %collective-permute-start.1 = (f32[52,8,128]{2,1,0:T(8,128)}, f32[52,8,128]{2,1,0:T(8,128)S(1)}, u32[]{:S(2)}, u32[]{:S(2)}) collective-permute-start(f32[52,8,128]{2,1,0:T(8,128)} %get-tuple-element.16), channel_id=1, source_target_pairs={{64,0},{128,64},{192,128},{256,192},{320,256},{384,320},{448,384},... | collective-permute-start | bytes 638984 | tf_op jit(solution)/shard_map/ppermute | solution.py:424
  18.8 0.0 copy-start
  18.8 0.9 %copy-done = f32[15,4,8,128]{3,2,1,0:T(8,128)S(1)} copy-done((f32[15,4,8,128]{3,2,1,0:T(8,128)S(1)}, f32[15,4,8,128]{3,2,1,0:T(8,128)}, u32[]{:S(2)}) %copy-start) | copy-done | bytes 245784
  19.7 0.3 shard_map.68
  20.1 4.5 %collective-permute-start.2 = (f32[30,8,128]{2,1,0:T(8,128)S(1)}, f32[30,8,128]{2,1,0:T(8,128)S(1)}, u32[]{:S(2)}, u32[]{:S(2)}) collective-permute-start(f32[30,8,128]{2,1,0:T(8,128)S(1)} %get-tuple-element.17), channel_id=1, source_target_pairs={{0,8},{8,16},{16,24},{24,32},{32,40},{40,48},{48,56},{1,9},{9,17},... | collective-permute-start | bytes 368648 | tf_op jit(solution)/shard_map/ppermute | solution.py:424
  24.6 1.9 %collective-permute-start.3 = (f32[30,8,128]{2,1,0:T(8,128)S(1)}, f32[30,8,128]{2,1,0:T(8,128)S(1)}, u32[]{:S(2)}, u32[]{:S(2)}) collective-permute-start(f32[30,8,128]{2,1,0:T(8,128)S(1)} %get-tuple-element.18), channel_id=1, source_target_pairs={{8,0},{16,8},{24,16},{32,24},{40,32},{48,40},{56,48},{9,1},{17,9},... | collective-permute-start | bytes 368648 | tf_op jit(solution)/shard_map/ppermute | solution.py:424
  26.5 0.0 collective-permute-done.2.own_up
  26.5 5.2 %collective-permute-done.3.own_down = f32[30,8,128]{2,1,0:T(8,128)S(1)} collective-permute-done((f32[30,8,128]{2,1,0:T(8,128)S(1)}, f32[30,8,128]{2,1,0:T(8,128)S(1)}, u32[]{:S(2)}, u32[]{:S(2)}) %collective-permute-start.3) | collective-permute-done | bytes 122912 | tf_op jit(solution)/shard_map/ppermute | solution.py:424
  31.7 0.9 %collective-permute-done.left_ref = f32[52,8,128]{2,1,0:T(8,128)S(1)} collective-permute-done((f32[52,8,128]{2,1,0:T(8,128)}, f32[52,8,128]{2,1,0:T(8,128)S(1)}, u32[]{:S(2)}, u32[]{:S(2)}) %collective-permute-start) | collective-permute-done | bytes 213024 | tf_op jit(solution)/shard_map/ppermute | solution.py:424
  32.7 1.4 %collective-permute-done.1.right_ref = f32[52,8,128]{2,1,0:T(8,128)S(1)} collective-permute-done((f32[52,8,128]{2,1,0:T(8,128)}, f32[52,8,128]{2,1,0:T(8,128)S(1)}, u32[]{:S(2)}, u32[]{:S(2)}) %collective-permute-start.1) | collective-permute-done | bytes 213024 | tf_op jit(solution)/shard_map/ppermute | solution.py:424
  34.1 4.5 %collective-permute-start.4 = (f32[52,8,128]{2,1,0:T(8,128)S(1)}, f32[52,8,128]{2,1,0:T(8,128)S(1)}, u32[]{:S(2)}, u32[]{:S(2)}) collective-permute-start(f32[52,8,128]{2,1,0:T(8,128)S(1)} %get-tuple-element.19), channel_id=1, source_target_pairs={{0,8},{8,16},{16,24},{24,32},{32,40},{40,48},{48,56},{1,9},{9,17},... | collective-permute-start | bytes 638984 | tf_op jit(solution)/shard_map/ppermute | solution.py:424
  38.6 1.9 %collective-permute-start.5 = (f32[52,8,128]{2,1,0:T(8,128)S(1)}, f32[52,8,128]{2,1,0:T(8,128)S(1)}, u32[]{:S(2)}, u32[]{:S(2)}) collective-permute-start(f32[52,8,128]{2,1,0:T(8,128)S(1)} %get-tuple-element.20), channel_id=1, source_target_pairs={{8,0},{16,8},{24,16},{32,24},{40,32},{48,40},{56,48},{9,1},{17,9},... | collective-permute-start | bytes 638984 | tf_op jit(solution)/shard_map/ppermute | solution.py:424
  40.5 0.8 %collective-permute-done.4.up_ref = f32[52,8,128]{2,1,0:T(8,128)S(1)} collective-permute-done((f32[52,8,128]{2,1,0:T(8,128)S(1)}, f32[52,8,128]{2,1,0:T(8,128)S(1)}, u32[]{:S(2)}, u32[]{:S(2)}) %collective-permute-start.4) | collective-permute-done | bytes 213024 | tf_op jit(solution)/shard_map/ppermute | solution.py:424
  41.4 5.0 %collective-permute-done.5.down_ref = f32[52,8,128]{2,1,0:T(8,128)S(1)} collective-permute-done((f32[52,8,128]{2,1,0:T(8,128)S(1)}, f32[52,8,128]{2,1,0:T(8,128)S(1)}, u32[]{:S(2)}, u32[]{:S(2)}) %collective-permute-start.5) | collective-permute-done | bytes 213024 | tf_op jit(solution)/shard_map/ppermute | solution.py:424
  46.4 0.1 shard_map.71.edge_ref
  46.5 9.7 %collective-permute-start.6 = (f32[15,16,128]{2,1,0:T(8,128)S(1)}, f32[15,16,128]{2,1,0:T(8,128)S(1)}, u32[]{:S(2)}, u32[]{:S(2)}) collective-permute-start(f32[15,16,128]{2,1,0:T(8,128)S(1)} %shard_map.71.edge_ref), channel_id=1, source_target_pairs={{0,1},{1,2},{2,3},{3,4},{4,5},{5,6},{6,7},{8,9},{9,10},{10,11},{11... | collective-permute-start | bytes 368648 | tf_op jit(solution)/shard_map/ppermute | solution.py:424
  56.2 1.9 %collective-permute-start.7 = (f32[15,16,128]{2,1,0:T(8,128)S(1)}, f32[15,16,128]{2,1,0:T(8,128)S(1)}, u32[]{:S(2)}, u32[]{:S(2)}) collective-permute-start(f32[15,16,128]{2,1,0:T(8,128)S(1)} %shard_map.71.edge_ref), channel_id=1, source_target_pairs={{1,0},{2,1},{3,2},{4,3},{5,4},{6,5},{7,6},{9,8},{10,9},{11,10},{12... | collective-permute-start | bytes 368648 | tf_op jit(solution)/shard_map/ppermute | solution.py:424
  58.1 0.6 shard_map.70
  58.7 0.0 collective-permute-done.6.below_ref
  58.7 3.7 %collective-permute-done.7.above_ref = f32[15,16,128]{2,1,0:T(8,128)S(1)} collective-permute-done((f32[15,16,128]{2,1,0:T(8,128)S(1)}, f32[15,16,128]{2,1,0:T(8,128)S(1)}, u32[]{:S(2)}, u32[]{:S(2)}) %collective-permute-start.7) | collective-permute-done | bytes 122912 | tf_op jit(solution)/shard_map/ppermute | solution.py:424
  62.4 3.5 %shard_map.72 = (f32[10,4,8,128]{3,2,1,0:T(8,128)}, f32[4,4,8,128]{3,2,1,0:T(8,128)}, f32[4,8,128]{2,1,0:T(8,128)}) custom-call(f32[15,12,16,128]{3,2,1,0:T(8,128)S(1)} %get-tuple-element.21.first_state, f32[24,12,16,128]{3,2,1,0:T(8,128)S(1)} %get-tuple-element.22.first_sent, f32[15,16,128]{2,1,0:T(8,128)S(1)} %shard_map.71.edge_ref, ...), custom_call_target="tpu_custom_call" | custom-call | tf_op jit(solution)/shard_map/pallas_call | solution.py:490
  (1 shorter events, 0.0 us)
Async XLA Ops:
  2.6 30.1 %collective-permute-start = (f32[52,8,128]{2,1,0:T(8,128)}, f32[52,8,128]{2,1,0:T(8,128)S(1)}, u32[]{:S(2)}, u32[]{:S(2)}) collective-permute-start(f32[52,8,128]{2,1,0:T(8,128)} %get-tuple-element.15), channel_id=1, source_target_pairs={{0,64},{64,128},{128,192},{192,256},{256,320},{320,384},{384,448},... | collective-permute-start | bytes 638984 | tf_op jit(solution)/shard_map/ppermute | solution.py:424
  16.9 17.2 %collective-permute-start.1 = (f32[52,8,128]{2,1,0:T(8,128)}, f32[52,8,128]{2,1,0:T(8,128)S(1)}, u32[]{:S(2)}, u32[]{:S(2)}) collective-permute-start(f32[52,8,128]{2,1,0:T(8,128)} %get-tuple-element.16), channel_id=1, source_target_pairs={{64,0},{128,64},{192,128},{256,192},{320,256},{384,320},{448,384},... | collective-permute-start | bytes 638984 | tf_op jit(solution)/shard_map/ppermute | solution.py:424
  18.8 0.9 %copy-start = (f32[15,4,8,128]{3,2,1,0:T(8,128)S(1)}, f32[15,4,8,128]{3,2,1,0:T(8,128)}, u32[]{:S(2)}) copy-start(f32[15,4,8,128]{3,2,1,0:T(8,128)} %get-tuple-element.13.block_in) | copy-start | bytes 737284
  20.1 6.5 %collective-permute-start.2 = (f32[30,8,128]{2,1,0:T(8,128)S(1)}, f32[30,8,128]{2,1,0:T(8,128)S(1)}, u32[]{:S(2)}, u32[]{:S(2)}) collective-permute-start(f32[30,8,128]{2,1,0:T(8,128)S(1)} %get-tuple-element.17), channel_id=1, source_target_pairs={{0,8},{8,16},{16,24},{24,32},{32,40},{40,48},{48,56},{1,9},{9,17},... | collective-permute-start | bytes 368648 | tf_op jit(solution)/shard_map/ppermute | solution.py:424
  24.6 7.1 %collective-permute-start.3 = (f32[30,8,128]{2,1,0:T(8,128)S(1)}, f32[30,8,128]{2,1,0:T(8,128)S(1)}, u32[]{:S(2)}, u32[]{:S(2)}) collective-permute-start(f32[30,8,128]{2,1,0:T(8,128)S(1)} %get-tuple-element.18), channel_id=1, source_target_pairs={{8,0},{16,8},{24,16},{32,24},{40,32},{48,40},{56,48},{9,1},{17,9},... | collective-permute-start | bytes 368648 | tf_op jit(solution)/shard_map/ppermute | solution.py:424
  34.1 7.3 %collective-permute-start.4 = (f32[52,8,128]{2,1,0:T(8,128)S(1)}, f32[52,8,128]{2,1,0:T(8,128)S(1)}, u32[]{:S(2)}, u32[]{:S(2)}) collective-permute-start(f32[52,8,128]{2,1,0:T(8,128)S(1)} %get-tuple-element.19), channel_id=1, source_target_pairs={{0,8},{8,16},{16,24},{24,32},{32,40},{40,48},{48,56},{1,9},{9,17},... | collective-permute-start | bytes 638984 | tf_op jit(solution)/shard_map/ppermute | solution.py:424
  38.6 7.8 %collective-permute-start.5 = (f32[52,8,128]{2,1,0:T(8,128)S(1)}, f32[52,8,128]{2,1,0:T(8,128)S(1)}, u32[]{:S(2)}, u32[]{:S(2)}) collective-permute-start(f32[52,8,128]{2,1,0:T(8,128)S(1)} %get-tuple-element.20), channel_id=1, source_target_pairs={{8,0},{16,8},{24,16},{32,24},{40,32},{48,40},{56,48},{9,1},{17,9},... | collective-permute-start | bytes 638984 | tf_op jit(solution)/shard_map/ppermute | solution.py:424
  46.5 12.2 %collective-permute-start.6 = (f32[15,16,128]{2,1,0:T(8,128)S(1)}, f32[15,16,128]{2,1,0:T(8,128)S(1)}, u32[]{:S(2)}, u32[]{:S(2)}) collective-permute-start(f32[15,16,128]{2,1,0:T(8,128)S(1)} %shard_map.71.edge_ref), channel_id=1, source_target_pairs={{0,1},{1,2},{2,3},{3,4},{4,5},{5,6},{6,7},{8,9},{9,10},{10,11},{11... | collective-permute-start | bytes 368648 | tf_op jit(solution)/shard_map/ppermute | solution.py:424
  56.2 6.2 %collective-permute-start.7 = (f32[15,16,128]{2,1,0:T(8,128)S(1)}, f32[15,16,128]{2,1,0:T(8,128)S(1)}, u32[]{:S(2)}, u32[]{:S(2)}) collective-permute-start(f32[15,16,128]{2,1,0:T(8,128)S(1)} %shard_map.71.edge_ref), channel_id=1, source_target_pairs={{1,0},{2,1},{3,2},{4,3},{5,4},{6,5},{7,6},{9,8},{10,9},{11,10},{12... | collective-permute-start | bytes 368648 | tf_op jit(solution)/shard_map/ppermute | solution.py:424

commit v5 on v4

--- a/solution.py
+++ b/solution.py
@@ -158,8 +158,13 @@
     return pltpu.roll(value, shift, axis)
 
 
-def first_slot():
-    return 4 * lax.rem(lax.axis_index("gx"), 4)
+def base_at(x):
+    return lax.rem(48 * lax.axis_index("gx") + 12 * x + 80, LANES)
+
+
+def within(x, first, end, shape):
+    place = (lanes_of(shape) + (LANES - base_at(x) - first)) & (LANES - 1)
+    return place < end - first
 
 
 def towards(sign):
@@ -174,7 +179,7 @@
     for copy in copies:
         copy.wait()
     for x in range(DEEP):
-        slot = first_slot() + x
+        turn = lax.rem(base_at(DEEP + x) + 8, LANES)
         fluid = fluid_ref[x].astype(jnp.float32)
         react = react_ref[x].astype(jnp.float32)
         flow = [flow_ref[k, x] * fluid for k in range(10)]
@@ -187,10 +192,10 @@
                 parts = [flow_pops[c] for c in towards(sign)] + [species_pops[towards(sign)[0]], fluid]
                 parts[0] = jnp.where(fluid > 0.5, parts[0], react)
                 for k, value in enumerate(parts):
-                    ref[NEAR + k] = roll(value, 8 * slot + 4, 1)
+                    ref[NEAR + k] = roll(value, turn, 1)
         post[0] = jnp.where(fluid > 0.5, post[0], react)
         for k, value in enumerate(post + [fluid]):
-            value = roll(value, 8 * slot + 4, 1)
+            value = roll(value, turn, 1)
             block_ref[k, x] = value
             if x > 0:
                 right_ref[3 * k + x - 1] = value
@@ -227,10 +232,6 @@
         put_rows(up_ref, down_ref, k, left_ref[k], right_ref[k])
 
 
-def slot_at(x):
-    return lax.rem(first_slot() + x + 12, 16)
-
-
 TALL = (2 * ROWS, LANES)
 
 
@@ -259,19 +260,18 @@
 
 def edges_kernel(own_ref, left_ref, right_ref, own_up, own_down, up_ref, down_ref, edge_ref):
     refs = (own_ref, left_ref, right_ref)
-    slot_of = lanes_of((ROWS, LANES)) // 8
-    here = [slot_of == slot_at(x) for x in range(12)]
+    here = [within(x, 4, 12, (ROWS, LANES)) for x in range(12)]
     for field in range(FIELDS):
         near = jnp.zeros((ROWS, LANES), jnp.float32)
         beyond = near
         for x, value in rows_beyond(field, own_up, own_down, up_ref, down_ref).items():
             near = jnp.where(here[x], layer_of(field, x, *refs), near)
             beyond = jnp.where(here[x], value, beyond)
-        if field < 7:
-            one, two = halves(up_ref, down_ref, FAR_ROWS + field)
-            for x, value, ref in ((0, one, left_ref), (11, two, right_ref)):
-                near = jnp.where(here[x], ref[NEAR + field], near)
-                beyond = jnp.where(here[x], value, beyond)
+        if field < 14:
+            x, ref = ((0, left_ref), (11, right_ref))[field // 7]
+            value = halves(up_ref, down_ref, FAR_ROWS + field % 7)[field // 7]
+            near = jnp.where(here[x], ref[NEAR + field % 7], near)
+            beyond = jnp.where(here[x], value, beyond)
         edge_ref[field, 0:ROWS] = near
         edge_ref[field, ROWS : 2 * ROWS] = beyond
 
@@ -290,7 +290,7 @@
 
 def moved(value, c):
     cx, cy, cz = MOVING[c]
-    return roll(roll(value, 8 * cx + cz, 1), cy, 0)
+    return roll(roll(value, 12 * cx + cz, 1), cy, 0)
 
 
 def send(state_ref, sent_ref, x):
@@ -302,119 +302,117 @@
         sent_ref[NFLOW + c, x] = moved(species_pops[c], c)
 
 
-def first_sends_kernel(own_ref, left_ref, right_ref, own_up, own_down, up_ref, down_ref, state_ref, sent_ref):
+def release(arriving_species):
+    parts = [value[0:ROWS] for value in arriving_species]
+    parts = [jnp.where(is_number(part), SPECIES_WEIGHT - part, 0.0) for part in parts]
+    return (parts[0] + parts[1]) + (parts[2] + parts[3]) + (parts[4] + parts[5])
+
+
+def results(post, flow, species, released):
+    fluid = is_number(post[0])
+    out = [jnp.where(fluid, value, 0.0) for value in flow + species]
+    return out + [jnp.where(post[10] > LARGEST, REACT_RATE * released, 0.0)]
+
+
+def layers_kernel(
+    own_ref, left_ref, right_ref, own_up, own_down, up_ref, down_ref, result_ref, near_ref, far_ref, state, sent
+):
     refs = (own_ref, left_ref, right_ref)
     for field in range(FIELDS):
         for x, value in rows_beyond(field, own_up, own_down, up_ref, down_ref).items():
-            state_ref[field, x, 0:ROWS] = layer_of(field, x, *refs)
-            state_ref[field, x, ROWS : 2 * ROWS] = value
+            state[field, x, 0:ROWS] = layer_of(field, x, *refs)
+            state[field, x, ROWS : 2 * ROWS] = value
     for x in range(1, 11):
-        rho, conc = marked(state_ref[0, x], state_ref[10, x], state_ref[FLUID, x])
-        state_ref[0, x] = rho
-        state_ref[10, x] = conc
-        send(state_ref, sent_ref, x)
+        rho, conc = marked(state[0, x], state[10, x], state[FLUID, x])
+        state[0, x] = rho
+        state[10, x] = conc
+    for side in range(2):
+        own = [within(x, 0, 8, TALL) if side else within(x, 8, 16, TALL) for x in range(1, 11)]
+        for field in range(14):
+            near = jnp.full(TALL, SOLID if field in (0, 10) else 0.0, jnp.float32)
+            for x in range(1, 11):
+                near = jnp.where(own[x - 1], state[field, x], near)
+            near_ref[side, field] = near
     beyond = [halves(up_ref, down_ref, FAR_ROWS + k) for k in range(7)]
     for end, (x, sign, ref) in enumerate(((0, 1, left_ref), (11, -1, right_ref))):
-        parts = [jnp.concatenate([ref[NEAR + k], beyond[k][end]]) for k in range(7)]
-        parts = marked_far(parts)
+        parts = marked_far([jnp.concatenate([ref[NEAR + k], beyond[k][end]]) for k in range(7)])
         along = towards(sign)
         for k, c in enumerate(along):
-            sent_ref[c, x] = moved(parts[k], c)
-        sent_ref[NFLOW + along[0], x] = moved(parts[5], along[0])
-
-
-def steps_kernel(
-    first_state,
-    first_sent,
-    edge_ref,
-    below_ref,
-    above_ref,
-    flow_out,
-    species_out,
-    dissolved_out,
-    state,
-    sent,
-    strips,
-    strip_sent,
-):
-    lane = lanes_of(TALL)
-    inner = lane % 8 < 4
-
-    far_strips = []
-    for side in range(2):
-        for field in range(FIELDS):
-            near, beyond = edge_ref[field], (below_ref, above_ref)[side][field]
-            strips[side, field] = jnp.where(inner, near, beyond) if side else jnp.where(inner, beyond, near)
-        far_strips.append(marked_far([strips[side, k] for k in range(7)]))
-        rho, conc = marked(strips[side, 0], strips[side, 10], strips[side, FLUID])
-        strips[side, 0] = rho
-        strips[side, 10] = conc
-
-    def turned_back(value, x):
-        return roll(value, 124 - 8 * slot_at(x), 1)
-
+            sent[c, x] = moved(parts[k], c)
+        sent[NFLOW + along[0], x] = moved(parts[5], along[0])
+        for k in range(6):
+            far_ref[end, k] = parts[k]
     released = [jnp.zeros((ROWS, LANES), jnp.float32)] * DEEP
     for step in range(STEPS):
         last = step == STEPS - 1
-        state_now, sent_now = (first_state, first_sent) if step == 0 else (state, sent)
-        for side in range(2):
-            post = [strips[side, k] for k in range(14)]
-            _, flow_pops = flow_populations(post[:10])
-            _, species_pops = species_populations(post[10:])
-            if step == 0:
-                for x, sign in ((0, 1), (11, -1)):
-                    here = lane // 8 == slot_at(x)
-                    for k, c in enumerate(towards(sign)):
-                        flow_pops[c] = jnp.where(here, far_strips[side][k], flow_pops[c])
-                    c = towards(sign)[0]
-                    species_pops[c] = jnp.where(here, far_strips[side][5], species_pops[c])
-            wanted = [c for c in range(NFLOW) if not last or MOVING[c][2] == (1, -1)[side]]
-            arriving = {c: moved(flow_pops[c], c) for c in wanted}
-            arriving_species = {c: moved(species_pops[c], c) for c in wanted if c < NSPEC}
-            for c in wanted:
-                if MOVING[c][2] == (1, -1)[side]:
-                    strip_sent[c] = arriving[c]
-                    if c < NSPEC:
-                        strip_sent[NFLOW + c] = arriving_species[c]
-            if not last:
-                new_flow, new_species = pass_on(post, arriving, arriving_species)
-                for k, value in enumerate(next_post(post, new_flow, new_species)):
-                    strips[side, k] = value
-        if step > 0:
-            for x in range(step, 12 - step):
-                send(state, sent, x)
+        for x in range(max(step, 1), 12 - max(step, 1)):
+            send(state, sent, x)
         height = ROWS if last else 2 * ROWS
         for x in range(step + 1, 11 - step):
-            first = lane[0:height] == 8 * slot_at(x) + 4
-            end = lane[0:height] == 8 * slot_at(x) + 3
-
-            def arrives(place, c):
-                cx, _, cz = MOVING[c]
-                value = sent_now[place, x - cx, 0:height]
-                if cz:
-                    value = jnp.where(first if cz > 0 else end, strip_sent[place, 0:height], value)
-                return value
-
-            post = [state_now[k, x, 0:height] for k in range(14)]
-            arriving = [arrives(c, c) for c in range(NFLOW)]
-            arriving_species = [arrives(NFLOW + c, c) for c in range(NSPEC)]
+            post = [state[k, x, 0:height] for k in range(14)]
+            arriving = [sent[c, x - MOVING[c][0], 0:height] for c in range(NFLOW)]
+            arriving_species = [sent[NFLOW + c, x - MOVING[c][0], 0:height] for c in range(NSPEC)]
             new_flow, new_species = pass_on(post, arriving, arriving_species)
-            if 0 <= x - DEEP < DEEP:
-                parts = [value[0:ROWS] for value in arriving_species]
-                parts = [jnp.where(is_number(part), SPECIES_WEIGHT - part, 0.0) for part in parts]
-                parts = (parts[0] + parts[1]) + (parts[2] + parts[3]) + (parts[4] + parts[5])
-                released[x - DEEP] = released[x - DEEP] + parts
+            own = x - DEEP
+            if 0 <= own < DEEP:
+                released[own] = released[own] + release(arriving_species)
             if last:
-                fluid = is_number(post[0])
-                for k in range(10):
-                    flow_out[k, x - DEEP] = turned_back(jnp.where(fluid, new_flow[k], 0.0), x)
-                for k in range(4):
-                    species_out[k, x - DEEP] = turned_back(jnp.where(fluid, new_species[k], 0.0), x)
-                gone = jnp.where(post[10] > LARGEST, REACT_RATE * released[x - DEEP], 0.0)
-                dissolved_out[x - DEEP] = turned_back(gone, x)
+                for k, value in enumerate(results(post, new_flow, new_species, released[own])):
+                    result_ref[k, own] = value
             else:
                 for k, value in enumerate(next_post(post, new_flow, new_species)):
                     state[k, x] = value
+
+
+def strips_kernel(result_ref, near_ref, far_ref, below_ref, above_ref, flow_out, species_out, dissolved_out, strips):
+    for side, ref in enumerate((below_ref, above_ref)):
+        first = 0 if side else 4
+        place = (lanes_of(TALL) + (LANES - base_at(1) - first)) & (LANES - 1)
+        place = place - 12 * ((place * 43) >> 9)
+        outside = place >= 8 if side else place < 4
+        rho, conc = marked(ref[0], ref[10], ref[FLUID])
+        post = [jnp.where(outside, rho if k == 0 else conc if k == 10 else ref[k], near_ref[side, k]) for k in range(14)]
+        released = jnp.zeros((ROWS, LANES), jnp.float32)
+        for step in range(STEPS):
+            last = step == STEPS - 1
+            _, flow_pops = flow_populations(post[:10])
+            _, species_pops = species_populations(post[10:])
+            arriving = [moved(flow_pops[c], c) for c in range(NFLOW)]
+            arriving_species = [moved(species_pops[c], c) for c in range(NSPEC)]
+            if step == 0:
+                for end, (x, sign) in enumerate(((0, 1), (11, -1))):
+                    here = within(x + sign, first, first + 12, TALL)
+                    there = within(x, 8, 12, TALL) if side else within(x, 4, 8, TALL)
+                    parts = marked_far([ref[7 * end + k] for k in range(7)])
+                    parts = [jnp.where(there, part, far_ref[end, k]) for k, part in enumerate(parts)]
+                    for k, c in enumerate(towards(sign)):
+                        arriving[c] = jnp.where(here, moved(parts[k], c), arriving[c])
+                    c = towards(sign)[0]
+                    arriving_species[c] = jnp.where(here, moved(parts[5], c), arriving_species[c])
+            released = released + release(arriving_species)
+            if last:
+                post = [value[0:ROWS] for value in post]
+                arriving = [value[0:ROWS] for value in arriving]
+                arriving_species = [value[0:ROWS] for value in arriving_species]
+            new_flow, new_species = pass_on(post, arriving, arriving_species)
+            if last:
+                for k, value in enumerate(results(post, new_flow, new_species, released)):
+                    strips[side, k] = value
+            else:
+                post = next_post(post, new_flow, new_species)
+    for own in range(DEEP):
+        x = DEEP + own
+        low, high = within(x, 8, 12, (ROWS, LANES)), within(x, 4, 8, (ROWS, LANES))
+        back = lax.rem(2 * LANES - 8 - base_at(x), LANES)
+        for k in range(15):
+            value = jnp.where(low, strips[0, k], jnp.where(high, strips[1, k], result_ref[k, own]))
+            value = roll(value, back, 1)
+            if k < 10:
+                flow_out[k, own] = value
+            elif k < 14:
+                species_out[k - 10, own] = value
+            else:
+                dissolved_out[own] = value
 
 
 def shifted(upward, downward, axis, wrap):
@@ -476,19 +474,24 @@
         compiler_params=small,
     )(block, left, right, *rows)
     below, above = shifted(edge, edge, "gz", False)
-    state, sent = pl.pallas_call(
-        first_sends_kernel,
+    result, near, far = pl.pallas_call(
+        layers_kernel,
         out_shape=(
-            jax.ShapeDtypeStruct((FIELDS, 12) + TALL, f32),
-            jax.ShapeDtypeStruct((NFLOW + NSPEC, 12) + TALL, f32),
+            jax.ShapeDtypeStruct((15, DEEP, ROWS, LANES), f32),
+            jax.ShapeDtypeStruct((2, 14) + TALL, f32),
+            jax.ShapeDtypeStruct((2, 6) + TALL, f32),
         ),
         in_specs=vmem(7),
-        out_specs=tuple(vmem(2)),
+        out_specs=tuple(vmem(3)),
+        scratch_shapes=[
+            pltpu.VMEM((FIELDS, 12) + TALL, f32),
+            pltpu.VMEM((NFLOW + NSPEC, 12) + TALL, f32),
+        ],
         compiler_params=small,
         cost_estimate=pl.CostEstimate(flops=10**7, bytes_accessed=10**7, transcendentals=0),
     )(block, left, right, *rows)
     return pl.pallas_call(
-        steps_kernel,
+        strips_kernel,
         out_shape=(
             jax.ShapeDtypeStruct(flow_moments.shape, f32),
             jax.ShapeDtypeStruct(species_moments.shape, f32),
@@ -496,14 +499,9 @@
         ),
         in_specs=vmem(5),
         out_specs=tuple(vmem(3)),
-        scratch_shapes=[
-            pltpu.VMEM((FIELDS, 12) + TALL, f32),
-            pltpu.VMEM((NFLOW + NSPEC, 12) + TALL, f32),
-            pltpu.VMEM((2, FIELDS) + TALL, f32),
-            pltpu.VMEM((NFLOW + NSPEC,) + TALL, f32),
-        ],
+        scratch_shapes=[pltpu.VMEM((2, 15, ROWS, LANES), f32)],
         compiler_params=small,
-    )(state, sent, edge, below, above)
+    )(result, near, far, below, above)
 
 
 def solution(mesh):

time: 66.3 us -> 64.4 us (0.971)
  waiting for transfers between devices: 17 us -> 15.3 us
    ppermute x8, waiting for transfers between devices: 17 us -> 15.3 us  [shifted(): return (lax.ppermute(upward, axis, up), lax.ppermute(downward, axis, down))]
  transfers between devices with their start and end apart: 8 -> 8, of which waited for: 6 -> 6; matrix products, arithmetic and copies ran while one was open for 0% -> 0% of each run, Pallas kernels for 1% -> 4%
where the time goes in v5:
time: 64.4 us; the launch traced here: 64 us
  starting transfers between devices  40.7 us (63%)
  waiting for transfers between devices  15.3 us (24%)
  Pallas kernels  6.37 us (10%)
  local copies, waits for them, and re-layouts  0.94 us (1%)
  between operations  0.75 us (1%)
    ppermute x8, starting transfers between devices, shifted(): return (lax.ppermute(upward, axis, up), lax.ppermute(downward, axis, down))  40.7 us
    ppermute x8, waiting for transfers between devices, shifted(): return (lax.ppermute(upward, axis, up), lax.ppermute(downward, axis, down))  15.3 us
    pallas_call x1, Pallas kernels, per_device(): pl.pallas_call(layers_kernel, out_shape=(jax.ShapeDtypeStruct((15, DEEP,...  2.37 us
    pallas_call x1, Pallas kernels, per_device(): pl.pallas_call(start_kernel, out_shape=(jax.ShapeDtypeStruct((FIELDS, DEE...  1.95 us
    pallas_call x1, Pallas kernels, per_device(): pl.pallas_call(strips_kernel, out_shape=(jax.ShapeDtypeStruct(flow_moment...  1.61 us
  transfers between devices with their start and end apart: 8, of which 6 were waited for; matrix products, arithmetic and copies ran while one was open for 0% of the time, Pallas kernels for 4%

profile of v5, /device:TPU:57, one launch (start us, length us, event | category | flops | bytes accessed | tf_op | source)
XLA Modules:
  0.0 64.0 jit_solution(13537768724256900813)
XLA Ops:
  0.6 1.9 %shard_map.67 = (f32[15,4,8,128]{3,2,1,0:T(8,128)}, f32[52,8,128]{2,1,0:T(8,128)}, f32[52,8,128]{2,1,0:T(8,128)}) custom-call(f32[10,4,8,128]{3,2,1,0:T(8,128)} %flow_in.1, f32[4,4,8,128]{3,2,1,0:T(8,128)} %species_in.1, s32[4,8,128]{2,1,0:T(8,128)} %fluid_in.1, s32[4,8,128]{2,1,0:T(8,128)} %react_in.1), custom_call_target="tpu_custom_call" | custom-call | tf_op jit(solution)/shard_map/pallas_call | solution.py:433
  2.6 14.3 %collective-permute-start = (f32[52,8,128]{2,1,0:T(8,128)}, f32[52,8,128]{2,1,0:T(8,128)S(1)}, u32[]{:S(2)}, u32[]{:S(2)}) collective-permute-start(f32[52,8,128]{2,1,0:T(8,128)} %get-tuple-element.16), channel_id=1, source_target_pairs={{0,64},{64,128},{128,192},{192,256},{256,320},{320,384},{384,448},... | collective-permute-start | bytes 638984 | tf_op jit(solution)/shard_map/ppermute | solution.py:422
  16.9 1.9 %collective-permute-start.1 = (f32[52,8,128]{2,1,0:T(8,128)}, f32[52,8,128]{2,1,0:T(8,128)S(1)}, u32[]{:S(2)}, u32[]{:S(2)}) collective-permute-start(f32[52,8,128]{2,1,0:T(8,128)} %get-tuple-element.17), channel_id=1, source_target_pairs={{64,0},{128,64},{192,128},{256,192},{320,256},{384,320},{448,384},... | collective-permute-start | bytes 638984 | tf_op jit(solution)/shard_map/ppermute | solution.py:422
  18.8 0.0 copy-start
  18.8 0.9 %copy-done = f32[15,4,8,128]{3,2,1,0:T(8,128)S(1)} copy-done((f32[15,4,8,128]{3,2,1,0:T(8,128)S(1)}, f32[15,4,8,128]{3,2,1,0:T(8,128)}, u32[]{:S(2)}) %copy-start) | copy-done | bytes 245784
  19.7 0.3 shard_map.68
  20.1 4.5 %collective-permute-start.2 = (f32[30,8,128]{2,1,0:T(8,128)S(1)}, f32[30,8,128]{2,1,0:T(8,128)S(1)}, u32[]{:S(2)}, u32[]{:S(2)}) collective-permute-start(f32[30,8,128]{2,1,0:T(8,128)S(1)} %get-tuple-element.18), channel_id=1, source_target_pairs={{0,8},{8,16},{16,24},{24,32},{32,40},{40,48},{48,56},{1,9},{9,17},... | collective-permute-start | bytes 368648 | tf_op jit(solution)/shard_map/ppermute | solution.py:422
  24.6 1.9 %collective-permute-start.3 = (f32[30,8,128]{2,1,0:T(8,128)S(1)}, f32[30,8,128]{2,1,0:T(8,128)S(1)}, u32[]{:S(2)}, u32[]{:S(2)}) collective-permute-start(f32[30,8,128]{2,1,0:T(8,128)S(1)} %get-tuple-element.19), channel_id=1, source_target_pairs={{8,0},{16,8},{24,16},{32,24},{40,32},{48,40},{56,48},{9,1},{17,9},... | collective-permute-start | bytes 368648 | tf_op jit(solution)/shard_map/ppermute | solution.py:422
  26.5 0.0 collective-permute-done.2.own_up
  26.5 5.2 %collective-permute-done.3.own_down = f32[30,8,128]{2,1,0:T(8,128)S(1)} collective-permute-done((f32[30,8,128]{2,1,0:T(8,128)S(1)}, f32[30,8,128]{2,1,0:T(8,128)S(1)}, u32[]{:S(2)}, u32[]{:S(2)}) %collective-permute-start.3) | collective-permute-done | bytes 122912 | tf_op jit(solution)/shard_map/ppermute | solution.py:422
  31.7 0.9 %collective-permute-done.left_ref = f32[52,8,128]{2,1,0:T(8,128)S(1)} collective-permute-done((f32[52,8,128]{2,1,0:T(8,128)}, f32[52,8,128]{2,1,0:T(8,128)S(1)}, u32[]{:S(2)}, u32[]{:S(2)}) %collective-permute-start) | collective-permute-done | bytes 213024 | tf_op jit(solution)/shard_map/ppermute | solution.py:422
  32.7 1.4 %collective-permute-done.1.right_ref = f32[52,8,128]{2,1,0:T(8,128)S(1)} collective-permute-done((f32[52,8,128]{2,1,0:T(8,128)}, f32[52,8,128]{2,1,0:T(8,128)S(1)}, u32[]{:S(2)}, u32[]{:S(2)}) %collective-permute-start.1) | collective-permute-done | bytes 213024 | tf_op jit(solution)/shard_map/ppermute | solution.py:422
  34.1 4.5 %collective-permute-start.4 = (f32[52,8,128]{2,1,0:T(8,128)S(1)}, f32[52,8,128]{2,1,0:T(8,128)S(1)}, u32[]{:S(2)}, u32[]{:S(2)}) collective-permute-start(f32[52,8,128]{2,1,0:T(8,128)S(1)} %get-tuple-element.20), channel_id=1, source_target_pairs={{0,8},{8,16},{16,24},{24,32},{32,40},{40,48},{48,56},{1,9},{9,17},... | collective-permute-start | bytes 638984 | tf_op jit(solution)/shard_map/ppermute | solution.py:422
  38.6 1.9 %collective-permute-start.5 = (f32[52,8,128]{2,1,0:T(8,128)S(1)}, f32[52,8,128]{2,1,0:T(8,128)S(1)}, u32[]{:S(2)}, u32[]{:S(2)}) collective-permute-start(f32[52,8,128]{2,1,0:T(8,128)S(1)} %get-tuple-element.21), channel_id=1, source_target_pairs={{8,0},{16,8},{24,16},{32,24},{40,32},{48,40},{56,48},{9,1},{17,9},... | collective-permute-start | bytes 638984 | tf_op jit(solution)/shard_map/ppermute | solution.py:422
  40.5 0.8 %collective-permute-done.4.up_ref = f32[52,8,128]{2,1,0:T(8,128)S(1)} collective-permute-done((f32[52,8,128]{2,1,0:T(8,128)S(1)}, f32[52,8,128]{2,1,0:T(8,128)S(1)}, u32[]{:S(2)}, u32[]{:S(2)}) %collective-permute-start.4) | collective-permute-done | bytes 213024 | tf_op jit(solution)/shard_map/ppermute | solution.py:422
  41.4 5.0 %collective-permute-done.5.down_ref = f32[52,8,128]{2,1,0:T(8,128)S(1)} collective-permute-done((f32[52,8,128]{2,1,0:T(8,128)S(1)}, f32[52,8,128]{2,1,0:T(8,128)S(1)}, u32[]{:S(2)}, u32[]{:S(2)}) %collective-permute-start.5) | collective-permute-done | bytes 213024 | tf_op jit(solution)/shard_map/ppermute | solution.py:422
  46.4 0.1 shard_map.71
  46.5 9.7 %collective-permute-start.6 = (f32[15,16,128]{2,1,0:T(8,128)S(1)}, f32[15,16,128]{2,1,0:T(8,128)S(1)}, u32[]{:S(2)}, u32[]{:S(2)}) collective-permute-start(f32[15,16,128]{2,1,0:T(8,128)S(1)} %shard_map.71), channel_id=1, source_target_pairs={{0,1},{1,2},{2,3},{3,4},{4,5},{5,6},{6,7},{8,9},{9,10},{10,11},{11... | collective-permute-start | bytes 368648 | tf_op jit(solution)/shard_map/ppermute | solution.py:422
  56.2 1.9 %collective-permute-start.7 = (f32[15,16,128]{2,1,0:T(8,128)S(1)}, f32[15,16,128]{2,1,0:T(8,128)S(1)}, u32[]{:S(2)}, u32[]{:S(2)}) collective-permute-start(f32[15,16,128]{2,1,0:T(8,128)S(1)} %shard_map.71), channel_id=1, source_target_pairs={{1,0},{2,1},{3,2},{4,3},{5,4},{6,5},{7,6},{9,8},{10,9},{11,10},{12... | collective-permute-start | bytes 368648 | tf_op jit(solution)/shard_map/ppermute | solution.py:422
  58.1 2.4 %shard_map.70 = (f32[15,4,8,128]{3,2,1,0:T(8,128)S(1)}, f32[2,14,16,128]{3,2,1,0:T(8,128)S(1)}, f32[2,6,16,128]{3,2,1,0:T(8,128)S(1)}) custom-call(f32[15,4,8,128]{3,2,1,0:T(8,128)S(1)} %get-tuple-element.15.own_ref, f32[52,8,128]{2,1,0:T(8,128)S(1)} %collective-permute-done.left_ref, f32[52,8,128]{2,1,0:T(8,128)S(1)} %collective-permute-done.1.right_ref, ...), custom_call_target="tpu_custom_call" | custom-call | flops 10000000 | bytes 10000000 | tf_op jit(solution)/shard_map/pallas_call | solution.py:477
  60.5 0.0 collective-permute-done.6.below_ref
  60.5 1.9 %collective-permute-done.7.above_ref = f32[15,16,128]{2,1,0:T(8,128)S(1)} collective-permute-done((f32[15,16,128]{2,1,0:T(8,128)S(1)}, f32[15,16,128]{2,1,0:T(8,128)S(1)}, u32[]{:S(2)}, u32[]{:S(2)}) %collective-permute-start.7) | collective-permute-done | bytes 122912 | tf_op jit(solution)/shard_map/ppermute | solution.py:422
  62.4 1.6 %shard_map.72 = (f32[10,4,8,128]{3,2,1,0:T(8,128)}, f32[4,4,8,128]{3,2,1,0:T(8,128)}, f32[4,8,128]{2,1,0:T(8,128)}) custom-call(f32[15,4,8,128]{3,2,1,0:T(8,128)S(1)} %get-tuple-element.22.result_ref, f32[2,14,16,128]{3,2,1,0:T(8,128)S(1)} %get-tuple-element.23.near_ref, f32[2,6,16,128]{3,2,1,0:T(8,128)S(1)} %get-tuple-element.24.far_ref, ...), custom_call_target="tpu_custom_call" | custom-call | tf_op jit(solution)/shard_map/pallas_call | solution.py:493
  (1 shorter events, 0.0 us)
Async XLA Ops:
  2.6 30.1 %collective-permute-start = (f32[52,8,128]{2,1,0:T(8,128)}, f32[52,8,128]{2,1,0:T(8,128)S(1)}, u32[]{:S(2)}, u32[]{:S(2)}) collective-permute-start(f32[52,8,128]{2,1,0:T(8,128)} %get-tuple-element.16), channel_id=1, source_target_pairs={{0,64},{64,128},{128,192},{192,256},{256,320},{320,384},{384,448},... | collective-permute-start | bytes 638984 | tf_op jit(solution)/shard_map/ppermute | solution.py:422
  16.9 17.2 %collective-permute-start.1 = (f32[52,8,128]{2,1,0:T(8,128)}, f32[52,8,128]{2,1,0:T(8,128)S(1)}, u32[]{:S(2)}, u32[]{:S(2)}) collective-permute-start(f32[52,8,128]{2,1,0:T(8,128)} %get-tuple-element.17), channel_id=1, source_target_pairs={{64,0},{128,64},{192,128},{256,192},{320,256},{384,320},{448,384},... | collective-permute-start | bytes 638984 | tf_op jit(solution)/shard_map/ppermute | solution.py:422
  18.8 0.9 %copy-start = (f32[15,4,8,128]{3,2,1,0:T(8,128)S(1)}, f32[15,4,8,128]{3,2,1,0:T(8,128)}, u32[]{:S(2)}) copy-start(f32[15,4,8,128]{3,2,1,0:T(8,128)} %get-tuple-element.14.block_in) | copy-start | bytes 737284
  20.1 6.5 %collective-permute-start.2 = (f32[30,8,128]{2,1,0:T(8,128)S(1)}, f32[30,8,128]{2,1,0:T(8,128)S(1)}, u32[]{:S(2)}, u32[]{:S(2)}) collective-permute-start(f32[30,8,128]{2,1,0:T(8,128)S(1)} %get-tuple-element.18), channel_id=1, source_target_pairs={{0,8},{8,16},{16,24},{24,32},{32,40},{40,48},{48,56},{1,9},{9,17},... | collective-permute-start | bytes 368648 | tf_op jit(solution)/shard_map/ppermute | solution.py:422
  24.6 7.1 %collective-permute-start.3 = (f32[30,8,128]{2,1,0:T(8,128)S(1)}, f32[30,8,128]{2,1,0:T(8,128)S(1)}, u32[]{:S(2)}, u32[]{:S(2)}) collective-permute-start(f32[30,8,128]{2,1,0:T(8,128)S(1)} %get-tuple-element.19), channel_id=1, source_target_pairs={{8,0},{16,8},{24,16},{32,24},{40,32},{48,40},{56,48},{9,1},{17,9},... | collective-permute-start | bytes 368648 | tf_op jit(solution)/shard_map/ppermute | solution.py:422
  34.1 7.3 %collective-permute-start.4 = (f32[52,8,128]{2,1,0:T(8,128)S(1)}, f32[52,8,128]{2,1,0:T(8,128)S(1)}, u32[]{:S(2)}, u32[]{:S(2)}) collective-permute-start(f32[52,8,128]{2,1,0:T(8,128)S(1)} %get-tuple-element.20), channel_id=1, source_target_pairs={{0,8},{8,16},{16,24},{24,32},{32,40},{40,48},{48,56},{1,9},{9,17},... | collective-permute-start | bytes 638984 | tf_op jit(solution)/shard_map/ppermute | solution.py:422
  38.6 7.8 %collective-permute-start.5 = (f32[52,8,128]{2,1,0:T(8,128)S(1)}, f32[52,8,128]{2,1,0:T(8,128)S(1)}, u32[]{:S(2)}, u32[]{:S(2)}) collective-permute-start(f32[52,8,128]{2,1,0:T(8,128)S(1)} %get-tuple-element.21), channel_id=1, source_target_pairs={{8,0},{16,8},{24,16},{32,24},{40,32},{48,40},{56,48},{9,1},{17,9},... | collective-permute-start | bytes 638984 | tf_op jit(solution)/shard_map/ppermute | solution.py:422
  46.5 14.0 %collective-permute-start.6 = (f32[15,16,128]{2,1,0:T(8,128)S(1)}, f32[15,16,128]{2,1,0:T(8,128)S(1)}, u32[]{:S(2)}, u32[]{:S(2)}) collective-permute-start(f32[15,16,128]{2,1,0:T(8,128)S(1)} %shard_map.71), channel_id=1, source_target_pairs={{0,1},{1,2},{2,3},{3,4},{4,5},{5,6},{6,7},{8,9},{9,10},{10,11},{11... | collective-permute-start | bytes 368648 | tf_op jit(solution)/shard_map/ppermute | solution.py:422
  56.2 6.2 %collective-permute-start.7 = (f32[15,16,128]{2,1,0:T(8,128)S(1)}, f32[15,16,128]{2,1,0:T(8,128)S(1)}, u32[]{:S(2)}, u32[]{:S(2)}) collective-permute-start(f32[15,16,128]{2,1,0:T(8,128)S(1)} %shard_map.71), channel_id=1, source_target_pairs={{1,0},{2,1},{3,2},{4,3},{5,4},{6,5},{7,6},{9,8},{10,9},{11,10},{12... | collective-permute-start | bytes 368648 | tf_op jit(solution)/shard_map/ppermute | solution.py:422

commit v6 on v5

--- a/solution.py
+++ b/solution.py
@@ -171,19 +171,12 @@
     return [c for c in range(NFLOW) if MOVING[c][0] == sign]
 
 
-def start_kernel(flow_in, species_in, fluid_in, react_in, block_ref, right_ref, left_ref, flow_ref, species_ref, fluid_ref, react_ref, done):
-    pairs = ((flow_in, flow_ref), (species_in, species_ref), (fluid_in, fluid_ref), (react_in, react_ref))
-    copies = [pltpu.make_async_copy(one, two, done.at[k]) for k, (one, two) in enumerate(pairs)]
-    for copy in copies:
-        copy.start()
-    for copy in copies:
-        copy.wait()
+def start_kernel(inputs_ref, block_ref, right_ref, left_ref):
     for x in range(DEEP):
         turn = lax.rem(base_at(DEEP + x) + 8, LANES)
-        fluid = fluid_ref[x].astype(jnp.float32)
-        react = react_ref[x].astype(jnp.float32)
-        flow = [flow_ref[k, x] * fluid for k in range(10)]
-        species = [species_ref[k, x] * fluid for k in range(4)]
+        fluid, react = inputs_ref[14, x], inputs_ref[15, x]
+        flow = [inputs_ref[k, x] * fluid for k in range(10)]
+        species = [inputs_ref[k, x] * fluid for k in range(10, 14)]
         post = collide(flow, species)
         for far, sign, ref in ((0, 1, right_ref), (3, -1, left_ref)):
             if x == far:
@@ -365,41 +358,46 @@
 
 
 def strips_kernel(result_ref, near_ref, far_ref, below_ref, above_ref, flow_out, species_out, dissolved_out, strips):
+    firsts, posts, fars = (4, 0), [], []
     for side, ref in enumerate((below_ref, above_ref)):
-        first = 0 if side else 4
-        place = (lanes_of(TALL) + (LANES - base_at(1) - first)) & (LANES - 1)
+        place = (lanes_of(TALL) + (LANES - base_at(1) - firsts[side])) & (LANES - 1)
         place = place - 12 * ((place * 43) >> 9)
         outside = place >= 8 if side else place < 4
         rho, conc = marked(ref[0], ref[10], ref[FLUID])
-        post = [jnp.where(outside, rho if k == 0 else conc if k == 10 else ref[k], near_ref[side, k]) for k in range(14)]
-        released = jnp.zeros((ROWS, LANES), jnp.float32)
-        for step in range(STEPS):
-            last = step == STEPS - 1
+        marks = {0: rho, 10: conc}
+        posts.append([jnp.where(outside, marks[k] if k in marks else ref[k], near_ref[side, k]) for k in range(14)])
+        for end, x in enumerate((0, 11)):
+            there = within(x, 8, 12, TALL) if side else within(x, 4, 8, TALL)
+            parts = marked_far([ref[7 * end + k] for k in range(7)])
+            fars.append([jnp.where(there, part, far_ref[end, k]) for k, part in enumerate(parts)])
+    released = [jnp.zeros((ROWS, LANES), jnp.float32)] * 2
+    for step in range(STEPS):
+        last = step == STEPS - 1
+        for side in range(2):
+            post = posts[side]
             _, flow_pops = flow_populations(post[:10])
             _, species_pops = species_populations(post[10:])
             arriving = [moved(flow_pops[c], c) for c in range(NFLOW)]
             arriving_species = [moved(species_pops[c], c) for c in range(NSPEC)]
             if step == 0:
                 for end, (x, sign) in enumerate(((0, 1), (11, -1))):
-                    here = within(x + sign, first, first + 12, TALL)
-                    there = within(x, 8, 12, TALL) if side else within(x, 4, 8, TALL)
-                    parts = marked_far([ref[7 * end + k] for k in range(7)])
-                    parts = [jnp.where(there, part, far_ref[end, k]) for k, part in enumerate(parts)]
+                    here = within(x + sign, firsts[side], firsts[side] + 12, TALL)
+                    parts = fars[2 * side + end]
                     for k, c in enumerate(towards(sign)):
                         arriving[c] = jnp.where(here, moved(parts[k], c), arriving[c])
                     c = towards(sign)[0]
                     arriving_species[c] = jnp.where(here, moved(parts[5], c), arriving_species[c])
-            released = released + release(arriving_species)
+            released[side] = released[side] + release(arriving_species)
             if last:
                 post = [value[0:ROWS] for value in post]
                 arriving = [value[0:ROWS] for value in arriving]
                 arriving_species = [value[0:ROWS] for value in arriving_species]
             new_flow, new_species = pass_on(post, arriving, arriving_species)
             if last:
-                for k, value in enumerate(results(post, new_flow, new_species, released)):
+                for k, value in enumerate(results(post, new_flow, new_species, released[side])):
                     strips[side, k] = value
             else:
-                post = next_post(post, new_flow, new_species)
+                posts[side] = next_post(post, new_flow, new_species)
     for own in range(DEEP):
         x = DEEP + own
         low, high = within(x, 8, 12, (ROWS, LANES)), within(x, 4, 8, (ROWS, LANES))
@@ -429,21 +427,16 @@
 def per_device(flow_moments, species_moments, fluid_mask, reactive_mask):
     f32 = jnp.float32
     small = pltpu.CompilerParams(vmem_limit_bytes=16 * 1024 * 1024)
+    masks = [mask.astype(f32)[None] for mask in (fluid_mask, reactive_mask)]
+    inputs = jnp.concatenate([flow_moments, species_moments] + masks)
     half = jax.ShapeDtypeStruct((HALF, ROWS, LANES), f32)
     block, to_right, to_left = pl.pallas_call(
         start_kernel,
         out_shape=(jax.ShapeDtypeStruct((FIELDS, DEEP, ROWS, LANES), f32), half, half),
-        in_specs=[pl.BlockSpec(memory_space=pltpu.HBM)] * 4,
+        in_specs=vmem(1),
         out_specs=tuple(vmem(3)),
-        scratch_shapes=[
-            pltpu.VMEM(flow_moments.shape, f32),
-            pltpu.VMEM(species_moments.shape, f32),
-            pltpu.VMEM(fluid_mask.shape, fluid_mask.dtype),
-            pltpu.VMEM(reactive_mask.shape, reactive_mask.dtype),
-            pltpu.SemaphoreType.DMA((4,)),
-        ],
-        compiler_params=pltpu.CompilerParams(vmem_limit_bytes=56 * 1024 * 1024),
-    )(flow_moments, species_moments, fluid_mask, reactive_mask)
+        compiler_params=small,
+    )(inputs)
     left, right = shifted(to_right, to_left, "gx", True)
     own_tiles = jax.ShapeDtypeStruct((OWN_TILES, ROWS, LANES), f32)
     block, own_to_up, own_to_down = pl.pallas_call(

time: 64.4 us -> 64 us (level)
  Pallas kernels: 6.37 us -> 4.52 us
  other arithmetic: 0 us -> 1.7 us
  local copies, waits for them, and re-layouts: 0.94 us -> 0.06 us
  waiting for transfers between devices: 15.3 us -> 16 us
    pallas_call x1, Pallas kernels: 1.95 us -> 0.16 us  [per_device(): pl.pallas_call(start_kernel, out_shape=(jax.ShapeDtypeStruct((FIELDS, DEE...]
    concatenate x0 -> x1, other arithmetic: none -> 0.93 us  [per_device(): inputs = jnp.concatenate([flow_moments, species_moments] + masks)]
    unnamed x2, local copies, waits for them, and re-layouts: 0.94 us -> 0.06 us
    broadcast_in_dim x0 -> x1, other arithmetic: none -> 0.77 us  [per_device(): masks = [mask.astype(f32)[None] for mask in (fluid_mask, reactive_mask)]]
    ppermute x8, waiting for transfers between devices: 15.3 us -> 16 us  [shifted(): return (lax.ppermute(upward, axis, up), lax.ppermute(downward, axis, down))]
where the time goes in v6:
time: 64 us; the launch traced here: 63.6 us
  starting transfers between devices  40.6 us (63%)
  waiting for transfers between devices  16 us (25%)
  Pallas kernels  4.52 us (7%)
  other arithmetic  1.7 us (3%)
  between operations  0.75 us (1%)
    ppermute x8, starting transfers between devices, shifted(): return (lax.ppermute(upward, axis, up), lax.ppermute(downward, axis, down))  40.6 us
    ppermute x8, waiting for transfers between devices, shifted(): return (lax.ppermute(upward, axis, up), lax.ppermute(downward, axis, down))  16 us
    pallas_call x1, Pallas kernels, per_device(): pl.pallas_call(layers_kernel, out_shape=(jax.ShapeDtypeStruct((15, DEEP,...  2.37 us
    pallas_call x1, Pallas kernels, per_device(): pl.pallas_call(strips_kernel, out_shape=(jax.ShapeDtypeStruct(flow_moment...  1.51 us
  transfers between devices with their start and end apart: 8, of which 6 were waited for; matrix products, arithmetic and copies ran while one was open for 0% of the time, Pallas kernels for 4%

profile of v6, /device:TPU:57, one launch (start us, length us, event | category | flops | bytes accessed | tf_op | source)
XLA Modules:
  0.0 63.6 jit_solution(12875673816894648685)
XLA Ops:
  0.6 0.0 copy-start
  0.6 0.8 %convert_bitcast_fusion = (f32[1,4,8,128]{3,2,1,0:T(8,128)S(1)}, f32[1,4,8,128]{3,2,1,0:T(8,128)S(1)}) fusion(s32[4,8,128]{2,1,0:T(8,128)} %param.7, s32[4,8,128]{2,1,0:T(8,128)} %param.6), kind=kLoop, calls=%fused_computation.1 | loop fusion | flops 8192 | bytes 65536 | tf_op jit(solution)/shard_map/broadcast_in_dim | solution.py:430
  1.4 0.1 copy-done
  1.5 0.9 %pad_maximum_fusion.inputs_ref = f32[16,4,8,128]{3,2,1,0:T(8,128)S(1)} fusion(f32[1,4,8,128]{3,2,1,0:T(8,128)S(1)} %get-tuple-element.25, f32[1,4,8,128]{3,2,1,0:T(8,128)S(1)} %get-tuple-element.26, f32[4,4,8,128]{3,2,1,0:T(8,128)S(1)} %copy-done, f32[10,4,8,128]{3,2,1,0:T(8,128)} %param.4), kind=kLoop, calls=%fused_computation | loop fusion | flops 196608 | bytes 524288 | tf_op jit(solution)/shard_map/concatenate | solution.py:431
  2.4 0.2 shard_map.67
  2.6 14.3 %collective-permute-start = (f32[52,8,128]{2,1,0:T(8,128)S(1)}, f32[52,8,128]{2,1,0:T(8,128)S(1)}, u32[]{:S(2)}, u32[]{:S(2)}) collective-permute-start(f32[52,8,128]{2,1,0:T(8,128)S(1)} %get-tuple-element.16), channel_id=1, source_target_pairs={{0,64},{64,128},{128,192},{192,256},{256,320},{320,384},{384,448},... | collective-permute-start | bytes 638984 | tf_op jit(solution)/shard_map/ppermute | solution.py:420
  16.9 1.9 %collective-permute-start.1 = (f32[52,8,128]{2,1,0:T(8,128)S(1)}, f32[52,8,128]{2,1,0:T(8,128)S(1)}, u32[]{:S(2)}, u32[]{:S(2)}) collective-permute-start(f32[52,8,128]{2,1,0:T(8,128)S(1)} %get-tuple-element.17), channel_id=1, source_target_pairs={{64,0},{128,64},{192,128},{256,192},{320,256},{384,320},{448,384},... | collective-permute-start | bytes 638984 | tf_op jit(solution)/shard_map/ppermute | solution.py:420
  18.8 0.3 shard_map.68
  19.1 4.5 %collective-permute-start.2 = (f32[30,8,128]{2,1,0:T(8,128)S(1)}, f32[30,8,128]{2,1,0:T(8,128)S(1)}, u32[]{:S(2)}, u32[]{:S(2)}) collective-permute-start(f32[30,8,128]{2,1,0:T(8,128)S(1)} %get-tuple-element.18), channel_id=1, source_target_pairs={{0,8},{8,16},{16,24},{24,32},{32,40},{40,48},{48,56},{1,9},{9,17},... | collective-permute-start | bytes 368648 | tf_op jit(solution)/shard_map/ppermute | solution.py:420
  23.7 1.9 %collective-permute-start.3 = (f32[30,8,128]{2,1,0:T(8,128)S(1)}, f32[30,8,128]{2,1,0:T(8,128)S(1)}, u32[]{:S(2)}, u32[]{:S(2)}) collective-permute-start(f32[30,8,128]{2,1,0:T(8,128)S(1)} %get-tuple-element.19), channel_id=1, source_target_pairs={{8,0},{16,8},{24,16},{32,24},{40,32},{48,40},{56,48},{9,1},{17,9},... | collective-permute-start | bytes 368648 | tf_op jit(solution)/shard_map/ppermute | solution.py:420
  25.6 0.0 collective-permute-done.2.own_up
  25.6 5.2 %collective-permute-done.3.own_down = f32[30,8,128]{2,1,0:T(8,128)S(1)} collective-permute-done((f32[30,8,128]{2,1,0:T(8,128)S(1)}, f32[30,8,128]{2,1,0:T(8,128)S(1)}, u32[]{:S(2)}, u32[]{:S(2)}) %collective-permute-start.3) | collective-permute-done | bytes 122912 | tf_op jit(solution)/shard_map/ppermute | solution.py:420
  30.8 1.5 %collective-permute-done.left_ref = f32[52,8,128]{2,1,0:T(8,128)S(1)} collective-permute-done((f32[52,8,128]{2,1,0:T(8,128)S(1)}, f32[52,8,128]{2,1,0:T(8,128)S(1)}, u32[]{:S(2)}, u32[]{:S(2)}) %collective-permute-start) | collective-permute-done | bytes 213024 | tf_op jit(solution)/shard_map/ppermute | solution.py:420
  32.3 1.5 %collective-permute-done.1.right_ref = f32[52,8,128]{2,1,0:T(8,128)S(1)} collective-permute-done((f32[52,8,128]{2,1,0:T(8,128)S(1)}, f32[52,8,128]{2,1,0:T(8,128)S(1)}, u32[]{:S(2)}, u32[]{:S(2)}) %collective-permute-start.1) | collective-permute-done | bytes 213024 | tf_op jit(solution)/shard_map/ppermute | solution.py:420
  33.8 4.5 %collective-permute-start.4 = (f32[52,8,128]{2,1,0:T(8,128)S(1)}, f32[52,8,128]{2,1,0:T(8,128)S(1)}, u32[]{:S(2)}, u32[]{:S(2)}) collective-permute-start(f32[52,8,128]{2,1,0:T(8,128)S(1)} %get-tuple-element.20), channel_id=1, source_target_pairs={{0,8},{8,16},{16,24},{24,32},{32,40},{40,48},{48,56},{1,9},{9,17},... | collective-permute-start | bytes 638984 | tf_op jit(solution)/shard_map/ppermute | solution.py:420
  38.4 1.9 %collective-permute-start.5 = (f32[52,8,128]{2,1,0:T(8,128)S(1)}, f32[52,8,128]{2,1,0:T(8,128)S(1)}, u32[]{:S(2)}, u32[]{:S(2)}) collective-permute-start(f32[52,8,128]{2,1,0:T(8,128)S(1)} %get-tuple-element.21), channel_id=1, source_target_pairs={{8,0},{16,8},{24,16},{32,24},{40,32},{48,40},{56,48},{9,1},{17,9},... | collective-permute-start | bytes 638984 | tf_op jit(solution)/shard_map/ppermute | solution.py:420
  40.3 0.8 %collective-permute-done.4.up_ref = f32[52,8,128]{2,1,0:T(8,128)S(1)} collective-permute-done((f32[52,8,128]{2,1,0:T(8,128)S(1)}, f32[52,8,128]{2,1,0:T(8,128)S(1)}, u32[]{:S(2)}, u32[]{:S(2)}) %collective-permute-start.4) | collective-permute-done | bytes 213024 | tf_op jit(solution)/shard_map/ppermute | solution.py:420
  41.1 5.0 %collective-permute-done.5.down_ref = f32[52,8,128]{2,1,0:T(8,128)S(1)} collective-permute-done((f32[52,8,128]{2,1,0:T(8,128)S(1)}, f32[52,8,128]{2,1,0:T(8,128)S(1)}, u32[]{:S(2)}, u32[]{:S(2)}) %collective-permute-start.5) | collective-permute-done | bytes 213024 | tf_op jit(solution)/shard_map/ppermute | solution.py:420
  46.2 0.1 shard_map.71
  46.3 9.6 %collective-permute-start.6 = (f32[15,16,128]{2,1,0:T(8,128)S(1)}, f32[15,16,128]{2,1,0:T(8,128)S(1)}, u32[]{:S(2)}, u32[]{:S(2)}) collective-permute-start(f32[15,16,128]{2,1,0:T(8,128)S(1)} %shard_map.71), channel_id=1, source_target_pairs={{0,1},{1,2},{2,3},{3,4},{4,5},{5,6},{6,7},{8,9},{9,10},{10,11},{11... | collective-permute-start | bytes 368648 | tf_op jit(solution)/shard_map/ppermute | solution.py:420
  55.9 1.9 %collective-permute-start.7 = (f32[15,16,128]{2,1,0:T(8,128)S(1)}, f32[15,16,128]{2,1,0:T(8,128)S(1)}, u32[]{:S(2)}, u32[]{:S(2)}) collective-permute-start(f32[15,16,128]{2,1,0:T(8,128)S(1)} %shard_map.71), channel_id=1, source_target_pairs={{1,0},{2,1},{3,2},{4,3},{5,4},{6,5},{7,6},{9,8},{10,9},{11,10},{12... | collective-permute-start | bytes 368648 | tf_op jit(solution)/shard_map/ppermute | solution.py:420
  57.8 2.4 %shard_map.70 = (f32[15,4,8,128]{3,2,1,0:T(8,128)S(1)}, f32[2,14,16,128]{3,2,1,0:T(8,128)S(1)}, f32[2,6,16,128]{3,2,1,0:T(8,128)S(1)}) custom-call(f32[15,4,8,128]{3,2,1,0:T(8,128)S(1)} %get-tuple-element.15.own_ref, f32[52,8,128]{2,1,0:T(8,128)S(1)} %collective-permute-done.left_ref, f32[52,8,128]{2,1,0:T(8,128)S(1)} %collective-permute-done.1.right_ref, ...), custom_call_target="tpu_custom_call" | custom-call | flops 10000000 | bytes 10000000 | tf_op jit(solution)/shard_map/pallas_call | solution.py:470
  60.2 0.0 collective-permute-done.6.below_ref
  60.2 1.9 %collective-permute-done.7.above_ref = f32[15,16,128]{2,1,0:T(8,128)S(1)} collective-permute-done((f32[15,16,128]{2,1,0:T(8,128)S(1)}, f32[15,16,128]{2,1,0:T(8,128)S(1)}, u32[]{:S(2)}, u32[]{:S(2)}) %collective-permute-start.7) | collective-permute-done | bytes 122912 | tf_op jit(solution)/shard_map/ppermute | solution.py:420
  62.1 1.5 %shard_map.72 = (f32[10,4,8,128]{3,2,1,0:T(8,128)}, f32[4,4,8,128]{3,2,1,0:T(8,128)}, f32[4,8,128]{2,1,0:T(8,128)}) custom-call(f32[15,4,8,128]{3,2,1,0:T(8,128)S(1)} %get-tuple-element.22.result_ref, f32[2,14,16,128]{3,2,1,0:T(8,128)S(1)} %get-tuple-element.23.near_ref, f32[2,6,16,128]{3,2,1,0:T(8,128)S(1)} %get-tuple-element.24.far_ref, ...), custom_call_target="tpu_custom_call" | custom-call | tf_op jit(solution)/shard_map/pallas_call | solution.py:486
  (1 shorter events, 0.0 us)
Async XLA Ops:
  0.6 0.8 %copy-start = (f32[4,4,8,128]{3,2,1,0:T(8,128)S(1)}, f32[4,4,8,128]{3,2,1,0:T(8,128)}, u32[]{:S(2)}) copy-start(f32[4,4,8,128]{3,2,1,0:T(8,128)} %param.5) | copy-start | bytes 196612
  2.6 29.8 %collective-permute-start = (f32[52,8,128]{2,1,0:T(8,128)S(1)}, f32[52,8,128]{2,1,0:T(8,128)S(1)}, u32[]{:S(2)}, u32[]{:S(2)}) collective-permute-start(f32[52,8,128]{2,1,0:T(8,128)S(1)} %get-tuple-element.16), channel_id=1, source_target_pairs={{0,64},{64,128},{128,192},{192,256},{256,320},{320,384},{384,448},... | collective-permute-start | bytes 638984 | tf_op jit(solution)/shard_map/ppermute | solution.py:420
  16.9 17.0 %collective-permute-start.1 = (f32[52,8,128]{2,1,0:T(8,128)S(1)}, f32[52,8,128]{2,1,0:T(8,128)S(1)}, u32[]{:S(2)}, u32[]{:S(2)}) collective-permute-start(f32[52,8,128]{2,1,0:T(8,128)S(1)} %get-tuple-element.17), channel_id=1, source_target_pairs={{64,0},{128,64},{192,128},{256,192},{320,256},{384,320},{448,384},... | collective-permute-start | bytes 638984 | tf_op jit(solution)/shard_map/ppermute | solution.py:420
  19.1 6.5 %collective-permute-start.2 = (f32[30,8,128]{2,1,0:T(8,128)S(1)}, f32[30,8,128]{2,1,0:T(8,128)S(1)}, u32[]{:S(2)}, u32[]{:S(2)}) collective-permute-start(f32[30,8,128]{2,1,0:T(8,128)S(1)} %get-tuple-element.18), channel_id=1, source_target_pairs={{0,8},{8,16},{16,24},{24,32},{32,40},{40,48},{48,56},{1,9},{9,17},... | collective-permute-start | bytes 368648 | tf_op jit(solution)/shard_map/ppermute | solution.py:420
  23.7 7.1 %collective-permute-start.3 = (f32[30,8,128]{2,1,0:T(8,128)S(1)}, f32[30,8,128]{2,1,0:T(8,128)S(1)}, u32[]{:S(2)}, u32[]{:S(2)}) collective-permute-start(f32[30,8,128]{2,1,0:T(8,128)S(1)} %get-tuple-element.19), channel_id=1, source_target_pairs={{8,0},{16,8},{24,16},{32,24},{40,32},{48,40},{56,48},{9,1},{17,9},... | collective-permute-start | bytes 368648 | tf_op jit(solution)/shard_map/ppermute | solution.py:420
  33.8 7.3 %collective-permute-start.4 = (f32[52,8,128]{2,1,0:T(8,128)S(1)}, f32[52,8,128]{2,1,0:T(8,128)S(1)}, u32[]{:S(2)}, u32[]{:S(2)}) collective-permute-start(f32[52,8,128]{2,1,0:T(8,128)S(1)} %get-tuple-element.20), channel_id=1, source_target_pairs={{0,8},{8,16},{16,24},{24,32},{32,40},{40,48},{48,56},{1,9},{9,17},... | collective-permute-start | bytes 638984 | tf_op jit(solution)/shard_map/ppermute | solution.py:420
  38.4 7.8 %collective-permute-start.5 = (f32[52,8,128]{2,1,0:T(8,128)S(1)}, f32[52,8,128]{2,1,0:T(8,128)S(1)}, u32[]{:S(2)}, u32[]{:S(2)}) collective-permute-start(f32[52,8,128]{2,1,0:T(8,128)S(1)} %get-tuple-element.21), channel_id=1, source_target_pairs={{8,0},{16,8},{24,16},{32,24},{40,32},{48,40},{56,48},{9,1},{17,9},... | collective-permute-start | bytes 638984 | tf_op jit(solution)/shard_map/ppermute | solution.py:420
  46.3 13.9 %collective-permute-start.6 = (f32[15,16,128]{2,1,0:T(8,128)S(1)}, f32[15,16,128]{2,1,0:T(8,128)S(1)}, u32[]{:S(2)}, u32[]{:S(2)}) collective-permute-start(f32[15,16,128]{2,1,0:T(8,128)S(1)} %shard_map.71), channel_id=1, source_target_pairs={{0,1},{1,2},{2,3},{3,4},{4,5},{5,6},{6,7},{8,9},{9,10},{10,11},{11... | collective-permute-start | bytes 368648 | tf_op jit(solution)/shard_map/ppermute | solution.py:420
  55.9 6.2 %collective-permute-start.7 = (f32[15,16,128]{2,1,0:T(8,128)S(1)}, f32[15,16,128]{2,1,0:T(8,128)S(1)}, u32[]{:S(2)}, u32[]{:S(2)}) collective-permute-start(f32[15,16,128]{2,1,0:T(8,128)S(1)} %shard_map.71), channel_id=1, source_target_pairs={{1,0},{2,1},{3,2},{4,3},{5,4},{6,5},{7,6},{9,8},{10,9},{11,10},{12... | collective-permute-start | bytes 368648 | tf_op jit(solution)/shard_map/ppermute | solution.py:420

commit v7 on v6

--- a/solution.py
+++ b/solution.py
@@ -171,12 +171,19 @@
     return [c for c in range(NFLOW) if MOVING[c][0] == sign]
 
 
-def start_kernel(inputs_ref, block_ref, right_ref, left_ref):
+def start_kernel(flow_in, species_in, fluid_in, react_in, block_ref, right_ref, left_ref, flow_ref, species_ref, fluid_ref, react_ref, done):
+    pairs = ((flow_in, flow_ref), (species_in, species_ref), (fluid_in, fluid_ref), (react_in, react_ref))
+    copies = [pltpu.make_async_copy(one, two, done.at[k]) for k, (one, two) in enumerate(pairs)]
+    for copy in copies:
+        copy.start()
+    for copy in copies:
+        copy.wait()
     for x in range(DEEP):
         turn = lax.rem(base_at(DEEP + x) + 8, LANES)
-        fluid, react = inputs_ref[14, x], inputs_ref[15, x]
-        flow = [inputs_ref[k, x] * fluid for k in range(10)]
-        species = [inputs_ref[k, x] * fluid for k in range(10, 14)]
+        fluid = fluid_ref[x].astype(jnp.float32)
+        react = react_ref[x].astype(jnp.float32)
+        flow = [flow_ref[k, x] * fluid for k in range(10)]
+        species = [species_ref[k, x] * fluid for k in range(4)]
         post = collide(flow, species)
         for far, sign, ref in ((0, 1, right_ref), (3, -1, left_ref)):
             if x == far:
@@ -427,16 +434,21 @@
 def per_device(flow_moments, species_moments, fluid_mask, reactive_mask):
     f32 = jnp.float32
     small = pltpu.CompilerParams(vmem_limit_bytes=16 * 1024 * 1024)
-    masks = [mask.astype(f32)[None] for mask in (fluid_mask, reactive_mask)]
-    inputs = jnp.concatenate([flow_moments, species_moments] + masks)
     half = jax.ShapeDtypeStruct((HALF, ROWS, LANES), f32)
     block, to_right, to_left = pl.pallas_call(
         start_kernel,
         out_shape=(jax.ShapeDtypeStruct((FIELDS, DEEP, ROWS, LANES), f32), half, half),
-        in_specs=vmem(1),
+        in_specs=[pl.BlockSpec(memory_space=pltpu.HBM)] * 4,
         out_specs=tuple(vmem(3)),
+        scratch_shapes=[
+            pltpu.VMEM(flow_moments.shape, f32),
+            pltpu.VMEM(species_moments.shape, f32),
+            pltpu.VMEM(fluid_mask.shape, fluid_mask.dtype),
+            pltpu.VMEM(reactive_mask.shape, reactive_mask.dtype),
+            pltpu.SemaphoreType.DMA((4,)),
+        ],
         compiler_params=small,
-    )(inputs)
+    )(*[pltpu.with_memory_space_constraint(value, pltpu.HBM) for value in (flow_moments, species_moments, fluid_mask, reactive_mask)])
     left, right = shifted(to_right, to_left, "gx", True)
     own_tiles = jax.ShapeDtypeStruct((OWN_TILES, ROWS, LANES), f32)
     block, own_to_up, own_to_down = pl.pallas_call(

time: 64 us -> 63.1 us (0.986)
  other arithmetic: 1.7 us -> 0 us
  Pallas kernels: 4.52 us -> 5.47 us
    pallas_call x1, Pallas kernels: 0.16 us -> 1.12 us  [per_device(): pl.pallas_call(start_kernel, out_shape=(jax.ShapeDtypeStruct((FIELDS, DEE...]
    concatenate x1 -> x0, other arithmetic: 0.93 us -> none  [per_device(): inputs = jnp.concatenate([flow_moments, species_moments] + masks)]
    broadcast_in_dim x1 -> x0, other arithmetic: 0.77 us -> none  [per_device(): masks = [mask.astype(f32)[None] for mask in (fluid_mask, reactive_mask)]]
where the time goes in v7:
time: 63.1 us; the launch traced here: 62.8 us
  starting transfers between devices  40.6 us (64%)
  waiting for transfers between devices  16 us (25%)
  Pallas kernels  5.47 us (9%)
  between operations  0.74 us (1%)
    ppermute x8, starting transfers between devices, shifted(): return (lax.ppermute(upward, axis, up), lax.ppermute(downward, axis, down))  40.6 us
    ppermute x8, waiting for transfers between devices, shifted(): return (lax.ppermute(upward, axis, up), lax.ppermute(downward, axis, down))  16 us
    pallas_call x1, Pallas kernels, per_device(): pl.pallas_call(layers_kernel, out_shape=(jax.ShapeDtypeStruct((15, DEEP,...  2.37 us
    pallas_call x1, Pallas kernels, per_device(): pl.pallas_call(strips_kernel, out_shape=(jax.ShapeDtypeStruct(flow_moment...  1.51 us
  transfers between devices with their start and end apart: 8, of which 6 were waited for; matrix products, arithmetic and copies ran while one was open for 0% of the time, Pallas kernels for 4%

profile of v7, /device:TPU:57, one launch (start us, length us, event | category | flops | bytes accessed | tf_op | source)
XLA Modules:
  0.0 62.8 jit_solution(9368965665566830225)
XLA Ops:
  0.6 1.1 %shard_map.67 = (f32[15,4,8,128]{3,2,1,0:T(8,128)S(1)}, f32[52,8,128]{2,1,0:T(8,128)S(1)}, f32[52,8,128]{2,1,0:T(8,128)S(1)}) custom-call(f32[10,4,8,128]{3,2,1,0:T(8,128)} %flow_in.1, f32[4,4,8,128]{3,2,1,0:T(8,128)} %species_in.1, s32[4,8,128]{2,1,0:T(8,128)} %fluid_in.1, s32[4,8,128]{2,1,0:T(8,128)} %react_in.1), custom_call_target="tpu_custom_call" | custom-call | tf_op jit(solution)/shard_map/pallas_call | solution.py:438
  1.8 14.3 %collective-permute-start = (f32[52,8,128]{2,1,0:T(8,128)S(1)}, f32[52,8,128]{2,1,0:T(8,128)S(1)}, u32[]{:S(2)}, u32[]{:S(2)}) collective-permute-start(f32[52,8,128]{2,1,0:T(8,128)S(1)} %get-tuple-element.16), channel_id=1, source_target_pairs={{0,64},{64,128},{128,192},{192,256},{256,320},{320,384},{384,448},... | collective-permute-start | bytes 638984 | tf_op jit(solution)/shard_map/ppermute | solution.py:427
  16.0 1.9 %collective-permute-start.1 = (f32[52,8,128]{2,1,0:T(8,128)S(1)}, f32[52,8,128]{2,1,0:T(8,128)S(1)}, u32[]{:S(2)}, u32[]{:S(2)}) collective-permute-start(f32[52,8,128]{2,1,0:T(8,128)S(1)} %get-tuple-element.17), channel_id=1, source_target_pairs={{64,0},{128,64},{192,128},{256,192},{320,256},{384,320},{448,384},... | collective-permute-start | bytes 638984 | tf_op jit(solution)/shard_map/ppermute | solution.py:427
  18.0 0.3 shard_map.68
  18.3 4.5 %collective-permute-start.2 = (f32[30,8,128]{2,1,0:T(8,128)S(1)}, f32[30,8,128]{2,1,0:T(8,128)S(1)}, u32[]{:S(2)}, u32[]{:S(2)}) collective-permute-start(f32[30,8,128]{2,1,0:T(8,128)S(1)} %get-tuple-element.18), channel_id=1, source_target_pairs={{0,8},{8,16},{16,24},{24,32},{32,40},{40,48},{48,56},{1,9},{9,17},... | collective-permute-start | bytes 368648 | tf_op jit(solution)/shard_map/ppermute | solution.py:427
  22.9 1.9 %collective-permute-start.3 = (f32[30,8,128]{2,1,0:T(8,128)S(1)}, f32[30,8,128]{2,1,0:T(8,128)S(1)}, u32[]{:S(2)}, u32[]{:S(2)}) collective-permute-start(f32[30,8,128]{2,1,0:T(8,128)S(1)} %get-tuple-element.19), channel_id=1, source_target_pairs={{8,0},{16,8},{24,16},{32,24},{40,32},{48,40},{56,48},{9,1},{17,9},... | collective-permute-start | bytes 368648 | tf_op jit(solution)/shard_map/ppermute | solution.py:427
  24.8 0.0 collective-permute-done.2.own_up
  24.8 5.2 %collective-permute-done.3.own_down = f32[30,8,128]{2,1,0:T(8,128)S(1)} collective-permute-done((f32[30,8,128]{2,1,0:T(8,128)S(1)}, f32[30,8,128]{2,1,0:T(8,128)S(1)}, u32[]{:S(2)}, u32[]{:S(2)}) %collective-permute-start.3) | collective-permute-done | bytes 122912 | tf_op jit(solution)/shard_map/ppermute | solution.py:427
  30.0 1.5 %collective-permute-done.left_ref = f32[52,8,128]{2,1,0:T(8,128)S(1)} collective-permute-done((f32[52,8,128]{2,1,0:T(8,128)S(1)}, f32[52,8,128]{2,1,0:T(8,128)S(1)}, u32[]{:S(2)}, u32[]{:S(2)}) %collective-permute-start) | collective-permute-done | bytes 213024 | tf_op jit(solution)/shard_map/ppermute | solution.py:427
  31.5 1.5 %collective-permute-done.1.right_ref = f32[52,8,128]{2,1,0:T(8,128)S(1)} collective-permute-done((f32[52,8,128]{2,1,0:T(8,128)S(1)}, f32[52,8,128]{2,1,0:T(8,128)S(1)}, u32[]{:S(2)}, u32[]{:S(2)}) %collective-permute-start.1) | collective-permute-done | bytes 213024 | tf_op jit(solution)/shard_map/ppermute | solution.py:427
  33.0 4.5 %collective-permute-start.4 = (f32[52,8,128]{2,1,0:T(8,128)S(1)}, f32[52,8,128]{2,1,0:T(8,128)S(1)}, u32[]{:S(2)}, u32[]{:S(2)}) collective-permute-start(f32[52,8,128]{2,1,0:T(8,128)S(1)} %get-tuple-element.20), channel_id=1, source_target_pairs={{0,8},{8,16},{16,24},{24,32},{32,40},{40,48},{48,56},{1,9},{9,17},... | collective-permute-start | bytes 638984 | tf_op jit(solution)/shard_map/ppermute | solution.py:427
  37.6 1.9 %collective-permute-start.5 = (f32[52,8,128]{2,1,0:T(8,128)S(1)}, f32[52,8,128]{2,1,0:T(8,128)S(1)}, u32[]{:S(2)}, u32[]{:S(2)}) collective-permute-start(f32[52,8,128]{2,1,0:T(8,128)S(1)} %get-tuple-element.21), channel_id=1, source_target_pairs={{8,0},{16,8},{24,16},{32,24},{40,32},{48,40},{56,48},{9,1},{17,9},... | collective-permute-start | bytes 638984 | tf_op jit(solution)/shard_map/ppermute | solution.py:427
  39.5 0.8 %collective-permute-done.4.up_ref = f32[52,8,128]{2,1,0:T(8,128)S(1)} collective-permute-done((f32[52,8,128]{2,1,0:T(8,128)S(1)}, f32[52,8,128]{2,1,0:T(8,128)S(1)}, u32[]{:S(2)}, u32[]{:S(2)}) %collective-permute-start.4) | collective-permute-done | bytes 213024 | tf_op jit(solution)/shard_map/ppermute | solution.py:427
  40.3 5.0 %collective-permute-done.5.down_ref = f32[52,8,128]{2,1,0:T(8,128)S(1)} collective-permute-done((f32[52,8,128]{2,1,0:T(8,128)S(1)}, f32[52,8,128]{2,1,0:T(8,128)S(1)}, u32[]{:S(2)}, u32[]{:S(2)}) %collective-permute-start.5) | collective-permute-done | bytes 213024 | tf_op jit(solution)/shard_map/ppermute | solution.py:427
  45.4 0.1 shard_map.71
  45.5 9.6 %collective-permute-start.6 = (f32[15,16,128]{2,1,0:T(8,128)S(1)}, f32[15,16,128]{2,1,0:T(8,128)S(1)}, u32[]{:S(2)}, u32[]{:S(2)}) collective-permute-start(f32[15,16,128]{2,1,0:T(8,128)S(1)} %shard_map.71), channel_id=1, source_target_pairs={{0,1},{1,2},{2,3},{3,4},{4,5},{5,6},{6,7},{8,9},{9,10},{10,11},{11... | collective-permute-start | bytes 368648 | tf_op jit(solution)/shard_map/ppermute | solution.py:427
  55.1 1.9 %collective-permute-start.7 = (f32[15,16,128]{2,1,0:T(8,128)S(1)}, f32[15,16,128]{2,1,0:T(8,128)S(1)}, u32[]{:S(2)}, u32[]{:S(2)}) collective-permute-start(f32[15,16,128]{2,1,0:T(8,128)S(1)} %shard_map.71), channel_id=1, source_target_pairs={{1,0},{2,1},{3,2},{4,3},{5,4},{6,5},{7,6},{9,8},{10,9},{11,10},{12... | collective-permute-start | bytes 368648 | tf_op jit(solution)/shard_map/ppermute | solution.py:427
  57.0 2.4 %shard_map.70 = (f32[15,4,8,128]{3,2,1,0:T(8,128)S(1)}, f32[2,14,16,128]{3,2,1,0:T(8,128)S(1)}, f32[2,6,16,128]{3,2,1,0:T(8,128)S(1)}) custom-call(f32[15,4,8,128]{3,2,1,0:T(8,128)S(1)} %get-tuple-element.15.own_ref, f32[52,8,128]{2,1,0:T(8,128)S(1)} %collective-permute-done.left_ref, f32[52,8,128]{2,1,0:T(8,128)S(1)} %collective-permute-done.1.right_ref, ...), custom_call_target="tpu_custom_call" | custom-call | flops 10000000 | bytes 10000000 | tf_op jit(solution)/shard_map/pallas_call | solution.py:482
  59.4 0.0 collective-permute-done.6.below_ref
  59.4 1.9 %collective-permute-done.7.above_ref = f32[15,16,128]{2,1,0:T(8,128)S(1)} collective-permute-done((f32[15,16,128]{2,1,0:T(8,128)S(1)}, f32[15,16,128]{2,1,0:T(8,128)S(1)}, u32[]{:S(2)}, u32[]{:S(2)}) %collective-permute-start.7) | collective-permute-done | bytes 122912 | tf_op jit(solution)/shard_map/ppermute | solution.py:427
  61.3 1.5 %shard_map.72 = (f32[10,4,8,128]{3,2,1,0:T(8,128)}, f32[4,4,8,128]{3,2,1,0:T(8,128)}, f32[4,8,128]{2,1,0:T(8,128)}) custom-call(f32[15,4,8,128]{3,2,1,0:T(8,128)S(1)} %get-tuple-element.22.result_ref, f32[2,14,16,128]{3,2,1,0:T(8,128)S(1)} %get-tuple-element.23.near_ref, f32[2,6,16,128]{3,2,1,0:T(8,128)S(1)} %get-tuple-element.24.far_ref, ...), custom_call_target="tpu_custom_call" | custom-call | tf_op jit(solution)/shard_map/pallas_call | solution.py:498
  (1 shorter events, 0.0 us)
Async XLA Ops:
  1.8 29.8 %collective-permute-start = (f32[52,8,128]{2,1,0:T(8,128)S(1)}, f32[52,8,128]{2,1,0:T(8,128)S(1)}, u32[]{:S(2)}, u32[]{:S(2)}) collective-permute-start(f32[52,8,128]{2,1,0:T(8,128)S(1)} %get-tuple-element.16), channel_id=1, source_target_pairs={{0,64},{64,128},{128,192},{192,256},{256,320},{320,384},{384,448},... | collective-permute-start | bytes 638984 | tf_op jit(solution)/shard_map/ppermute | solution.py:427
  16.0 17.0 %collective-permute-start.1 = (f32[52,8,128]{2,1,0:T(8,128)S(1)}, f32[52,8,128]{2,1,0:T(8,128)S(1)}, u32[]{:S(2)}, u32[]{:S(2)}) collective-permute-start(f32[52,8,128]{2,1,0:T(8,128)S(1)} %get-tuple-element.17), channel_id=1, source_target_pairs={{64,0},{128,64},{192,128},{256,192},{320,256},{384,320},{448,384},... | collective-permute-start | bytes 638984 | tf_op jit(solution)/shard_map/ppermute | solution.py:427
  18.3 6.5 %collective-permute-start.2 = (f32[30,8,128]{2,1,0:T(8,128)S(1)}, f32[30,8,128]{2,1,0:T(8,128)S(1)}, u32[]{:S(2)}, u32[]{:S(2)}) collective-permute-start(f32[30,8,128]{2,1,0:T(8,128)S(1)} %get-tuple-element.18), channel_id=1, source_target_pairs={{0,8},{8,16},{16,24},{24,32},{32,40},{40,48},{48,56},{1,9},{9,17},... | collective-permute-start | bytes 368648 | tf_op jit(solution)/shard_map/ppermute | solution.py:427
  22.9 7.1 %collective-permute-start.3 = (f32[30,8,128]{2,1,0:T(8,128)S(1)}, f32[30,8,128]{2,1,0:T(8,128)S(1)}, u32[]{:S(2)}, u32[]{:S(2)}) collective-permute-start(f32[30,8,128]{2,1,0:T(8,128)S(1)} %get-tuple-element.19), channel_id=1, source_target_pairs={{8,0},{16,8},{24,16},{32,24},{40,32},{48,40},{56,48},{9,1},{17,9},... | collective-permute-start | bytes 368648 | tf_op jit(solution)/shard_map/ppermute | solution.py:427
  33.0 7.3 %collective-permute-start.4 = (f32[52,8,128]{2,1,0:T(8,128)S(1)}, f32[52,8,128]{2,1,0:T(8,128)S(1)}, u32[]{:S(2)}, u32[]{:S(2)}) collective-permute-start(f32[52,8,128]{2,1,0:T(8,128)S(1)} %get-tuple-element.20), channel_id=1, source_target_pairs={{0,8},{8,16},{16,24},{24,32},{32,40},{40,48},{48,56},{1,9},{9,17},... | collective-permute-start | bytes 638984 | tf_op jit(solution)/shard_map/ppermute | solution.py:427
  37.6 7.8 %collective-permute-start.5 = (f32[52,8,128]{2,1,0:T(8,128)S(1)}, f32[52,8,128]{2,1,0:T(8,128)S(1)}, u32[]{:S(2)}, u32[]{:S(2)}) collective-permute-start(f32[52,8,128]{2,1,0:T(8,128)S(1)} %get-tuple-element.21), channel_id=1, source_target_pairs={{8,0},{16,8},{24,16},{32,24},{40,32},{48,40},{56,48},{9,1},{17,9},... | collective-permute-start | bytes 638984 | tf_op jit(solution)/shard_map/ppermute | solution.py:427
  45.5 13.9 %collective-permute-start.6 = (f32[15,16,128]{2,1,0:T(8,128)S(1)}, f32[15,16,128]{2,1,0:T(8,128)S(1)}, u32[]{:S(2)}, u32[]{:S(2)}) collective-permute-start(f32[15,16,128]{2,1,0:T(8,128)S(1)} %shard_map.71), channel_id=1, source_target_pairs={{0,1},{1,2},{2,3},{3,4},{4,5},{5,6},{6,7},{8,9},{9,10},{10,11},{11... | collective-permute-start | bytes 368648 | tf_op jit(solution)/shard_map/ppermute | solution.py:427
  55.1 6.2 %collective-permute-start.7 = (f32[15,16,128]{2,1,0:T(8,128)S(1)}, f32[15,16,128]{2,1,0:T(8,128)S(1)}, u32[]{:S(2)}, u32[]{:S(2)}) collective-permute-start(f32[15,16,128]{2,1,0:T(8,128)S(1)} %shard_map.71), channel_id=1, source_target_pairs={{1,0},{2,1},{3,2},{4,3},{5,4},{6,5},{7,6},{9,8},{10,9},{11,10},{12... | collective-permute-start | bytes 368648 | tf_op jit(solution)/shard_map/ppermute | solution.py:427

commit v8 on v7

--- a/solution.py
+++ b/solution.py
@@ -364,7 +364,7 @@
                     state[k, x] = value
 
 
-def strips_kernel(result_ref, near_ref, far_ref, below_ref, above_ref, flow_out, species_out, dissolved_out, strips):
+def strips_kernel(result_ref, near_ref, far_ref, above_ref, below_ref, flow_out, species_out, dissolved_out, strips):
     firsts, posts, fars = (4, 0), [], []
     for side, ref in enumerate((below_ref, above_ref)):
         place = (lanes_of(TALL) + (LANES - base_at(1) - firsts[side])) & (LANES - 1)
@@ -424,7 +424,8 @@
     count = lax.axis_size(axis)
     up = [(i, (i + 1) % count) for i in range(count if wrap else count - 1)]
     down = [(j, i) for i, j in up]
-    return lax.ppermute(upward, axis, up), lax.ppermute(downward, axis, down)
+    after = lax.ppermute(downward, axis, down)
+    return lax.ppermute(upward, axis, up), after
 
 
 def vmem(count):
@@ -506,7 +507,7 @@
         out_specs=tuple(vmem(3)),
         scratch_shapes=[pltpu.VMEM((2, 15, ROWS, LANES), f32)],
         compiler_params=small,
-    )(result, near, far, below, above)
+    )(result, near, far, above, below)
 
 
 def solution(mesh):

time: 63.1 us -> 61.3 us (0.971)
  waiting for transfers between devices: 16 us -> 14.1 us
    ppermute x8, waiting for transfers between devices: 16 us -> 14.1 us  [the longest x4 11.7 us: shifted(): after = lax.ppermute(downward, axis, down)]
  transfers between devices with their start and end apart: 8 -> 8, of which waited for: 6 -> 5; matrix products, arithmetic and copies ran while one was open for 0% -> 0% of each run, Pallas kernels for 4% -> 4%
where the time goes in v8:
time: 61.3 us; the launch traced here: 60.9 us
  starting transfers between devices  40.6 us (66%)
  waiting for transfers between devices  14.1 us (23%)
  Pallas kernels  5.48 us (9%)
  between operations  0.75 us (1%)
    ppermute x4, starting transfers between devices, shifted(): return (lax.ppermute(upward, axis, up), after)  29.3 us
    ppermute x4, waiting for transfers between devices, shifted(): after = lax.ppermute(downward, axis, down)  11.7 us
    ppermute x4, starting transfers between devices, shifted(): after = lax.ppermute(downward, axis, down)  11.3 us
    ppermute x4, waiting for transfers between devices, shifted(): return (lax.ppermute(upward, axis, up), after)  2.38 us
    pallas_call x1, Pallas kernels, per_device(): pl.pallas_call(layers_kernel, out_shape=(jax.ShapeDtypeStruct((15, DEEP,...  2.37 us
    pallas_call x1, Pallas kernels, per_device(): pl.pallas_call(strips_kernel, out_shape=(jax.ShapeDtypeStruct(flow_moment...  1.51 us
  transfers between devices with their start and end apart: 8, of which 5 were waited for; matrix products, arithmetic and copies ran while one was open for 0% of the time, Pallas kernels for 4%

profile of v8, /device:TPU:57, one launch (start us, length us, event | category | flops | bytes accessed | tf_op | source)
XLA Modules:
  0.0 60.9 jit_solution(1560613196792223805)
XLA Ops:
  0.6 1.1 %shard_map.67 = (f32[15,4,8,128]{3,2,1,0:T(8,128)S(1)}, f32[52,8,128]{2,1,0:T(8,128)S(1)}, f32[52,8,128]{2,1,0:T(8,128)S(1)}) custom-call(f32[10,4,8,128]{3,2,1,0:T(8,128)} %flow_in.1, f32[4,4,8,128]{3,2,1,0:T(8,128)} %species_in.1, s32[4,8,128]{2,1,0:T(8,128)} %fluid_in.1, s32[4,8,128]{2,1,0:T(8,128)} %react_in.1), custom_call_target="tpu_custom_call" | custom-call | tf_op jit(solution)/shard_map/pallas_call | solution.py:439
  1.8 14.3 %collective-permute-start = (f32[52,8,128]{2,1,0:T(8,128)S(1)}, f32[52,8,128]{2,1,0:T(8,128)S(1)}, u32[]{:S(2)}, u32[]{:S(2)}) collective-permute-start(f32[52,8,128]{2,1,0:T(8,128)S(1)} %get-tuple-element.16), channel_id=1, source_target_pairs={{0,64},{64,128},{128,192},{192,256},{256,320},{320,384},{384,448},... | collective-permute-start | bytes 638984 | tf_op jit(solution)/shard_map/ppermute | solution.py:428
  16.0 1.9 %collective-permute-start.1 = (f32[52,8,128]{2,1,0:T(8,128)S(1)}, f32[52,8,128]{2,1,0:T(8,128)S(1)}, u32[]{:S(2)}, u32[]{:S(2)}) collective-permute-start(f32[52,8,128]{2,1,0:T(8,128)S(1)} %get-tuple-element.17), channel_id=1, source_target_pairs={{64,0},{128,64},{192,128},{256,192},{320,256},{384,320},{448,384},... | collective-permute-start | bytes 638984 | tf_op jit(solution)/shard_map/ppermute | solution.py:427
  18.0 0.3 shard_map.68
  18.3 4.5 %collective-permute-start.2 = (f32[30,8,128]{2,1,0:T(8,128)S(1)}, f32[30,8,128]{2,1,0:T(8,128)S(1)}, u32[]{:S(2)}, u32[]{:S(2)}) collective-permute-start(f32[30,8,128]{2,1,0:T(8,128)S(1)} %get-tuple-element.18), channel_id=1, source_target_pairs={{0,8},{8,16},{16,24},{24,32},{32,40},{40,48},{48,56},{1,9},{9,17},... | collective-permute-start | bytes 368648 | tf_op jit(solution)/shard_map/ppermute | solution.py:428
  22.9 1.9 %collective-permute-start.3 = (f32[30,8,128]{2,1,0:T(8,128)S(1)}, f32[30,8,128]{2,1,0:T(8,128)S(1)}, u32[]{:S(2)}, u32[]{:S(2)}) collective-permute-start(f32[30,8,128]{2,1,0:T(8,128)S(1)} %get-tuple-element.19), channel_id=1, source_target_pairs={{8,0},{16,8},{24,16},{32,24},{40,32},{48,40},{56,48},{9,1},{17,9},... | collective-permute-start | bytes 368648 | tf_op jit(solution)/shard_map/ppermute | solution.py:427
  24.8 0.0 collective-permute-done.2.own_up
  24.8 5.2 %collective-permute-done.3.own_down = f32[30,8,128]{2,1,0:T(8,128)S(1)} collective-permute-done((f32[30,8,128]{2,1,0:T(8,128)S(1)}, f32[30,8,128]{2,1,0:T(8,128)S(1)}, u32[]{:S(2)}, u32[]{:S(2)}) %collective-permute-start.3) | collective-permute-done | bytes 122912 | tf_op jit(solution)/shard_map/ppermute | solution.py:427
  30.0 1.5 %collective-permute-done.left_ref = f32[52,8,128]{2,1,0:T(8,128)S(1)} collective-permute-done((f32[52,8,128]{2,1,0:T(8,128)S(1)}, f32[52,8,128]{2,1,0:T(8,128)S(1)}, u32[]{:S(2)}, u32[]{:S(2)}) %collective-permute-start) | collective-permute-done | bytes 213024 | tf_op jit(solution)/shard_map/ppermute | solution.py:428
  31.5 1.5 %collective-permute-done.1.right_ref = f32[52,8,128]{2,1,0:T(8,128)S(1)} collective-permute-done((f32[52,8,128]{2,1,0:T(8,128)S(1)}, f32[52,8,128]{2,1,0:T(8,128)S(1)}, u32[]{:S(2)}, u32[]{:S(2)}) %collective-permute-start.1) | collective-permute-done | bytes 213024 | tf_op jit(solution)/shard_map/ppermute | solution.py:427
  33.0 4.5 %collective-permute-start.4 = (f32[52,8,128]{2,1,0:T(8,128)S(1)}, f32[52,8,128]{2,1,0:T(8,128)S(1)}, u32[]{:S(2)}, u32[]{:S(2)}) collective-permute-start(f32[52,8,128]{2,1,0:T(8,128)S(1)} %get-tuple-element.20), channel_id=1, source_target_pairs={{0,8},{8,16},{16,24},{24,32},{32,40},{40,48},{48,56},{1,9},{9,17},... | collective-permute-start | bytes 638984 | tf_op jit(solution)/shard_map/ppermute | solution.py:428
  37.6 1.9 %collective-permute-start.5 = (f32[52,8,128]{2,1,0:T(8,128)S(1)}, f32[52,8,128]{2,1,0:T(8,128)S(1)}, u32[]{:S(2)}, u32[]{:S(2)}) collective-permute-start(f32[52,8,128]{2,1,0:T(8,128)S(1)} %get-tuple-element.21), channel_id=1, source_target_pairs={{8,0},{16,8},{24,16},{32,24},{40,32},{48,40},{56,48},{9,1},{17,9},... | collective-permute-start | bytes 638984 | tf_op jit(solution)/shard_map/ppermute | solution.py:427
  39.5 0.8 %collective-permute-done.4.up_ref = f32[52,8,128]{2,1,0:T(8,128)S(1)} collective-permute-done((f32[52,8,128]{2,1,0:T(8,128)S(1)}, f32[52,8,128]{2,1,0:T(8,128)S(1)}, u32[]{:S(2)}, u32[]{:S(2)}) %collective-permute-start.4) | collective-permute-done | bytes 213024 | tf_op jit(solution)/shard_map/ppermute | solution.py:428
  40.3 5.0 %collective-permute-done.5.down_ref = f32[52,8,128]{2,1,0:T(8,128)S(1)} collective-permute-done((f32[52,8,128]{2,1,0:T(8,128)S(1)}, f32[52,8,128]{2,1,0:T(8,128)S(1)}, u32[]{:S(2)}, u32[]{:S(2)}) %collective-permute-start.5) | collective-permute-done | bytes 213024 | tf_op jit(solution)/shard_map/ppermute | solution.py:427
  45.4 0.1 shard_map.71
  45.5 5.6 %collective-permute-start.6 = (f32[15,16,128]{2,1,0:T(8,128)S(1)}, f32[15,16,128]{2,1,0:T(8,128)S(1)}, u32[]{:S(2)}, u32[]{:S(2)}) collective-permute-start(f32[15,16,128]{2,1,0:T(8,128)S(1)} %shard_map.71), channel_id=1, source_target_pairs={{1,0},{2,1},{3,2},{4,3},{5,4},{6,5},{7,6},{9,8},{10,9},{11,10},{12... | collective-permute-start | bytes 368648 | tf_op jit(solution)/shard_map/ppermute | solution.py:427
  51.0 5.9 %collective-permute-start.7 = (f32[15,16,128]{2,1,0:T(8,128)S(1)}, f32[15,16,128]{2,1,0:T(8,128)S(1)}, u32[]{:S(2)}, u32[]{:S(2)}) collective-permute-start(f32[15,16,128]{2,1,0:T(8,128)S(1)} %shard_map.71), channel_id=1, source_target_pairs={{0,1},{1,2},{2,3},{3,4},{4,5},{5,6},{6,7},{8,9},{9,10},{10,11},{11... | collective-permute-start | bytes 368648 | tf_op jit(solution)/shard_map/ppermute | solution.py:428
  57.0 2.4 %shard_map.70 = (f32[15,4,8,128]{3,2,1,0:T(8,128)S(1)}, f32[2,14,16,128]{3,2,1,0:T(8,128)S(1)}, f32[2,6,16,128]{3,2,1,0:T(8,128)S(1)}) custom-call(f32[15,4,8,128]{3,2,1,0:T(8,128)S(1)} %get-tuple-element.15.own_ref, f32[52,8,128]{2,1,0:T(8,128)S(1)} %collective-permute-done.left_ref, f32[52,8,128]{2,1,0:T(8,128)S(1)} %collective-permute-done.1.right_ref, ...), custom_call_target="tpu_custom_call" | custom-call | flops 10000000 | bytes 10000000 | tf_op jit(solution)/shard_map/pallas_call | solution.py:483
  59.4 0.0 collective-permute-done.6.above_ref
  59.4 0.0 collective-permute-done.7.below_ref
  59.4 1.5 %shard_map.72 = (f32[10,4,8,128]{3,2,1,0:T(8,128)}, f32[4,4,8,128]{3,2,1,0:T(8,128)}, f32[4,8,128]{2,1,0:T(8,128)}) custom-call(f32[15,4,8,128]{3,2,1,0:T(8,128)S(1)} %get-tuple-element.22.result_ref, f32[2,14,16,128]{3,2,1,0:T(8,128)S(1)} %get-tuple-element.23.near_ref, f32[2,6,16,128]{3,2,1,0:T(8,128)S(1)} %get-tuple-element.24.far_ref, ...), custom_call_target="tpu_custom_call" | custom-call | tf_op jit(solution)/shard_map/pallas_call | solution.py:499
  (1 shorter events, 0.0 us)
Async XLA Ops:
  1.8 29.8 %collective-permute-start = (f32[52,8,128]{2,1,0:T(8,128)S(1)}, f32[52,8,128]{2,1,0:T(8,128)S(1)}, u32[]{:S(2)}, u32[]{:S(2)}) collective-permute-start(f32[52,8,128]{2,1,0:T(8,128)S(1)} %get-tuple-element.16), channel_id=1, source_target_pairs={{0,64},{64,128},{128,192},{192,256},{256,320},{320,384},{384,448},... | collective-permute-start | bytes 638984 | tf_op jit(solution)/shard_map/ppermute | solution.py:428
  16.0 17.0 %collective-permute-start.1 = (f32[52,8,128]{2,1,0:T(8,128)S(1)}, f32[52,8,128]{2,1,0:T(8,128)S(1)}, u32[]{:S(2)}, u32[]{:S(2)}) collective-permute-start(f32[52,8,128]{2,1,0:T(8,128)S(1)} %get-tuple-element.17), channel_id=1, source_target_pairs={{64,0},{128,64},{192,128},{256,192},{320,256},{384,320},{448,384},... | collective-permute-start | bytes 638984 | tf_op jit(solution)/shard_map/ppermute | solution.py:427
  18.3 6.5 %collective-permute-start.2 = (f32[30,8,128]{2,1,0:T(8,128)S(1)}, f32[30,8,128]{2,1,0:T(8,128)S(1)}, u32[]{:S(2)}, u32[]{:S(2)}) collective-permute-start(f32[30,8,128]{2,1,0:T(8,128)S(1)} %get-tuple-element.18), channel_id=1, source_target_pairs={{0,8},{8,16},{16,24},{24,32},{32,40},{40,48},{48,56},{1,9},{9,17},... | collective-permute-start | bytes 368648 | tf_op jit(solution)/shard_map/ppermute | solution.py:428
  22.9 7.1 %collective-permute-start.3 = (f32[30,8,128]{2,1,0:T(8,128)S(1)}, f32[30,8,128]{2,1,0:T(8,128)S(1)}, u32[]{:S(2)}, u32[]{:S(2)}) collective-permute-start(f32[30,8,128]{2,1,0:T(8,128)S(1)} %get-tuple-element.19), channel_id=1, source_target_pairs={{8,0},{16,8},{24,16},{32,24},{40,32},{48,40},{56,48},{9,1},{17,9},... | collective-permute-start | bytes 368648 | tf_op jit(solution)/shard_map/ppermute | solution.py:427
  33.0 7.3 %collective-permute-start.4 = (f32[52,8,128]{2,1,0:T(8,128)S(1)}, f32[52,8,128]{2,1,0:T(8,128)S(1)}, u32[]{:S(2)}, u32[]{:S(2)}) collective-permute-start(f32[52,8,128]{2,1,0:T(8,128)S(1)} %get-tuple-element.20), channel_id=1, source_target_pairs={{0,8},{8,16},{16,24},{24,32},{32,40},{40,48},{48,56},{1,9},{9,17},... | collective-permute-start | bytes 638984 | tf_op jit(solution)/shard_map/ppermute | solution.py:428
  37.6 7.8 %collective-permute-start.5 = (f32[52,8,128]{2,1,0:T(8,128)S(1)}, f32[52,8,128]{2,1,0:T(8,128)S(1)}, u32[]{:S(2)}, u32[]{:S(2)}) collective-permute-start(f32[52,8,128]{2,1,0:T(8,128)S(1)} %get-tuple-element.21), channel_id=1, source_target_pairs={{8,0},{16,8},{24,16},{32,24},{40,32},{48,40},{56,48},{9,1},{17,9},... | collective-permute-start | bytes 638984 | tf_op jit(solution)/shard_map/ppermute | solution.py:427
  45.5 13.9 %collective-permute-start.6 = (f32[15,16,128]{2,1,0:T(8,128)S(1)}, f32[15,16,128]{2,1,0:T(8,128)S(1)}, u32[]{:S(2)}, u32[]{:S(2)}) collective-permute-start(f32[15,16,128]{2,1,0:T(8,128)S(1)} %shard_map.71), channel_id=1, source_target_pairs={{1,0},{2,1},{3,2},{4,3},{5,4},{6,5},{7,6},{9,8},{10,9},{11,10},{12... | collective-permute-start | bytes 368648 | tf_op jit(solution)/shard_map/ppermute | solution.py:427
  51.0 8.3 %collective-permute-start.7 = (f32[15,16,128]{2,1,0:T(8,128)S(1)}, f32[15,16,128]{2,1,0:T(8,128)S(1)}, u32[]{:S(2)}, u32[]{:S(2)}) collective-permute-start(f32[15,16,128]{2,1,0:T(8,128)S(1)} %shard_map.71), channel_id=1, source_target_pairs={{0,1},{1,2},{2,3},{3,4},{4,5},{5,6},{6,7},{8,9},{9,10},{10,11},{11... | collective-permute-start | bytes 368648 | tf_op jit(solution)/shard_map/ppermute | solution.py:428
